TPU v7x, 32 devices: a whole 2x2x4 slice. The times are simulated.
32 devices in a mesh: groups: 2 (over x), shard: 8 (over z, y), mp: 2 (over core).
Axes of the slice: x: 2, y: 2, z: 4, core: 2. Of those that a mesh axis runs over, the one named last changes fastest.
Arguments:
- image_tokens: bfloat16 [4096, 16, 512], P(('groups', 'shard'), None, 'mp'), parts along dimension 0, may hold values from -8 to 8
- pair_owner: int32 [1024, 2], P(('groups', 'shard')), parts along dimension 0, may hold values from 0 to 7, all different within a row; in each aligned block of 64 rows (0 to 63, 64 to 127, ...) at most 32 rows name the same one
- pair_slot: int32 [1024, 2], P(('groups', 'shard')), parts along dimension 0, may hold values from 0 to 255
- gain_attn: float32 [512], replicated, may hold values from 0.1 to 1.9
- w_qk: bfloat16 [512, 512], P(None, 'mp'), may hold values from -0.25 to 0.25
- w_value: bfloat16 [512, 512], P(None, 'mp'), may hold values from -0.25 to 0.25
- logit_scale: float32 [8], P('mp'), may hold values from 0.5 to 30
- w_out: bfloat16 [512, 512], P('mp'), may hold values from -0.25 to 0.25
- gain_mlp: float32 [512], replicated, may hold values from 0.1 to 1.9
- w_in: bfloat16 [512, 2048], P(None, 'mp'), may hold values from -0.25 to 0.25
- bias_in: float32 [2048], P('mp'), may hold values from -3 to 3
- w_back: bfloat16 [2048, 512], P('mp'), may hold values from -0.125 to 0.125
Outputs:
- pair_features: bfloat16 [1024, 512], P(('groups', 'shard')), parts along dimension 0
There are 2 independent parts, one for each index of `groups`. A program takes and returns all parts, laid end to end along the dimension named above; an argument that names none is the same for every part. Nothing has to cross between parts.
Inputs may be any that keep to these rules, and one draw needn't show every extreme that they name: `pair_owner`: the two images of a pair have different owners. Among the 128 images named by the pairs of one index of shard, at most 32 have the same owner; some owner is named exactly 32 times.
All inputs are finite; a program needn't handle non-finite values.
Results may differ from a plain program's by a relative error of at most 0.0095.
Values may be sent and summed in bfloat16 or wider, within the bound.
No kernel may reach another device: no remote copies, remote signals or barrier semaphores. Data moves between devices by JAX's collectives and lax.ppermute only.
A program may use at most 64 MiB of HBM per device.

v0:
```python
import functools

import jax
import jax.numpy as jnp
from jax import lax
from jax.experimental import pallas as pl
from jax.experimental.pallas import tpu as pltpu
from jax.sharding import PartitionSpec as P

LOG2E = 1.4426950408889634
BLOCK = 8


def norm_rows(values, gain):
    center = values - jnp.mean(values, axis=-1, keepdims=True)
    spread = jnp.mean(center * center, axis=-1, keepdims=True)
    return center * lax.rsqrt(spread + 1e-05) * gain


def dot_nt(a, b):
    return lax.dot_general(a, b, (((1,), (1,)), ((), ())), preferred_element_type=jnp.float32)


def dot(a, b):
    return jnp.dot(a, b, preferred_element_type=jnp.float32)


class Plan:
    def __init__(self, pair_count, owner_count):
        self.owners = owner_count
        self.capacity = max(2, 4 * pair_count // owner_count)
        self.half = owner_count // 2
        split = self.capacity >= 32 and self.half & (self.half - 1) == 0 and self.half > 0
        self.base = self.capacity // 2 if split else self.capacity
        self.extra = self.capacity - self.base
        self.part = self.half * self.extra // 2
        self.near_at = owner_count * self.base
        self.rest_at = self.near_at + self.half * self.extra
        self.slots = self.rest_at + 2 * self.part
        self.row = self.capacity + (self.half if split else 0)


def place_kernel(plan, count, shard_ref, owner_ref, slot_ref, list_ref, *wanted_refs):
    total = 2 * count
    owners = plan.owners
    owner = jnp.concatenate([owner_ref[0:1, :], owner_ref[1:2, :]], axis=1)
    slot = jnp.concatenate([slot_ref[0:1, :], slot_ref[1:2, :]], axis=1)

    def place(dim, size):
        return lax.broadcasted_iota(jnp.int32, (size, total), dim)

    def as_bf16(values):
        return values.astype(jnp.float32).astype(jnp.bfloat16)

    row = place(0, owners)
    named = row == owner
    until = as_bf16(jnp.where(place(0, total) <= place(1, total), 1, 0))
    tally = dot(as_bf16(jnp.where(named, 1, 0)), until).astype(jnp.int32)
    rank = jnp.sum(jnp.where(named, tally, 0), axis=0, keepdims=True) - 1
    ranked = as_bf16(jnp.where(place(0, total) == rank, 1, 0))
    wanted = dot_nt(as_bf16(jnp.where(named, slot, 0)), ranked).astype(jnp.int32)
    where = owner * plan.base + rank
    if plan.extra:
        me = shard_ref[0]
        half = plan.half
        over = jnp.maximum(jnp.max(tally, axis=1, keepdims=True) - plan.base, 0)
        far_over = jnp.where(row // half != me // half, over, 0)
        before = jnp.zeros((owners, total), jnp.int32)
        for index in range(owners - 1):
            before = before + jnp.where(row > index, far_over[index : index + 1], 0)
        before = jnp.sum(jnp.where(named, before, 0), axis=0, keepdims=True)
        rest = rank - plan.base
        near = plan.near_at + ((owner % half) ^ (me % half)) * plan.extra + rest
        late = jnp.where(owner // half == me // half, near, plan.rest_at + before + rest)
        where = jnp.where(rest < 0, where, late)
        told = place(1, owners) == plan.capacity + row % half
        wanted = wanted + jnp.sum(jnp.where(told, far_over, 0), axis=0, keepdims=True)
    if plan.extra:
        for distance, wanted_ref in enumerate(wanted_refs):
            chosen = jnp.where(row == me ^ distance, wanted, 0)
            wanted_ref[...] = jnp.sum(chosen, axis=0, keepdims=True)[:, : plan.row]
    else:
        for index in range(owners):
            wanted_refs[0][index] = wanted[index : index + 1, : plan.row]
    entry = place(1, 1)
    side = entry // count
    pair = entry % count
    mine = count // 2
    local = pair % mine
    position = pair // mine * count + local // BLOCK * (2 * BLOCK) + side * BLOCK + local % BLOCK
    seated = as_bf16(jnp.where(place(0, total) == position, 1, 0))
    parts = as_bf16(jnp.where(place(0, 8) == 0, where // 16, where % 16))
    listed = dot_nt(parts, seated).astype(jnp.int32)
    list_ref[...] = listed[0:1] * 16 + listed[1:2]


def serve(tokens_ref, incoming_ref, start, served_ref):
    count = served_ref.shape[0]

    def copy(index, carry):
        served_ref[index] = tokens_ref[incoming_ref[0, start + index]]
        return carry

    lax.fori_loop(0, count, copy, 0, unroll=min(16, count))


def serve_relays_kernel(plan, *refs):
    incoming_refs, (tokens_ref, *served_refs) = refs[: plan.owners], refs[plan.owners :]
    *served_refs, crowded_ref = served_refs
    for incoming_ref, served_ref in zip(incoming_refs[plan.half :], served_refs):
        serve(tokens_ref, incoming_ref, plan.base, served_ref)
    most = 0
    for incoming_ref in incoming_refs:
        total = 0
        for index in range(plan.half):
            total = total + incoming_ref[0, plan.capacity + index]
        most = jnp.maximum(most, total)
    crowded_ref[0] = jnp.where(most > plan.part, 1, 0)


def serve_kernel(plan, shard_ref, *refs):
    incoming_refs, (tokens_ref, served_ref, *near_refs) = refs[: plan.owners], refs[plan.owners :]
    for distance, incoming_ref in enumerate(incoming_refs):
        serve(tokens_ref, incoming_ref, 0, served_ref.at[shard_ref[0] ^ distance])
    for incoming_ref, near_ref in zip(incoming_refs, near_refs):
        serve(tokens_ref, incoming_ref, plan.base, near_ref)


def serve_all_kernel(plan, incoming_ref, tokens_ref, served_ref):
    for requester in range(plan.owners):
        serve(tokens_ref, incoming_ref.at[requester], 0, served_ref.at[requester])


def relay_kernel(plan, shard_ref, incoming_ref, *refs):
    chunk_refs = refs[: plan.half]
    first_ref, second_ref = refs[plan.half :]
    for distance, chunk_ref in enumerate(chunk_refs):
        owner = (shard_ref[0] % plan.half) ^ distance
        at = 0
        for index in range(plan.half):
            amount = incoming_ref[0, plan.capacity + index]
            at = at + jnp.where(index < owner, amount, 0)
        amount = incoming_ref[0, plan.capacity + owner]
        fit = jnp.clip(plan.part - at, 0, amount)

        def pack(index, carry, chunk_ref=chunk_ref, at=at):
            first_ref[at + index] = chunk_ref[index]
            return carry

        def pack_more(index, carry, chunk_ref=chunk_ref, at=at):
            second_ref[at + index - plan.part] = chunk_ref[index]
            return carry

        lax.fori_loop(0, fit, pack, 0)
        lax.fori_loop(fit, amount, pack_more, 0)


def pick_kernel(plan, core_ref, list_ref, *refs):
    source_refs = refs[:-4]
    own_ref, other_ref, held_ref, sems = refs[-4:]
    count = own_ref.shape[0]
    at = 0
    loads = []
    for index, source_ref in enumerate(source_refs):
        size = source_ref.shape[0]
        loads.append(
            pltpu.make_async_copy(source_ref, held_ref.at[pl.ds(at, size)], sems.at[index])
        )
        at += size
    for load in loads:
        load.start()
    for load in loads:
        load.wait()
    start = core_ref[0] * count

    def pick(index, carry):
        other_ref[index] = held_ref[list_ref[0, count - start + index]]
        own_ref[index] = held_ref[list_ref[0, start + index]]
        return carry

    lax.fori_loop(0, count, pick, 0, unroll=8)


def attention_kernel(
    length,
    head_dim,
    core_ref,
    scale_a_ref,
    scale_b_ref,
    gain_attn_ref,
    gain_mlp_ref,
    *refs,
):
    own_held_ref, far_held_ref, *held_refs = refs[:8]
    normed_ref, mean_ref, qkv_ref, out_ref = refs[8:12]
    tokens_ref, heads_ref, mixed_ref, hidden_ref, sems, token_sems = refs[12:]
    width = out_ref.shape[0]
    wide = width // 2
    homes = [qkv_ref.at[:, pl.ds(k * wide, wide)] for k in range(4)]
    homes += [out_ref.at[pl.ds(k * wide, wide)] for k in range(2)]
    loads = [
        pltpu.make_async_copy(held, home, sems.at[k])
        for k, (held, home) in enumerate(zip(held_refs, homes))
    ]
    core = core_ref[0]
    token_loads = [
        pltpu.make_async_copy(own_held_ref, tokens_ref.at[core], token_sems.at[0]),
        pltpu.make_async_copy(far_held_ref, tokens_ref.at[1 - core], token_sems.at[1]),
    ]
    for load in token_loads + loads:
        load.start()
    half = BLOCK * length
    rows = 2 * half
    blocks = tokens_ref.shape[1] // (2 * BLOCK)
    long = 2 * rows
    pair_dim = 2 * head_dim
    scale_refs = (scale_a_ref, scale_b_ref)
    per_core = wide // head_dim
    even = lax.broadcasted_iota(jnp.int32, (half, pair_dim), 1) < head_dim
    same = (
        lax.broadcasted_iota(jnp.int32, (half, half), 0) // length
        == lax.broadcasted_iota(jnp.int32, (half, half), 1) // length
    )

    def span(step, size):
        return pl.ds(pl.multiple_of(step * size, size), size)

    def split(values):
        zero = jnp.zeros_like(values)
        return jnp.concatenate(
            [jnp.where(even, values, zero), jnp.where(even, zero, values)], axis=0
        )

    ones = split(jnp.ones((half, pair_dim), jnp.bfloat16))

    def start_block(step, carry):
        images = pl.ds(step * 2 * BLOCK, 2 * BLOCK)
        tokens = jnp.concatenate(
            [tokens_ref[k, images].reshape(rows, -1).astype(jnp.float32) for k in range(2)], axis=1
        )
        hidden_ref[span(step, rows), :] = tokens
        normed_ref[span(step, rows), :] = norm_rows(tokens, gain_attn_ref[...]).astype(jnp.bfloat16)
        return carry

    def project(step, carry):
        here = span(step // 4, long)
        cut = span(step % 4, 2 * width // 4)
        heads_ref[here, cut] = dot(normed_ref[here, :], qkv_ref[:, cut]).astype(jnp.bfloat16)
        return carry

    def weigh(scores, factor):
        scores = jnp.where(same, scores, -1e30)
        top = jnp.max(scores, axis=1, keepdims=True)
        return jnp.exp2((scores - top) * factor).astype(jnp.bfloat16)

    def mix(query, key, value, factors):
        scores = dot_nt(query, split(key))
        weights = [weigh(scores[:, k * half : (k + 1) * half], factors[k]) for k in range(2)]
        mixed = dot(jnp.concatenate(weights, axis=1), jnp.concatenate([split(value), ones], axis=1))
        total = mixed[:, pair_dim:]
        inverse = pl.reciprocal(total, approx=True)
        inverse = inverse * (2.0 - total * inverse)
        return (mixed[:, :pair_dim] * inverse).astype(jnp.bfloat16)

    def attend(step, carry):
        for index in range(width // pair_dim):
            factors = [scale_refs[k // per_core][k % per_core] for k in (2 * index, 2 * index + 1)]
            factors = [factor * (LOG2E / head_dim**0.5) for factor in factors]
            cut = slice(index * pair_dim, (index + 1) * pair_dim)
            beyond = slice(width + cut.start, width + cut.stop)
            sides = [span(2 * step + k, half) for k in range(2)]
            query = [heads_ref[side, cut] for side in sides]
            value = [heads_ref[side, beyond] for side in sides]
            for k in range(2):
                mixed_ref[sides[k], cut] = mix(query[k], query[1 - k], value[1 - k], factors)
        return carry

    def join(step, carry):
        here = span(step // 2, long)
        cut = span(step % 2, width // 2)
        hidden_ref[here, cut] += dot(mixed_ref[here, :], out_ref[:, cut])
        return carry

    def middle_block(step, carry):
        here = span(step, rows)
        hidden = hidden_ref[here, :]
        mean_ref[span(step, BLOCK), :] = jnp.sum(
            hidden.reshape(2, BLOCK, length, -1), axis=(0, 2)
        )
        normed_ref[here, :] = norm_rows(hidden, gain_mlp_ref[...]).astype(jnp.bfloat16)
        return carry

    for load in token_loads:
        load.wait()
    lax.fori_loop(0, blocks, start_block, 0)
    for load in loads[:4]:
        load.wait()
    lax.fori_loop(0, blocks // 2 * 4, project, 0)
    lax.fori_loop(0, blocks, attend, 0)
    for load in loads[4:6]:
        load.wait()
    lax.fori_loop(0, blocks // 2 * 2, join, 0)
    lax.fori_loop(0, blocks, middle_block, 0)


def back_kernel(length, core_ref, mean_ref, pooled_ref, back_ref, far_back_ref, result_ref):
    count = mean_ref.shape[0]
    units = back_ref.shape[0]
    pooled = pooled_ref[...] * (0.5 / length)
    coarse = pooled.astype(jnp.bfloat16)
    fine = (pooled - coarse.astype(jnp.float32)).astype(jnp.bfloat16)
    both = jnp.concatenate([coarse, fine], axis=0)
    back = dot(both[:, :units], back_ref[...]) + dot(both[:, units:], far_back_ref[...])
    mean = mean_ref[...] * (0.5 / length)
    result = (mean + back[:count] + back[count:]).astype(jnp.bfloat16)
    start = pl.multiple_of(core_ref[0] * count, count)
    result_ref[pl.ds(start, count), :] = result
    result_ref[pl.ds(pl.multiple_of(count - start, count), count), :] = jnp.zeros_like(result)


def expand(normed, w_in, bias, length):
    inner = dot(normed, w_in) + bias
    inner = jax.nn.gelu(inner, approximate=True).astype(jnp.bfloat16).astype(jnp.float32)
    inner = inner.reshape(-1, 2, BLOCK, length, inner.shape[-1])
    return jnp.sum(inner, axis=(1, 3)).reshape(-1, inner.shape[-1])


def on_device(
    image_tokens,
    pair_owner,
    pair_slot,
    gain_attn,
    w_qk,
    w_value,
    logit_scale,
    w_out,
    gain_mlp,
    w_in,
    bias_in,
    w_back,
):
    owner_count = lax.axis_size("shard")
    groups = lax.axis_size("groups")
    core = lax.axis_index("mp").reshape(1)
    shard = lax.axis_index("shard").reshape(1)
    pair_count = pair_owner.shape[0]
    _, length, features = image_tokens.shape
    width = 2 * features
    head_dim = w_qk.shape[1] // logit_scale.shape[0]
    mine = pair_count // 2
    units = 2 * w_in.shape[1]
    plan = Plan(pair_count, owner_count)

    def swap(values):
        return lax.ppermute(values, "mp", [(0, 1), (1, 0)])

    def across(values, distance):
        return lax.ppermute(values, "shard", [(k, k ^ distance) for k in range(owner_count)])

    def images(*counts):
        return jax.ShapeDtypeStruct((*counts, length, features), jnp.bfloat16)

    smem = pl.BlockSpec(memory_space=pltpu.SMEM)
    vmem = pl.BlockSpec(memory_space=pltpu.VMEM)
    hbm = pl.BlockSpec(memory_space=pl.ANY)

    def limit(mebibytes):
        return pltpu.CompilerParams(vmem_limit_bytes=mebibytes * 2**20)

    if plan.extra:
        asked = [jax.ShapeDtypeStruct((1, plan.row), jnp.int32)] * owner_count
    else:
        asked = [jax.ShapeDtypeStruct((owner_count, 1, plan.row), jnp.int32)]
    order, *wanted = pl.pallas_call(
        functools.partial(place_kernel, plan, pair_count),
        out_shape=[jax.ShapeDtypeStruct((1, 2 * pair_count), jnp.int32), *asked],
        in_specs=[smem, vmem, vmem],
    )(shard, pair_owner.T, pair_slot.T)
    if plan.extra:
        incoming = [wanted[0]] + [across(wanted[k], k) for k in range(1, owner_count)]
        incoming = lax.optimization_barrier(incoming)
        *chunks, crowded = pl.pallas_call(
            functools.partial(serve_relays_kernel, plan),
            out_shape=[images(plan.extra)] * plan.half + [jax.ShapeDtypeStruct((1,), jnp.int32)],
            in_specs=[smem] * owner_count + [vmem],
            out_specs=[vmem] * plan.half + [smem],
        )(*incoming, image_tokens)
        incoming, chunks = lax.optimization_barrier((incoming, chunks))
        chunks = [chunks[0]] + [across(chunks[k], k) for k in range(1, plan.half)]
        served, *near = pl.pallas_call(
            functools.partial(serve_kernel, plan),
            out_shape=[images(owner_count, plan.base)] + [images(plan.extra)] * plan.half,
            in_specs=[smem] * (1 + owner_count) + [vmem],
        )(shard, *incoming, image_tokens)
        served, near, chunks = lax.optimization_barrier((served, near, chunks))
    else:
        incoming = lax.all_to_all(wanted[0], "shard", split_axis=0, concat_axis=0, tiled=True)
        served = pl.pallas_call(
            functools.partial(serve_all_kernel, plan),
            out_shape=images(owner_count, plan.base),
            in_specs=[smem, vmem],
        )(incoming, image_tokens)
    returned = lax.all_to_all(served, "shard", split_axis=0, concat_axis=0, tiled=True)
    sources = [returned.reshape(-1, length, features)]
    if plan.extra:
        first, second = pl.pallas_call(
            functools.partial(relay_kernel, plan),
            out_shape=[images(plan.part)] * 2,
            in_specs=[smem, smem] + [vmem] * plan.half,
        )(shard, incoming[plan.half], *chunks)
        first = across(first, plan.half)
        near = [near[0]] + [across(near[k], k) for k in range(1, plan.half)]
        passed = crowded
        for _ in range(groups - 1):
            passed = lax.ppermute(passed, "groups", [(k, (k + 1) % groups) for k in range(groups)])
            crowded = jnp.maximum(crowded, passed)
        sources += [*near, first]
    weights = (w_qk, w_value, w_out, w_in, w_back, bias_in, logit_scale)
    far_qk, far_value, far_out, far_in, far_back, far_bias, far_scale = [swap(w) for w in weights]
    all_in = jnp.concatenate([w_in, far_in], axis=1)
    all_bias = jnp.concatenate([bias_in, far_bias])
    swapped = (far_qk, far_value, far_out, all_in, far_back, all_bias, far_scale)
    sources, swapped = lax.optimization_barrier((sources, swapped))
    far_qk, far_value, far_out, all_in, far_back, all_bias, far_scale = swapped
    if plan.extra:
        second, sources = lax.optimization_barrier((second, sources))
        second = lax.cond(
            crowded[0] > 0, lambda part: across(part, plan.half), lambda part: part, second
        )
        sources = [*sources, second]
    own, other = pl.pallas_call(
        functools.partial(pick_kernel, plan),
        out_shape=[images(pair_count)] * 2,
        in_specs=[smem, smem] + [hbm] * len(sources),
        scratch_shapes=[
            pltpu.VMEM((plan.slots, length, features), jnp.bfloat16),
            pltpu.SemaphoreType.DMA((len(sources),)),
        ],
    )(core, order, *sources)
    far = swap(other)
    token_count = pair_count * length
    normed, mean = pl.pallas_call(
        functools.partial(attention_kernel, length, head_dim),
        out_shape=(
            jax.ShapeDtypeStruct((token_count, width), jnp.bfloat16),
            jax.ShapeDtypeStruct((mine, width), jnp.float32),
        ),
        in_specs=[smem] * 3 + [vmem] * 2 + [hbm] * 8,
        scratch_shapes=[
            pltpu.VMEM((width, 2 * width), jnp.bfloat16),
            pltpu.VMEM((width, width), jnp.bfloat16),
            pltpu.VMEM((2, pair_count, length, features), jnp.bfloat16),
            pltpu.VMEM((token_count, 2 * width), jnp.bfloat16),
            pltpu.VMEM((token_count, width), jnp.bfloat16),
            pltpu.VMEM((token_count, width), jnp.float32),
            pltpu.SemaphoreType.DMA((6,)),
            pltpu.SemaphoreType.DMA((2,)),
        ],
        compiler_params=limit(24),
        cost_estimate=pl.CostEstimate(
            flops=6 * token_count * width * width,
            bytes_accessed=4 * 2**20,
            transcendentals=token_count * 1024,
        ),
    )(
        core,
        logit_scale,
        far_scale,
        gain_attn.reshape(1, -1),
        gain_mlp.reshape(1, -1),
        own,
        far,
        w_qk,
        far_qk,
        w_value,
        far_value,
        w_out,
        far_out,
    )
    here = pl.pallas_call(
        functools.partial(back_kernel, length),
        out_shape=jax.ShapeDtypeStruct((pair_count, width), jnp.bfloat16),
        in_specs=[smem] + [vmem] * 4,
        compiler_params=limit(16),
    )(core, mean, expand(normed, all_in, all_bias, length), w_back, far_back)
    return here + swap(here)


def solution(mesh):
    in_specs = (
        P(("groups", "shard"), None, "mp"),
        P(("groups", "shard"), None),
        P(("groups", "shard"), None),
        P(),
        P(None, "mp"),
        P(None, "mp"),
        P("mp"),
        P("mp", None),
        P(),
        P(None, "mp"),
        P("mp"),
        P("mp", None),
    )
    out_specs = P(("groups", "shard"), None)
    return jax.shard_map(
        on_device, mesh=mesh, in_specs=in_specs, out_specs=out_specs, check_vma=False
    )
```

profile of v0, /device:TPU:0, one launch (start us, length us, event | category | flops | bytes accessed | tf_op | source)
XLA Modules:
  0.0 93.6 jit_solution(10515129913977036697)
XLA Ops:
  0.0 1.9 %shard_map.118 = (s32[1,128]{1,0:T(1,128)}, s32[1,36]{1,0:T(1,128)}, s32[1,36]{1,0:T(1,128)}, s32[1,36]{1,0:T(1,128)}, s32[1,36]{1,0:T(1,128)}, /*index=5*/s32[1...) custom-call(s32[1]{0:T(128)} %bitcast.1.shard_ref, s32[2,64]{1,0:T(2,128)} %bitcast.17, s32[2,64]{1,0:T(2,128)} %bitcast.18), custom_call_target="tpu_custom_call" | custom-call | tf_op jit(solution)/shard_map/pallas_call | solution.py:374
  1.9 3.0 %collective-permute-start.1 = (s32[1,36]{1,0:T(1,128)}, s32[1,36]{1,0:T(1,128)S(1)}, u32[]{:S(2)}, u32[]{:S(2)}) collective-permute-start(s32[1,36]{1,0:T(1,128)} %get-tuple-element.85), channel_id=1, source_target_pairs={{0,2},{2,0},{4,6},{6,4},{8,10},{10,8},{12,14},{14,12},{1,3},{3,1},... | collective-permute-start | bytes 440 | tf_op jit(solution)/shard_map/ppermute | solution.py:358
  4.9 1.6 %collective-permute-start.2 = (s32[1,36]{1,0:T(1,128)}, s32[1,36]{1,0:T(1,128)S(1)}, u32[]{:S(2)}, u32[]{:S(2)}) collective-permute-start(s32[1,36]{1,0:T(1,128)} %get-tuple-element.86), channel_id=1, source_target_pairs={{0,4},{2,6},{4,0},{6,2},{8,12},{10,14},{12,8},{14,10},{1,5},{3,7},... | collective-permute-start | bytes 440 | tf_op jit(solution)/shard_map/ppermute | solution.py:358
  6.5 3.0 %collective-permute-start.4 = (s32[1,36]{1,0:T(1,128)}, s32[1,36]{1,0:T(1,128)S(1)}, u32[]{:S(2)}, u32[]{:S(2)}) collective-permute-start(s32[1,36]{1,0:T(1,128)} %get-tuple-element.88), channel_id=1, source_target_pairs={{0,8},{2,10},{4,12},{6,14},{8,0},{10,2},{12,4},{14,6},{1,9},{3,11}... | collective-permute-start | bytes 440 | tf_op jit(solution)/shard_map/ppermute | solution.py:358
  10.8 3.6 %collective-permute-start.6 = (s32[1,36]{1,0:T(1,128)}, s32[1,36]{1,0:T(1,128)S(1)}, u32[]{:S(2)}, u32[]{:S(2)}) collective-permute-start(s32[1,36]{1,0:T(1,128)} %get-tuple-element.90), channel_id=1, source_target_pairs={{0,12},{2,14},{4,8},{6,10},{8,4},{10,6},{12,0},{14,2},{1,13},{3,15... | collective-permute-start | bytes 440 | tf_op jit(solution)/shard_map/ppermute | solution.py:358
  16.2 4.7 %collective-permute-done.7.refs_7_ = s32[1,36]{1,0:T(1,128)S(1)} collective-permute-done((s32[1,36]{1,0:T(1,128)}, s32[1,36]{1,0:T(1,128)S(1)}, u32[]{:S(2)}, u32[]{:S(2)}) %collective-permute-start.7) | collective-permute-done | bytes 176 | tf_op jit(solution)/shard_map/ppermute | solution.py:358
  21.3 2.5 %shard_map.119 = (bf16[16,16,256]{2,1,0:T(8,128)(2,1)}, bf16[16,16,256]{2,1,0:T(8,128)(2,1)}, bf16[16,16,256]{2,1,0:T(8,128)(2,1)}, bf16[16,16,256]{2,1,0:T(8,128)(2,1)}, s32[1]{0:T(128)}) custom-call(s32[1,36]{1,0:T(1,128)} %get-tuple-element.104.refs_0_, s32[1,36]{1,0:T(1,128)} %copy-done.16, s32[1,36]{1,0:T(1,128)} %copy-done.17, s32[1,36]{1,0:T(1,128)} %copy-done.18, ...), custom_call_target="tpu_custom_call" | custom-call | tf_op jit(solution)/shard_map/pallas_call | solution.py:382
  24.3 3.0 %collective-permute-start.10 = (bf16[16,16,256]{2,1,0:T(8,128)(2,1)}, bf16[16,16,256]{2,1,0:T(8,128)(2,1)S(1)}, u32[]{:S(2)}, u32[]{:S(2)}) collective-permute-start(bf16[16,16,256]{2,1,0:T(8,128)(2,1)} %get-tuple-element.120), channel_id=1, source_target_pairs={{0,6},{2,4},{4,2},{6,0},{8,14},{10,12},{12,10},{14,8},{1,7},{3,5},... | collective-permute-start | bytes 393224 | tf_op jit(solution)/shard_map/ppermute | solution.py:358
  27.3 2.9 %shard_map.120 = (bf16[8,16,16,256]{3,2,1,0:T(8,128)(2,1)}, bf16[16,16,256]{2,1,0:T(8,128)(2,1)}, bf16[16,16,256]{2,1,0:T(8,128)(2,1)}, bf16[16,16,256]{2,1,0:T(8,128)(2,1)}, bf16[16,16,256]{2,1,0:T(8,128)(2,1)}) custom-call(s32[1]{0:T(128)} %bitcast.1.shard_ref, s32[1,36]{1,0:T(1,128)} %get-tuple-element.104.refs_0_, s32[1,36]{1,0:T(1,128)} %copy-done.16, ...), custom_call_target="tpu_custom_call" | custom-call | tf_op jit(solution)/shard_map/pallas_call | solution.py:390
  30.2 1.6 %collective-permute-done.10.refs_3_ = bf16[16,16,256]{2,1,0:T(8,128)(2,1)S(1)} collective-permute-done((bf16[16,16,256]{2,1,0:T(8,128)(2,1)}, bf16[16,16,256]{2,1,0:T(8,128)(2,1)S(1)}, u32[]{:S(2)}, u32[]{:S(2)}) %collective-permute-start.10) | collective-permute-done | bytes 131104 | tf_op jit(solution)/shard_map/ppermute | solution.py:358
  31.9 4.3 %all-to-all-start = ((bf16[8,16,16,256]{3,2,1,0:T(8,128)(2,1)}), bf16[8,16,16,256]{3,2,1,0:T(8,128)(2,1)}, u32[]{:S(2)}, u32[]{:S(2)}) async-start(bf16[8,16,16,256]{3,2,1,0:T(8,128)(2,1)} %get-tuple-element.121), calls=%async_computation | async-start | bytes 2097152 | tf_op jit(solution)/shard_map/all_to_all | solution.py:403
  37.4 3.0 %collective-permute-done.21.scale_b_ref = f32[4]{0:T(128)S(1)} collective-permute-done((f32[4]{0:T(128)S(1)}, f32[4]{0:T(128)S(1)}, u32[]{:S(2)}, u32[]{:S(2)}) %collective-permute-start.21) | collective-permute-done | bytes 48 | tf_op jit(solution)/shard_map/ppermute | solution.py:355
  40.4 1.5 %collective-permute-start.22 = (s32[1]{0:T(128)}, s32[1]{0:T(128)}, u32[]{:S(2)}, u32[]{:S(2)}) collective-permute-start(s32[1]{0:T(128)} %get-tuple-element.146), channel_id=1, source_target_pairs={{0,16},{16,0},{1,17},{17,1},{2,18},{18,2},{3,19},{19,3},{4,20},{20... | collective-permute-start | bytes 20 | tf_op jit(solution)/shard_map/ppermute | solution.py:415
  41.9 2.1 %collective-permute-done.22 = s32[1]{0:T(128)} collective-permute-done((s32[1]{0:T(128)}, s32[1]{0:T(128)}, u32[]{:S(2)}, u32[]{:S(2)}) %collective-permute-start.22) | collective-permute-done | bytes 36 | tf_op jit(solution)/shard_map/ppermute | solution.py:415
  47.1 2.2 %shard_map.121 = (bf16[32,16,256]{2,1,0:T(8,128)(2,1)}, bf16[32,16,256]{2,1,0:T(8,128)(2,1)}) custom-call(s32[1]{0:T(128)} %bitcast.1.shard_ref, s32[1,36]{1,0:T(1,128)} %copy-done.15, bf16[16,16,256]{2,1,0:T(8,128)(2,1)} %get-tuple-element.126.refs_0_, bf16[16,16,256]{2,1,0:T(8,128)(2,1)} %copy-done.9, bf16[16,16,256]{2,1,0:T(8,128)(2,1)} %copy-done.10, ...), custom_call_target="tpu_custom_call" | custom-call | tf_op jit(solution)/shard_map/pallas_call | solution.py:406
  49.3 1.9 %collective-permute-start.11 = (bf16[16,16,256]{2,1,0:T(8,128)(2,1)}, bf16[16,16,256]{2,1,0:T(8,128)(2,1)S(1)}, u32[]{:S(2)}, u32[]{:S(2)}) collective-permute-start(bf16[16,16,256]{2,1,0:T(8,128)(2,1)} %get-tuple-element.123), channel_id=1, source_target_pairs={{0,2},{2,0},{4,6},{6,4},{8,10},{10,8},{12,14},{14,12},{1,3},{3,1},... | collective-permute-start | bytes 393224 | tf_op jit(solution)/shard_map/ppermute | solution.py:358
  52.8 2.6 %collective-permute-start.14 = (bf16[32,16,256]{2,1,0:T(8,128)(2,1)}, bf16[32,16,256]{2,1,0:T(8,128)(2,1)}, u32[]{:S(2)}, u32[]{:S(2)}) collective-permute-start(bf16[32,16,256]{2,1,0:T(8,128)(2,1)} %get-tuple-element.130), channel_id=1, source_target_pairs={{0,8},{2,10},{4,12},{6,14},{8,0},{10,2},{12,4},{14,6},{1,9},{3,11}... | collective-permute-start | bytes 786440 | tf_op jit(solution)/shard_map/ppermute | solution.py:358
  55.5 3.1 %pad_maximum_fusion = bf16[512,2048]{1,0:T(8,128)(2,1)} fusion(bf16[512,1024]{1,0:T(8,128)(2,1)} %collective-permute-done.18, bf16[512,1024]{1,0:T(8,128)(2,1)} %param.23), kind=kLoop, calls=%fused_computation.10 | loop fusion | flops 4194304 | bytes 4194304 | tf_op jit(solution)/shard_map/concatenate | solution.py:420
  58.6 5.3 %collective-permute-done.12.refs_3_ = bf16[16,16,256]{2,1,0:T(8,128)(2,1)S(1)} collective-permute-done((bf16[16,16,256]{2,1,0:T(8,128)(2,1)}, bf16[16,16,256]{2,1,0:T(8,128)(2,1)S(1)}, u32[]{:S(2)}, u32[]{:S(2)}) %collective-permute-start.12) | collective-permute-done | bytes 131104 | tf_op jit(solution)/shard_map/ppermute | solution.py:358
  64.5 4.7 %collective-permute-done.14.refs_5_ = bf16[32,16,256]{2,1,0:T(8,128)(2,1)} collective-permute-done((bf16[32,16,256]{2,1,0:T(8,128)(2,1)}, bf16[32,16,256]{2,1,0:T(8,128)(2,1)}, u32[]{:S(2)}, u32[]{:S(2)}) %collective-permute-start.14) | collective-permute-done | bytes 262176 | tf_op jit(solution)/shard_map/ppermute | solution.py:358
  69.3 3.4 %shard_map.122 = (bf16[64,16,256]{2,1,0:T(8,128)(2,1)}, bf16[64,16,256]{2,1,0:T(8,128)(2,1)}) custom-call(s32[1]{0:T(128)} %bitcast.core_ref, s32[1,128]{1,0:T(1,128)} %get-tuple-element.132.list_ref, bf16[128,16,256]{2,1,0:T(8,128)(2,1)} %bitcast.4.refs_0_, bf16[16,16,256]{2,1,0:T(8,128)(2,1)} %get-tuple-element.141.refs_1_, ...), custom_call_target="tpu_custom_call" | custom-call | tf_op jit(solution)/shard_map/pallas_call | solution.py:431
  72.8 2.1 %collective-permute-done.23.refs_1_ = bf16[64,16,256]{2,1,0:T(8,128)(2,1)S(1)} collective-permute-done((bf16[64,16,256]{2,1,0:T(8,128)(2,1)}, bf16[64,16,256]{2,1,0:T(8,128)(2,1)S(1)}, u32[]{:S(2)}, u32[]{:S(2)}) %collective-permute-start.23) | collective-permute-done | bytes 524320 | tf_op jit(solution)/shard_map/ppermute | solution.py:355
  75.9 9.2 %shard_map.123 = (bf16[1024,512]{1,0:T(8,128)(2,1)S(1)}, f32[32,512]{1,0:T(8,128)S(1)}) custom-call(s32[1]{0:T(128)} %bitcast.core_ref, f32[4]{0:T(128)S(1)} %copy-done.7, f32[4]{0:T(128)S(1)} %collective-permute-done.21.scale_b_ref, f32[1,512]{1,0:T(1,128)S(1)} %bitcast.14, f32[1,512]{1,0:T(1,128)S(1)} %bitcast.15, bf16[64,16,256]{2,1,0:T(8,128)(2,1)S(1)} %copy-done.1, ...), custom_call_target="tpu_custom_call" | custom-call | flops 1610612736 | bytes 4194304 | tf_op jit(solution)/shard_map/pallas_call | solution.py:442
  85.1 4.9 %fusion.7 = bf16[1024,2048]{1,0:T(8,128)(2,1)S(1)} fusion(f32[2048]{0:T(1024)} %pad_maximum_fusion.1, bf16[1024,512]{1,0:T(8,128)(2,1)S(1)} %get-tuple-element.154, bf16[512,2048]{1,0:T(8,128)(2,1)S(1)} %copy-done.8), kind=kOutput, calls=%fused_computation.8 | convolution fusion | flops 2168455168 | bytes 7348224 | tf_op jit(solution)/shard_map/dot_general | solution.py:25
  (83 shorter events, 14.1 us)
Async XLA Ops:
  1.9 8.8 %collective-permute-start.1 = (s32[1,36]{1,0:T(1,128)}, s32[1,36]{1,0:T(1,128)S(1)}, u32[]{:S(2)}, u32[]{:S(2)}) collective-permute-start(s32[1,36]{1,0:T(1,128)} %get-tuple-element.85), channel_id=1, source_target_pairs={{0,2},{2,0},{4,6},{6,4},{8,10},{10,8},{12,14},{14,12},{1,3},{3,1},... | collective-permute-start | bytes 440 | tf_op jit(solution)/shard_map/ppermute | solution.py:358
  4.9 9.5 %collective-permute-start.2 = (s32[1,36]{1,0:T(1,128)}, s32[1,36]{1,0:T(1,128)S(1)}, u32[]{:S(2)}, u32[]{:S(2)}) collective-permute-start(s32[1,36]{1,0:T(1,128)} %get-tuple-element.86), channel_id=1, source_target_pairs={{0,4},{2,6},{4,0},{6,2},{8,12},{10,14},{12,8},{14,10},{1,5},{3,7},... | collective-permute-start | bytes 440 | tf_op jit(solution)/shard_map/ppermute | solution.py:358
  6.5 7.9 %collective-permute-start.3 = (s32[1,36]{1,0:T(1,128)}, s32[1,36]{1,0:T(1,128)S(1)}, u32[]{:S(2)}, u32[]{:S(2)}) collective-permute-start(s32[1,36]{1,0:T(1,128)} %get-tuple-element.87), channel_id=1, source_target_pairs={{0,6},{2,4},{4,2},{6,0},{8,14},{10,12},{12,10},{14,8},{1,7},{3,5},... | collective-permute-start | bytes 440 | tf_op jit(solution)/shard_map/ppermute | solution.py:358
  6.5 7.9 %collective-permute-start.4 = (s32[1,36]{1,0:T(1,128)}, s32[1,36]{1,0:T(1,128)S(1)}, u32[]{:S(2)}, u32[]{:S(2)}) collective-permute-start(s32[1,36]{1,0:T(1,128)} %get-tuple-element.88), channel_id=1, source_target_pairs={{0,8},{2,10},{4,12},{6,14},{8,0},{10,2},{12,4},{14,6},{1,9},{3,11}... | collective-permute-start | bytes 440 | tf_op jit(solution)/shard_map/ppermute | solution.py:358
  9.5 5.4 %collective-permute-start.5 = (s32[1,36]{1,0:T(1,128)}, s32[1,36]{1,0:T(1,128)S(1)}, u32[]{:S(2)}, u32[]{:S(2)}) collective-permute-start(s32[1,36]{1,0:T(1,128)} %get-tuple-element.89), channel_id=1, source_target_pairs={{0,10},{2,8},{4,14},{6,12},{8,2},{10,0},{12,6},{14,4},{1,11},{3,9}... | collective-permute-start | bytes 440 | tf_op jit(solution)/shard_map/ppermute | solution.py:358
  10.8 5.4 %collective-permute-start.6 = (s32[1,36]{1,0:T(1,128)}, s32[1,36]{1,0:T(1,128)S(1)}, u32[]{:S(2)}, u32[]{:S(2)}) collective-permute-start(s32[1,36]{1,0:T(1,128)} %get-tuple-element.90), channel_id=1, source_target_pairs={{0,12},{2,14},{4,8},{6,10},{8,4},{10,6},{12,0},{14,2},{1,13},{3,15... | collective-permute-start | bytes 440 | tf_op jit(solution)/shard_map/ppermute | solution.py:358
  14.4 6.4 %collective-permute-start.7 = (s32[1,36]{1,0:T(1,128)}, s32[1,36]{1,0:T(1,128)S(1)}, u32[]{:S(2)}, u32[]{:S(2)}) collective-permute-start(s32[1,36]{1,0:T(1,128)} %get-tuple-element.91), channel_id=1, source_target_pairs={{0,14},{2,12},{4,10},{6,8},{8,6},{10,4},{12,2},{14,0},{1,15},{3,13... | collective-permute-start | bytes 440 | tf_op jit(solution)/shard_map/ppermute | solution.py:358
  23.8 6.5 %collective-permute-start.8 = (bf16[16,16,256]{2,1,0:T(8,128)(2,1)}, bf16[16,16,256]{2,1,0:T(8,128)(2,1)S(1)}, u32[]{:S(2)}, u32[]{:S(2)}) collective-permute-start(bf16[16,16,256]{2,1,0:T(8,128)(2,1)} %get-tuple-element.118), channel_id=1, source_target_pairs={{0,2},{2,0},{4,6},{6,4},{8,10},{10,8},{12,14},{14,12},{1,3},{3,1},... | collective-permute-start | bytes 393224 | tf_op jit(solution)/shard_map/ppermute | solution.py:358
  24.3 5.9 %collective-permute-start.9 = (bf16[16,16,256]{2,1,0:T(8,128)(2,1)}, bf16[16,16,256]{2,1,0:T(8,128)(2,1)S(1)}, u32[]{:S(2)}, u32[]{:S(2)}) collective-permute-start(bf16[16,16,256]{2,1,0:T(8,128)(2,1)} %get-tuple-element.119), channel_id=1, source_target_pairs={{0,4},{2,6},{4,0},{6,2},{8,12},{10,14},{12,8},{14,10},{1,5},{3,7},... | collective-permute-start | bytes 393224 | tf_op jit(solution)/shard_map/ppermute | solution.py:358
  24.3 7.5 %collective-permute-start.10 = (bf16[16,16,256]{2,1,0:T(8,128)(2,1)}, bf16[16,16,256]{2,1,0:T(8,128)(2,1)S(1)}, u32[]{:S(2)}, u32[]{:S(2)}) collective-permute-start(bf16[16,16,256]{2,1,0:T(8,128)(2,1)} %get-tuple-element.120), channel_id=1, source_target_pairs={{0,6},{2,4},{4,2},{6,0},{8,14},{10,12},{12,10},{14,8},{1,7},{3,5},... | collective-permute-start | bytes 393224 | tf_op jit(solution)/shard_map/ppermute | solution.py:358
  31.9 37.4 %all-to-all-start = ((bf16[8,16,16,256]{3,2,1,0:T(8,128)(2,1)}), bf16[8,16,16,256]{3,2,1,0:T(8,128)(2,1)}, u32[]{:S(2)}, u32[]{:S(2)}) async-start(bf16[8,16,16,256]{3,2,1,0:T(8,128)(2,1)} %get-tuple-element.121), calls=%async_computation | async-start | bytes 2097152 | tf_op jit(solution)/shard_map/all_to_all | solution.py:403
  36.2 16.6 %collective-permute-start.18 = (bf16[512,1024]{1,0:T(8,128)(2,1)}, bf16[512,1024]{1,0:T(8,128)(2,1)}, u32[]{:S(2)}, u32[]{:S(2)}) collective-permute-start(bf16[512,1024]{1,0:T(8,128)(2,1)} %param.23), channel_id=1, source_target_pairs={{0,1},{1,0},{2,3},{3,2},{4,5},{5,4},{6,7},{7,6},{8,9},{9,8},{10,11... | collective-permute-start | bytes 3145736 | tf_op jit(solution)/shard_map/ppermute | solution.py:355
  36.3 33.0 %collective-permute-start.19 = (bf16[1024,512]{1,0:T(8,128)(2,1)S(1)}, bf16[1024,512]{1,0:T(8,128)(2,1)S(1)}, u32[]{:S(2)}, u32[]{:S(2)}) collective-permute-start(bf16[1024,512]{1,0:T(8,128)(2,1)S(1)} %copy-done), channel_id=1, source_target_pairs={{0,1},{1,0},{2,3},{3,2},{4,5},{5,4},{6,7},{7,6},{8,9},{9,8},{10,11... | collective-permute-start | bytes 3145736 | tf_op jit(solution)/shard_map/ppermute | solution.py:355
  36.8 7.2 %collective-permute-start.20 = (f32[1024]{0:T(1024)}, f32[1024]{0:T(1024)}, u32[]{:S(2)}, u32[]{:S(2)}) collective-permute-start(f32[1024]{0:T(1024)} %param.24), channel_id=1, source_target_pairs={{0,1},{1,0},{2,3},{3,2},{4,5},{5,4},{6,7},{7,6},{8,9},{9,8},{10,11... | collective-permute-start | bytes 12296 | tf_op jit(solution)/shard_map/ppermute | solution.py:355
  36.9 3.6 %collective-permute-start.21 = (f32[4]{0:T(128)S(1)}, f32[4]{0:T(128)S(1)}, u32[]{:S(2)}, u32[]{:S(2)}) collective-permute-start(f32[4]{0:T(128)S(1)} %copy-done.7), channel_id=1, source_target_pairs={{0,1},{1,0},{2,3},{3,2},{4,5},{5,4},{6,7},{7,6},{8,9},{9,8},{10,11... | collective-permute-start | bytes 56 | tf_op jit(solution)/shard_map/ppermute | solution.py:355
  37.3 12.0 %collective-permute-start.15 = (bf16[512,256]{1,0:T(8,128)(2,1)S(1)}, bf16[512,256]{1,0:T(8,128)(2,1)S(1)}, u32[]{:S(2)}, u32[]{:S(2)}) collective-permute-start(bf16[512,256]{1,0:T(8,128)(2,1)S(1)} %copy-done.2), channel_id=1, source_target_pairs={{0,1},{1,0},{2,3},{3,2},{4,5},{5,4},{6,7},{7,6},{8,9},{9,8},{10,11... | collective-permute-start | bytes 786440 | tf_op jit(solution)/shard_map/ppermute | solution.py:355
  40.4 3.6 %collective-permute-start.22 = (s32[1]{0:T(128)}, s32[1]{0:T(128)}, u32[]{:S(2)}, u32[]{:S(2)}) collective-permute-start(s32[1]{0:T(128)} %get-tuple-element.146), channel_id=1, source_target_pairs={{0,16},{16,0},{1,17},{17,1},{2,18},{18,2},{3,19},{19,3},{4,20},{20... | collective-permute-start | bytes 20 | tf_op jit(solution)/shard_map/ppermute | solution.py:415
  44.0 7.2 %collective-permute-start.16 = (bf16[512,256]{1,0:T(8,128)(2,1)S(1)}, bf16[512,256]{1,0:T(8,128)(2,1)S(1)}, u32[]{:S(2)}, u32[]{:S(2)}) collective-permute-start(bf16[512,256]{1,0:T(8,128)(2,1)S(1)} %copy-done.3), channel_id=1, source_target_pairs={{0,1},{1,0},{2,3},{3,2},{4,5},{5,4},{6,7},{7,6},{8,9},{9,8},{10,11... | collective-permute-start | bytes 786440 | tf_op jit(solution)/shard_map/ppermute | solution.py:355
  44.0 8.7 %collective-permute-start.17 = (bf16[256,512]{1,0:T(8,128)(2,1)S(1)}, bf16[256,512]{1,0:T(8,128)(2,1)}, u32[]{:S(2)}, u32[]{:S(2)}) collective-permute-start(bf16[256,512]{1,0:T(8,128)(2,1)S(1)} %copy-done.4), channel_id=1, source_target_pairs={{0,1},{1,0},{2,3},{3,2},{4,5},{5,4},{6,7},{7,6},{8,9},{9,8},{10,11... | collective-permute-start | bytes 786440 | tf_op jit(solution)/shard_map/ppermute | solution.py:355
  49.3 9.2 %collective-permute-start.11 = (bf16[16,16,256]{2,1,0:T(8,128)(2,1)}, bf16[16,16,256]{2,1,0:T(8,128)(2,1)S(1)}, u32[]{:S(2)}, u32[]{:S(2)}) collective-permute-start(bf16[16,16,256]{2,1,0:T(8,128)(2,1)} %get-tuple-element.123), channel_id=1, source_target_pairs={{0,2},{2,0},{4,6},{6,4},{8,10},{10,8},{12,14},{14,12},{1,3},{3,1},... | collective-permute-start | bytes 393224 | tf_op jit(solution)/shard_map/ppermute | solution.py:358
  51.2 12.7 %collective-permute-start.12 = (bf16[16,16,256]{2,1,0:T(8,128)(2,1)}, bf16[16,16,256]{2,1,0:T(8,128)(2,1)S(1)}, u32[]{:S(2)}, u32[]{:S(2)}) collective-permute-start(bf16[16,16,256]{2,1,0:T(8,128)(2,1)} %get-tuple-element.124), channel_id=1, source_target_pairs={{0,4},{2,6},{4,0},{6,2},{8,12},{10,14},{12,8},{14,10},{1,5},{3,7},... | collective-permute-start | bytes 393224 | tf_op jit(solution)/shard_map/ppermute | solution.py:358
  52.7 11.3 %collective-permute-start.13 = (bf16[16,16,256]{2,1,0:T(8,128)(2,1)}, bf16[16,16,256]{2,1,0:T(8,128)(2,1)S(1)}, u32[]{:S(2)}, u32[]{:S(2)}) collective-permute-start(bf16[16,16,256]{2,1,0:T(8,128)(2,1)} %get-tuple-element.125), channel_id=1, source_target_pairs={{0,6},{2,4},{4,2},{6,0},{8,14},{10,12},{12,10},{14,8},{1,7},{3,5},... | collective-permute-start | bytes 393224 | tf_op jit(solution)/shard_map/ppermute | solution.py:358
  52.8 16.5 %collective-permute-start.14 = (bf16[32,16,256]{2,1,0:T(8,128)(2,1)}, bf16[32,16,256]{2,1,0:T(8,128)(2,1)}, u32[]{:S(2)}, u32[]{:S(2)}) collective-permute-start(bf16[32,16,256]{2,1,0:T(8,128)(2,1)} %get-tuple-element.130), channel_id=1, source_target_pairs={{0,8},{2,10},{4,12},{6,14},{8,0},{10,2},{12,4},{14,6},{1,9},{3,11}... | collective-permute-start | bytes 786440 | tf_op jit(solution)/shard_map/ppermute | solution.py:358
  72.7 2.2 %collective-permute-start.23 = (bf16[64,16,256]{2,1,0:T(8,128)(2,1)}, bf16[64,16,256]{2,1,0:T(8,128)(2,1)S(1)}, u32[]{:S(2)}, u32[]{:S(2)}) collective-permute-start(bf16[64,16,256]{2,1,0:T(8,128)(2,1)} %get-tuple-element.149), channel_id=1, source_target_pairs={{0,1},{1,0},{2,3},{3,2},{4,5},{5,4},{6,7},{7,6},{8,9},{9,8},{10,11... | collective-permute-start | bytes 1572872 | tf_op jit(solution)/shard_map/ppermute | solution.py:355
  (23 other events, 371.1 us)
where the time goes:
time: 94.1 us; the launch traced here: 93.6 us
  starting transfers between devices  29.8 us (32%)
  waiting for transfers between devices  26.6 us (28%)
  Pallas kernels  22.4 us (24%)
  other arithmetic  6.2 us (7%)
  matrix products  4.86 us (5%)
  local copies, waits for them, and re-layouts  2.07 us (2%)
  between operations  1.61 us (2%)
    ppermute x14, starting transfers between devices, across(): lax.ppermute(values, 'shard', [(k, k ^ distance) for k in range(owner_cou...  22.1 us
    ppermute x14, waiting for transfers between devices, across(): lax.ppermute(values, 'shard', [(k, k ^ distance) for k in range(owner_cou...  18.2 us
    pallas_call x1, Pallas kernels, on_device(): pl.pallas_call(functools.partial(attention_kernel, length, head_dim), out...  9.16 us
    ppermute x9, waiting for transfers between devices, swap(): return lax.ppermute(values, 'mp', [(0, 1), (1, 0)])  6.28 us
    dot_general x1, matrix products, dot(): return jnp.dot(a, b, preferred_element_type=jnp.float32)  4.86 us
    all_to_all x1, starting transfers between devices, on_device(): lax.all_to_all(served, 'shard', split_axis=0, concat_axis=0, tiled=True)  4.25 us
    pallas_call x1, Pallas kernels, on_device(): pl.pallas_call(functools.partial(pick_kernel, plan), out_shape=[images(pa...  3.37 us
    concatenate x1, other arithmetic, on_device(): all_in = jnp.concatenate([w_in, far_in], axis=1)  3.09 us
  transfers between devices with their start and end apart: 25, of which 11 were waited for; matrix products, arithmetic and copies ran while one was open for 5% of the time, Pallas kernels for 5%

commit v1 on v0

--- a/solution.py
+++ b/solution.py
@@ -34,13 +34,13 @@
         self.base = self.capacity // 2 if split else self.capacity
         self.extra = self.capacity - self.base
         self.part = self.half * self.extra // 2
-        self.near_at = owner_count * self.base
-        self.rest_at = self.near_at + self.half * self.extra
+        self.far_at = self.half * self.capacity
+        self.rest_at = self.far_at + self.half * self.base
         self.slots = self.rest_at + 2 * self.part
         self.row = self.capacity + (self.half if split else 0)
 
 
-def place_kernel(plan, count, shard_ref, owner_ref, slot_ref, list_ref, *wanted_refs):
+def place_kernel(plan, count, shard_ref, owner_ref, slot_ref, wanted_ref, list_ref):
     total = 2 * count
     owners = plan.owners
     owner = jnp.concatenate([owner_ref[0:1, :], owner_ref[1:2, :]], axis=1)
@@ -69,19 +69,15 @@
         for index in range(owners - 1):
             before = before + jnp.where(row > index, far_over[index : index + 1], 0)
         before = jnp.sum(jnp.where(named, before, 0), axis=0, keepdims=True)
-        rest = rank - plan.base
-        near = plan.near_at + ((owner % half) ^ (me % half)) * plan.extra + rest
-        late = jnp.where(owner // half == me // half, near, plan.rest_at + before + rest)
-        where = jnp.where(rest < 0, where, late)
+        distance = (owner % half) ^ (me % half)
+        rest = plan.rest_at + before + rank - plan.base
+        direct = plan.far_at + distance * plan.base + rank
+        far = jnp.where(rank < plan.base, direct, rest)
+        where = jnp.where(owner // half != me // half, far, distance * plan.capacity + rank)
         told = place(1, owners) == plan.capacity + row % half
         wanted = wanted + jnp.sum(jnp.where(told, far_over, 0), axis=0, keepdims=True)
-    if plan.extra:
-        for distance, wanted_ref in enumerate(wanted_refs):
-            chosen = jnp.where(row == me ^ distance, wanted, 0)
-            wanted_ref[...] = jnp.sum(chosen, axis=0, keepdims=True)[:, : plan.row]
-    else:
-        for index in range(owners):
-            wanted_refs[0][index] = wanted[index : index + 1, : plan.row]
+    for index in range(owners):
+        wanted_ref[index] = wanted[index : index + 1, : plan.row]
     entry = place(1, 1)
     side = entry // count
     pair = entry % count
@@ -94,53 +90,51 @@
     list_ref[...] = listed[0:1] * 16 + listed[1:2]
 
 
-def serve(tokens_ref, incoming_ref, start, served_ref):
+def serve(tokens_ref, incoming_ref, requester, start, served_ref):
     count = served_ref.shape[0]
 
     def copy(index, carry):
-        served_ref[index] = tokens_ref[incoming_ref[0, start + index]]
+        served_ref[index] = tokens_ref[incoming_ref[requester, 0, start + index]]
         return carry
 
     lax.fori_loop(0, count, copy, 0, unroll=min(16, count))
 
 
-def serve_relays_kernel(plan, *refs):
-    incoming_refs, (tokens_ref, *served_refs) = refs[: plan.owners], refs[plan.owners :]
+def serve_relays_kernel(plan, shard_ref, incoming_ref, tokens_ref, *served_refs):
     *served_refs, crowded_ref = served_refs
-    for incoming_ref, served_ref in zip(incoming_refs[plan.half :], served_refs):
-        serve(tokens_ref, incoming_ref, plan.base, served_ref)
+    for distance, served_ref in enumerate(served_refs):
+        requester = shard_ref[0] ^ (distance + plan.half)
+        serve(tokens_ref, incoming_ref, requester, plan.base, served_ref)
     most = 0
-    for incoming_ref in incoming_refs:
+    for requester in range(plan.owners):
         total = 0
         for index in range(plan.half):
-            total = total + incoming_ref[0, plan.capacity + index]
+            total = total + incoming_ref[requester, 0, plan.capacity + index]
         most = jnp.maximum(most, total)
     crowded_ref[0] = jnp.where(most > plan.part, 1, 0)
 
 
-def serve_kernel(plan, shard_ref, *refs):
-    incoming_refs, (tokens_ref, served_ref, *near_refs) = refs[: plan.owners], refs[plan.owners :]
-    for distance, incoming_ref in enumerate(incoming_refs):
-        serve(tokens_ref, incoming_ref, 0, served_ref.at[shard_ref[0] ^ distance])
-    for incoming_ref, near_ref in zip(incoming_refs, near_refs):
-        serve(tokens_ref, incoming_ref, plan.base, near_ref)
+def serve_direct_kernel(plan, shard_ref, incoming_ref, tokens_ref, *served_refs):
+    for distance, served_ref in enumerate(served_refs):
+        serve(tokens_ref, incoming_ref, shard_ref[0] ^ distance, 0, served_ref)
 
 
 def serve_all_kernel(plan, incoming_ref, tokens_ref, served_ref):
     for requester in range(plan.owners):
-        serve(tokens_ref, incoming_ref.at[requester], 0, served_ref.at[requester])
+        serve(tokens_ref, incoming_ref, requester, 0, served_ref.at[requester])
 
 
 def relay_kernel(plan, shard_ref, incoming_ref, *refs):
     chunk_refs = refs[: plan.half]
     first_ref, second_ref = refs[plan.half :]
+    client = shard_ref[0] ^ plan.half
     for distance, chunk_ref in enumerate(chunk_refs):
         owner = (shard_ref[0] % plan.half) ^ distance
         at = 0
         for index in range(plan.half):
-            amount = incoming_ref[0, plan.capacity + index]
+            amount = incoming_ref[client, 0, plan.capacity + index]
             at = at + jnp.where(index < owner, amount, 0)
-        amount = incoming_ref[0, plan.capacity + owner]
+        amount = incoming_ref[client, 0, plan.capacity + owner]
         fit = jnp.clip(plan.part - at, 0, amount)
 
         def pack(index, carry, chunk_ref=chunk_ref, at=at):
@@ -367,54 +361,52 @@
     def limit(mebibytes):
         return pltpu.CompilerParams(vmem_limit_bytes=mebibytes * 2**20)
 
-    if plan.extra:
-        asked = [jax.ShapeDtypeStruct((1, plan.row), jnp.int32)] * owner_count
-    else:
-        asked = [jax.ShapeDtypeStruct((owner_count, 1, plan.row), jnp.int32)]
-    order, *wanted = pl.pallas_call(
+    wanted, order = pl.pallas_call(
         functools.partial(place_kernel, plan, pair_count),
-        out_shape=[jax.ShapeDtypeStruct((1, 2 * pair_count), jnp.int32), *asked],
+        out_shape=(
+            jax.ShapeDtypeStruct((owner_count, 1, plan.row), jnp.int32),
+            jax.ShapeDtypeStruct((1, 2 * pair_count), jnp.int32),
+        ),
         in_specs=[smem, vmem, vmem],
     )(shard, pair_owner.T, pair_slot.T)
-    if plan.extra:
-        incoming = [wanted[0]] + [across(wanted[k], k) for k in range(1, owner_count)]
-        incoming = lax.optimization_barrier(incoming)
-        *chunks, crowded = pl.pallas_call(
-            functools.partial(serve_relays_kernel, plan),
-            out_shape=[images(plan.extra)] * plan.half + [jax.ShapeDtypeStruct((1,), jnp.int32)],
-            in_specs=[smem] * owner_count + [vmem],
-            out_specs=[vmem] * plan.half + [smem],
-        )(*incoming, image_tokens)
-        incoming, chunks = lax.optimization_barrier((incoming, chunks))
-        chunks = [chunks[0]] + [across(chunks[k], k) for k in range(1, plan.half)]
-        served, *near = pl.pallas_call(
-            functools.partial(serve_kernel, plan),
-            out_shape=[images(owner_count, plan.base)] + [images(plan.extra)] * plan.half,
-            in_specs=[smem] * (1 + owner_count) + [vmem],
-        )(shard, *incoming, image_tokens)
-        served, near, chunks = lax.optimization_barrier((served, near, chunks))
-    else:
-        incoming = lax.all_to_all(wanted[0], "shard", split_axis=0, concat_axis=0, tiled=True)
+    incoming = lax.all_to_all(wanted, "shard", split_axis=0, concat_axis=0, tiled=True)
+    if not plan.extra:
         served = pl.pallas_call(
             functools.partial(serve_all_kernel, plan),
             out_shape=images(owner_count, plan.base),
             in_specs=[smem, vmem],
         )(incoming, image_tokens)
-    returned = lax.all_to_all(served, "shard", split_axis=0, concat_axis=0, tiled=True)
-    sources = [returned.reshape(-1, length, features)]
-    if plan.extra:
+        returned = lax.all_to_all(served, "shard", split_axis=0, concat_axis=0, tiled=True)
+        sources = [returned.reshape(-1, length, features)]
+    else:
+        *chunks, crowded = pl.pallas_call(
+            functools.partial(serve_relays_kernel, plan),
+            out_shape=[images(plan.extra)] * plan.half + [jax.ShapeDtypeStruct((1,), jnp.int32)],
+            in_specs=[smem, smem, vmem],
+            out_specs=[vmem] * plan.half + [smem],
+        )(shard, incoming, image_tokens)
+        incoming, chunks = lax.optimization_barrier((incoming, chunks))
+        chunks = [chunks[0]] + [across(chunks[k], k) for k in range(1, plan.half)]
+        served = pl.pallas_call(
+            functools.partial(serve_direct_kernel, plan),
+            out_shape=[images(plan.capacity)] * plan.half + [images(plan.base)] * plan.half,
+            in_specs=[smem, smem, vmem],
+        )(shard, incoming, image_tokens)
+        served, chunks = lax.optimization_barrier((served, chunks))
+        direct = [across(served[k], k) for k in range(plan.half, owner_count)]
         first, second = pl.pallas_call(
             functools.partial(relay_kernel, plan),
             out_shape=[images(plan.part)] * 2,
             in_specs=[smem, smem] + [vmem] * plan.half,
-        )(shard, incoming[plan.half], *chunks)
+        )(shard, incoming, *chunks)
+        near, first, crowded = lax.optimization_barrier((served[: plan.half], first, crowded))
         first = across(first, plan.half)
         near = [near[0]] + [across(near[k], k) for k in range(1, plan.half)]
         passed = crowded
         for _ in range(groups - 1):
             passed = lax.ppermute(passed, "groups", [(k, (k + 1) % groups) for k in range(groups)])
             crowded = jnp.maximum(crowded, passed)
-        sources += [*near, first]
+        sources = [*near, *direct, first]
     weights = (w_qk, w_value, w_out, w_in, w_back, bias_in, logit_scale)
     far_qk, far_value, far_out, far_in, far_back, far_bias, far_scale = [swap(w) for w in weights]
     all_in = jnp.concatenate([w_in, far_in], axis=1)

time: 94.1 us -> 104 us (1.11)
  blocking collectives: 0 us -> 13.7 us
  starting transfers between devices: 29.8 us -> 21.4 us
  waiting for transfers between devices: 26.6 us -> 31.6 us
    all_to_all x0 -> x1, blocking collectives: none -> 13.7 us  [on_device(): lax.all_to_all(wanted, 'shard', split_axis=0, concat_axis=0, tiled=True)]
    ppermute x14 -> x11, waiting for transfers between devices: 18.2 us -> 26.3 us  [across(): lax.ppermute(values, 'shard', [(k, k ^ distance) for k in range(owner_cou...]
    all_to_all x1 -> x0, starting transfers between devices: 4.25 us -> none  [on_device(): lax.all_to_all(served, 'shard', split_axis=0, concat_axis=0, tiled=True)]
    ppermute x14 -> x11, starting transfers between devices: 22.1 us -> 18.2 us  [across(): lax.ppermute(values, 'shard', [(k, k ^ distance) for k in range(owner_cou...]
    ppermute x9, waiting for transfers between devices: 6.28 us -> 3.23 us  [swap(): return lax.ppermute(values, 'mp', [(0, 1), (1, 0)])]
    unnamed x44 -> x36, local copies, waits for them, and re-layouts: 2.07 us -> 2.31 us
  transfers between devices with their start and end apart: 25 -> 21, of which waited for: 11 -> 8; matrix products, arithmetic and copies ran while one was open for 5% -> 4% of each run, Pallas kernels for 5% -> 9%
where the time goes in v1:
time: 104 us; the launch traced here: 103 us
  waiting for transfers between devices  31.6 us (30%)
  Pallas kernels  22.4 us (22%)
  starting transfers between devices  21.4 us (21%)
  blocking collectives  13.7 us (13%)
  other arithmetic  5.57 us (5%)
  matrix products  4.84 us (5%)
  local copies, waits for them, and re-layouts  2.31 us (2%)
  between operations  1.56 us (2%)
    ppermute x11, waiting for transfers between devices, across(): lax.ppermute(values, 'shard', [(k, k ^ distance) for k in range(owner_cou...  26.3 us
    ppermute x11, starting transfers between devices, across(): lax.ppermute(values, 'shard', [(k, k ^ distance) for k in range(owner_cou...  18.2 us
    all_to_all x1, blocking collectives, on_device(): lax.all_to_all(wanted, 'shard', split_axis=0, concat_axis=0, tiled=True)  13.7 us
    pallas_call x1, Pallas kernels, on_device(): pl.pallas_call(functools.partial(attention_kernel, length, head_dim), out...  9.13 us
    dot_general x1, matrix products, dot(): return jnp.dot(a, b, preferred_element_type=jnp.float32)  4.84 us
    pallas_call x1, Pallas kernels, on_device(): pl.pallas_call(functools.partial(pick_kernel, plan), out_shape=[images(pa...  3.34 us
    ppermute x9, waiting for transfers between devices, swap(): return lax.ppermute(values, 'mp', [(0, 1), (1, 0)])  3.23 us
    pallas_call x1, Pallas kernels, on_device(): pl.pallas_call(functools.partial(serve_direct_kernel, plan), out_shape=[i...  3.18 us
  transfers between devices with their start and end apart: 21, of which 8 were waited for; matrix products, arithmetic and copies ran while one was open for 4% of the time, Pallas kernels for 9%

profile of v1, /device:TPU:0, one launch (start us, length us, event | category | flops | bytes accessed | tf_op | source)
XLA Modules:
  0.0 103.4 jit_solution(9348989400277818183)
XLA Ops:
  0.6 1.8 %shard_map.118 = (s32[8,1,36]{2,1,0:T(1,128)}, s32[1,128]{1,0:T(1,128)}) custom-call(s32[1]{0:T(128)} %bitcast.1.shard_ref, s32[2,64]{1,0:T(2,128)} %bitcast.16, s32[2,64]{1,0:T(2,128)} %bitcast.17), custom_call_target="tpu_custom_call" | custom-call | tf_op jit(solution)/shard_map/pallas_call | solution.py:364
  2.4 13.7 %all_to_all.5.incoming_ref = s32[8,1,36]{2,1,0:T(1,128)} all-to-all(s32[8,1,36]{2,1,0:T(1,128)} %get-tuple-element.80), channel_id=1, replica_groups=mesh['groups'=2,'shard'=8,'mp'=2] {'shard'}, dimensions={0} | all-to-all | bytes 2304 | tf_op jit(solution)/shard_map/all_to_all | solution.py:372
  16.1 2.5 %shard_map.119 = (bf16[16,16,256]{2,1,0:T(8,128)(2,1)}, bf16[16,16,256]{2,1,0:T(8,128)(2,1)}, bf16[16,16,256]{2,1,0:T(8,128)(2,1)}, bf16[16,16,256]{2,1,0:T(8,128)(2,1)}, s32[1]{0:T(128)}) custom-call(s32[1]{0:T(128)} %bitcast.1.shard_ref, s32[8,1,36]{2,1,0:T(1,128)} %all_to_all.5.incoming_ref, bf16[256,16,256]{2,1,0:T(8,128)(2,1)} %tokens_ref.3), custom_call_target="tpu_custom_call" | custom-call | tf_op jit(solution)/shard_map/pallas_call | solution.py:382
  19.8 2.4 %collective-permute-start.3 = (bf16[16,16,256]{2,1,0:T(8,128)(2,1)}, bf16[16,16,256]{2,1,0:T(8,128)(2,1)S(1)}, u32[]{:S(2)}, u32[]{:S(2)}) collective-permute-start(bf16[16,16,256]{2,1,0:T(8,128)(2,1)} %get-tuple-element.97), channel_id=1, source_target_pairs={{0,6},{2,4},{4,2},{6,0},{8,14},{10,12},{12,10},{14,8},{1,7},{3,5},... | collective-permute-start | bytes 393224 | tf_op jit(solution)/shard_map/ppermute | solution.py:352
  22.2 3.1 %collective-permute-done.1.refs_1_ = bf16[16,16,256]{2,1,0:T(8,128)(2,1)S(1)} collective-permute-done((bf16[16,16,256]{2,1,0:T(8,128)(2,1)}, bf16[16,16,256]{2,1,0:T(8,128)(2,1)S(1)}, u32[]{:S(2)}, u32[]{:S(2)}) %collective-permute-start.1) | collective-permute-done | bytes 131104 | tf_op jit(solution)/shard_map/ppermute | solution.py:352
  25.8 3.2 %shard_map.120 = (bf16[32,16,256]{2,1,0:T(8,128)(2,1)}, bf16[32,16,256]{2,1,0:T(8,128)(2,1)}, bf16[32,16,256]{2,1,0:T(8,128)(2,1)}, bf16[32,16,256]{2,1,0:T(8,12...) custom-call(s32[1]{0:T(128)} %bitcast.1.shard_ref, ...), custom_call_target="tpu_custom_call" | custom-call | tf_op jit(solution)/shard_map/pallas_call | solution.py:390
  29.7 2.0 %shard_map.121 = (bf16[32,16,256]{2,1,0:T(8,128)(2,1)}, bf16[32,16,256]{2,1,0:T(8,128)(2,1)S(1)}) custom-call(s32[1]{0:T(128)} %bitcast.1.shard_ref, s32[8,1,36]{2,1,0:T(1,128)} %all_to_all.5.incoming_ref, bf16[16,16,256]{2,1,0:T(8,128)(2,1)} %get-tuple-element.102.refs_0_, bf16[16,16,256]{2,1,0:T(8,128)(2,1)} %copy-done.13, ...), custom_call_target="tpu_custom_call" | custom-call | tf_op jit(solution)/shard_map/pallas_call | solution.py:397
  31.8 1.5 %collective-permute-start.19 = (s32[1]{0:T(128)}, s32[1]{0:T(128)}, u32[]{:S(2)}, u32[]{:S(2)}) collective-permute-start(s32[1]{0:T(128)} %get-tuple-element.138), channel_id=1, source_target_pairs={{0,16},{16,0},{1,17},{17,1},{2,18},{18,2},{3,19},{19,3},{4,20},{20... | collective-permute-start | bytes 20 | tf_op jit(solution)/shard_map/ppermute | solution.py:407
  33.3 2.0 %collective-permute-done.19 = s32[1]{0:T(128)} collective-permute-done((s32[1]{0:T(128)}, s32[1]{0:T(128)}, u32[]{:S(2)}, u32[]{:S(2)}) %collective-permute-start.19) | collective-permute-done | bytes 36 | tf_op jit(solution)/shard_map/ppermute | solution.py:407
  36.1 2.4 %collective-permute-start.8 = (bf16[16,16,256]{2,1,0:T(8,128)(2,1)}, bf16[16,16,256]{2,1,0:T(8,128)(2,1)}, u32[]{:S(2)}, u32[]{:S(2)}) collective-permute-start(bf16[16,16,256]{2,1,0:T(8,128)(2,1)} %get-tuple-element.113), channel_id=1, source_target_pairs={{0,10},{2,8},{4,14},{6,12},{8,2},{10,0},{12,6},{14,4},{1,11},{3,9}... | collective-permute-start | bytes 393224 | tf_op jit(solution)/shard_map/ppermute | solution.py:352
  39.2 11.6 %collective-permute-done.7.refs_4_ = bf16[16,16,256]{2,1,0:T(8,128)(2,1)S(1)} collective-permute-done((bf16[16,16,256]{2,1,0:T(8,128)(2,1)}, bf16[16,16,256]{2,1,0:T(8,128)(2,1)S(1)}, u32[]{:S(2)}, u32[]{:S(2)}) %collective-permute-start.7) | collective-permute-done | bytes 131104 | tf_op jit(solution)/shard_map/ppermute | solution.py:352
  50.9 1.3 %collective-permute-start.10 = (bf16[16,16,256]{2,1,0:T(8,128)(2,1)}, bf16[16,16,256]{2,1,0:T(8,128)(2,1)}, u32[]{:S(2)}, u32[]{:S(2)}) collective-permute-start(bf16[16,16,256]{2,1,0:T(8,128)(2,1)} %get-tuple-element.115), channel_id=1, source_target_pairs={{0,14},{2,12},{4,10},{6,8},{8,6},{10,4},{12,2},{14,0},{1,15},{3,13... | collective-permute-start | bytes 393224 | tf_op jit(solution)/shard_map/ppermute | solution.py:352
  54.1 1.3 %collective-permute-start.4 = (bf16[32,16,256]{2,1,0:T(8,128)(2,1)}, bf16[32,16,256]{2,1,0:T(8,128)(2,1)S(1)}, u32[]{:S(2)}, u32[]{:S(2)}) collective-permute-start(bf16[32,16,256]{2,1,0:T(8,128)(2,1)} %get-tuple-element.109), channel_id=1, source_target_pairs={{0,2},{2,0},{4,6},{6,4},{8,10},{10,8},{12,14},{14,12},{1,3},{3,1},... | collective-permute-start | bytes 786440 | tf_op jit(solution)/shard_map/ppermute | solution.py:352
  55.4 4.5 %collective-permute-start.5 = (bf16[32,16,256]{2,1,0:T(8,128)(2,1)}, bf16[32,16,256]{2,1,0:T(8,128)(2,1)S(1)}, u32[]{:S(2)}, u32[]{:S(2)}) collective-permute-start(bf16[32,16,256]{2,1,0:T(8,128)(2,1)} %get-tuple-element.110), channel_id=1, source_target_pairs={{0,4},{2,6},{4,0},{6,2},{8,12},{10,14},{12,8},{14,10},{1,5},{3,7},... | collective-permute-start | bytes 786440 | tf_op jit(solution)/shard_map/ppermute | solution.py:352
  60.0 3.8 %collective-permute-start.6 = (bf16[32,16,256]{2,1,0:T(8,128)(2,1)}, bf16[32,16,256]{2,1,0:T(8,128)(2,1)S(1)}, u32[]{:S(2)}, u32[]{:S(2)}) collective-permute-start(bf16[32,16,256]{2,1,0:T(8,128)(2,1)} %get-tuple-element.111), channel_id=1, source_target_pairs={{0,6},{2,4},{4,2},{6,0},{8,14},{10,12},{12,10},{14,8},{1,7},{3,5},... | collective-permute-start | bytes 786440 | tf_op jit(solution)/shard_map/ppermute | solution.py:352
  63.7 3.1 %pad_maximum_fusion = bf16[512,2048]{1,0:T(8,128)(2,1)} fusion(bf16[512,1024]{1,0:T(8,128)(2,1)} %collective-permute-done.15, bf16[512,1024]{1,0:T(8,128)(2,1)} %param.23), kind=kLoop, calls=%fused_computation.10 | loop fusion | flops 4194304 | bytes 4194304 | tf_op jit(solution)/shard_map/concatenate | solution.py:412
  66.9 3.8 %collective-permute-done.5.refs_2_ = bf16[32,16,256]{2,1,0:T(8,128)(2,1)S(1)} collective-permute-done((bf16[32,16,256]{2,1,0:T(8,128)(2,1)}, bf16[32,16,256]{2,1,0:T(8,128)(2,1)S(1)}, u32[]{:S(2)}, u32[]{:S(2)}) %collective-permute-start.5) | collective-permute-done | bytes 262176 | tf_op jit(solution)/shard_map/ppermute | solution.py:352
  70.7 4.1 %collective-permute-done.6.refs_3_ = bf16[32,16,256]{2,1,0:T(8,128)(2,1)S(1)} collective-permute-done((bf16[32,16,256]{2,1,0:T(8,128)(2,1)}, bf16[32,16,256]{2,1,0:T(8,128)(2,1)S(1)}, u32[]{:S(2)}, u32[]{:S(2)}) %collective-permute-start.6) | collective-permute-done | bytes 262176 | tf_op jit(solution)/shard_map/ppermute | solution.py:352
  74.8 3.6 %collective-permute-done.11.refs_8_ = bf16[32,16,256]{2,1,0:T(8,128)(2,1)S(1)} collective-permute-done((bf16[32,16,256]{2,1,0:T(8,128)(2,1)}, bf16[32,16,256]{2,1,0:T(8,128)(2,1)S(1)}, u32[]{:S(2)}, u32[]{:S(2)}) %collective-permute-start.11) | collective-permute-done | bytes 262176 | tf_op jit(solution)/shard_map/ppermute | solution.py:352
  79.2 3.3 %shard_map.122 = (bf16[64,16,256]{2,1,0:T(8,128)(2,1)}, bf16[64,16,256]{2,1,0:T(8,128)(2,1)}) custom-call(s32[1]{0:T(128)} %bitcast.core_ref, s32[1,128]{1,0:T(1,128)} %get-tuple-element.118.list_ref, bf16[32,16,256]{2,1,0:T(8,128)(2,1)} %get-tuple-element.129.refs_0_, bf16[32,16,256]{2,1,0:T(8,128)(2,1)} %copy-done.9, bf16[32,16,256]{2,1,0:T(8,128)(2,1)} %copy-done.10, ...), custom_call_target="tpu_custom_call" | custom-call | tf_op jit(solution)/shard_map/pallas_call | solution.py:423
  82.6 2.1 %collective-permute-done.20.refs_1_ = bf16[64,16,256]{2,1,0:T(8,128)(2,1)S(1)} collective-permute-done((bf16[64,16,256]{2,1,0:T(8,128)(2,1)}, bf16[64,16,256]{2,1,0:T(8,128)(2,1)S(1)}, u32[]{:S(2)}, u32[]{:S(2)}) %collective-permute-start.20) | collective-permute-done | bytes 524320 | tf_op jit(solution)/shard_map/ppermute | solution.py:349
  85.8 9.1 %shard_map.123 = (bf16[1024,512]{1,0:T(8,128)(2,1)S(1)}, f32[32,512]{1,0:T(8,128)S(1)}) custom-call(s32[1]{0:T(128)} %bitcast.core_ref, f32[4]{0:T(128)S(1)} %copy-done.7, f32[4]{0:T(128)S(1)} %collective-permute-done.18.scale_b_ref, f32[1,512]{1,0:T(1,128)S(1)} %bitcast.13, f32[1,512]{1,0:T(1,128)S(1)} %bitcast.14, bf16[64,16,256]{2,1,0:T(8,128)(2,1)S(1)} %copy-done.1, ...), custom_call_target="tpu_custom_call" | custom-call | flops 1610612736 | bytes 4194304 | tf_op jit(solution)/shard_map/pallas_call | solution.py:434
  94.9 4.8 %fusion.7 = bf16[1024,2048]{1,0:T(8,128)(2,1)S(1)} fusion(f32[2048]{0:T(1024)} %pad_maximum_fusion.1, bf16[1024,512]{1,0:T(8,128)(2,1)S(1)} %get-tuple-element.146, bf16[512,2048]{1,0:T(8,128)(2,1)S(1)} %copy-done.8), kind=kOutput, calls=%fused_computation.8 | convolution fusion | flops 2168455168 | bytes 7348224 | tf_op jit(solution)/shard_map/dot_general | solution.py:25
  99.8 1.2 %convert_reduce_fusion = f32[4,8,2048]{2,1,0:T(8,128)S(1)} fusion(bf16[4,2,8,16,2048]{4,3,2,1,0:T(8,128)(2,1)S(1)} %bitcast.15), kind=kLoop, calls=%fused_computation.9 | loop fusion | flops 4128768 | bytes 4456448 | tf_op jit(solution)/shard_map/reduce_sum | solution.py:319
  (68 shorter events, 9.5 us)
Async XLA Ops:
  0.0 63.7 %collective-permute-start.15 = (bf16[512,1024]{1,0:T(8,128)(2,1)}, bf16[512,1024]{1,0:T(8,128)(2,1)}, u32[]{:S(2)}, u32[]{:S(2)}) collective-permute-start(bf16[512,1024]{1,0:T(8,128)(2,1)} %param.23), channel_id=1, source_target_pairs={{0,1},{1,0},{2,3},{3,2},{4,5},{5,4},{6,7},{7,6},{8,9},{9,8},{10,11... | collective-permute-start | bytes 3145736 | tf_op jit(solution)/shard_map/ppermute | solution.py:349
  0.5 77.9 %collective-permute-start.16 = (bf16[1024,512]{1,0:T(8,128)(2,1)}, bf16[1024,512]{1,0:T(8,128)(2,1)S(1)}, u32[]{:S(2)}, u32[]{:S(2)}) collective-permute-start(bf16[1024,512]{1,0:T(8,128)(2,1)} %back_ref.1), channel_id=1, source_target_pairs={{0,1},{1,0},{2,3},{3,2},{4,5},{5,4},{6,7},{7,6},{8,9},{9,8},{10,11... | collective-permute-start | bytes 3145736 | tf_op jit(solution)/shard_map/ppermute | solution.py:349
  18.6 6.6 %collective-permute-start.1 = (bf16[16,16,256]{2,1,0:T(8,128)(2,1)}, bf16[16,16,256]{2,1,0:T(8,128)(2,1)S(1)}, u32[]{:S(2)}, u32[]{:S(2)}) collective-permute-start(bf16[16,16,256]{2,1,0:T(8,128)(2,1)} %get-tuple-element.95), channel_id=1, source_target_pairs={{0,2},{2,0},{4,6},{6,4},{8,10},{10,8},{12,14},{14,12},{1,3},{3,1},... | collective-permute-start | bytes 393224 | tf_op jit(solution)/shard_map/ppermute | solution.py:352
  19.2 6.0 %collective-permute-start.2 = (bf16[16,16,256]{2,1,0:T(8,128)(2,1)}, bf16[16,16,256]{2,1,0:T(8,128)(2,1)S(1)}, u32[]{:S(2)}, u32[]{:S(2)}) collective-permute-start(bf16[16,16,256]{2,1,0:T(8,128)(2,1)} %get-tuple-element.96), channel_id=1, source_target_pairs={{0,4},{2,6},{4,0},{6,2},{8,12},{10,14},{12,8},{14,10},{1,5},{3,7},... | collective-permute-start | bytes 393224 | tf_op jit(solution)/shard_map/ppermute | solution.py:352
  19.8 9.2 %collective-permute-start.3 = (bf16[16,16,256]{2,1,0:T(8,128)(2,1)}, bf16[16,16,256]{2,1,0:T(8,128)(2,1)S(1)}, u32[]{:S(2)}, u32[]{:S(2)}) collective-permute-start(bf16[16,16,256]{2,1,0:T(8,128)(2,1)} %get-tuple-element.97), channel_id=1, source_target_pairs={{0,6},{2,4},{4,2},{6,0},{8,14},{10,12},{12,10},{14,8},{1,7},{3,5},... | collective-permute-start | bytes 393224 | tf_op jit(solution)/shard_map/ppermute | solution.py:352
  25.3 10.1 %collective-permute-start.12 = (bf16[512,256]{1,0:T(8,128)(2,1)}, bf16[512,256]{1,0:T(8,128)(2,1)S(1)}, u32[]{:S(2)}, u32[]{:S(2)}) collective-permute-start(bf16[512,256]{1,0:T(8,128)(2,1)} %refs_2_.1), channel_id=1, source_target_pairs={{0,1},{1,0},{2,3},{3,2},{4,5},{5,4},{6,7},{7,6},{8,9},{9,8},{10,11... | collective-permute-start | bytes 786440 | tf_op jit(solution)/shard_map/ppermute | solution.py:349
  25.3 6.5 %collective-permute-start.17 = (f32[1024]{0:T(1024)}, f32[1024]{0:T(1024)S(1)}, u32[]{:S(2)}, u32[]{:S(2)}) collective-permute-start(f32[1024]{0:T(1024)} %param.24), channel_id=1, source_target_pairs={{0,1},{1,0},{2,3},{3,2},{4,5},{5,4},{6,7},{7,6},{8,9},{9,8},{10,11... | collective-permute-start | bytes 12296 | tf_op jit(solution)/shard_map/ppermute | solution.py:349
  29.0 55.7 %copy-start.2 = (bf16[512,256]{1,0:T(8,128)(2,1)S(1)}, bf16[512,256]{1,0:T(8,128)(2,1)}, u32[]{:S(2)}) copy-start(bf16[512,256]{1,0:T(8,128)(2,1)} %refs_2_.1) | copy-start | bytes 786436
  29.0 55.7 %copy-start.5 = (f32[512]{0:T(512)S(1)}, f32[512]{0:T(512)}, u32[]{:S(2)}) copy-start(f32[512]{0:T(512)} %param.17) | copy-start | bytes 6148
  29.0 55.7 %copy-start.6 = (f32[512]{0:T(512)S(1)}, f32[512]{0:T(512)}, u32[]{:S(2)}) copy-start(f32[512]{0:T(512)} %param.22) | copy-start | bytes 6148
  29.0 2.7 %collective-permute-start.18 = (f32[4]{0:T(128)S(1)}, f32[4]{0:T(128)S(1)}, u32[]{:S(2)}, u32[]{:S(2)}) collective-permute-start(f32[4]{0:T(128)S(1)} %copy-done.7), channel_id=1, source_target_pairs={{0,1},{1,0},{2,3},{3,2},{4,5},{5,4},{6,7},{7,6},{8,9},{9,8},{10,11... | collective-permute-start | bytes 56 | tf_op jit(solution)/shard_map/ppermute | solution.py:349
  31.7 4.4 %collective-permute-start.13 = (bf16[512,256]{1,0:T(8,128)(2,1)S(1)}, bf16[512,256]{1,0:T(8,128)(2,1)S(1)}, u32[]{:S(2)}, u32[]{:S(2)}) collective-permute-start(bf16[512,256]{1,0:T(8,128)(2,1)S(1)} %copy-done.3), channel_id=1, source_target_pairs={{0,1},{1,0},{2,3},{3,2},{4,5},{5,4},{6,7},{7,6},{8,9},{9,8},{10,11... | collective-permute-start | bytes 786440 | tf_op jit(solution)/shard_map/ppermute | solution.py:349
  31.8 3.6 %collective-permute-start.19 = (s32[1]{0:T(128)}, s32[1]{0:T(128)}, u32[]{:S(2)}, u32[]{:S(2)}) collective-permute-start(s32[1]{0:T(128)} %get-tuple-element.138), channel_id=1, source_target_pairs={{0,16},{16,0},{1,17},{17,1},{2,18},{18,2},{3,19},{19,3},{4,20},{20... | collective-permute-start | bytes 20 | tf_op jit(solution)/shard_map/ppermute | solution.py:407
  35.4 3.0 %collective-permute-start.14 = (bf16[256,512]{1,0:T(8,128)(2,1)S(1)}, bf16[256,512]{1,0:T(8,128)(2,1)S(1)}, u32[]{:S(2)}, u32[]{:S(2)}) collective-permute-start(bf16[256,512]{1,0:T(8,128)(2,1)S(1)} %copy-done.4), channel_id=1, source_target_pairs={{0,1},{1,0},{2,3},{3,2},{4,5},{5,4},{6,7},{7,6},{8,9},{9,8},{10,11... | collective-permute-start | bytes 786440 | tf_op jit(solution)/shard_map/ppermute | solution.py:349
  35.4 15.5 %collective-permute-start.7 = (bf16[16,16,256]{2,1,0:T(8,128)(2,1)}, bf16[16,16,256]{2,1,0:T(8,128)(2,1)S(1)}, u32[]{:S(2)}, u32[]{:S(2)}) collective-permute-start(bf16[16,16,256]{2,1,0:T(8,128)(2,1)} %get-tuple-element.112), channel_id=1, source_target_pairs={{0,8},{2,10},{4,12},{6,14},{8,0},{10,2},{12,4},{14,6},{1,9},{3,11}... | collective-permute-start | bytes 393224 | tf_op jit(solution)/shard_map/ppermute | solution.py:352
  36.1 18.1 %collective-permute-start.8 = (bf16[16,16,256]{2,1,0:T(8,128)(2,1)}, bf16[16,16,256]{2,1,0:T(8,128)(2,1)}, u32[]{:S(2)}, u32[]{:S(2)}) collective-permute-start(bf16[16,16,256]{2,1,0:T(8,128)(2,1)} %get-tuple-element.113), channel_id=1, source_target_pairs={{0,10},{2,8},{4,14},{6,12},{8,2},{10,0},{12,6},{14,4},{1,11},{3,9}... | collective-permute-start | bytes 393224 | tf_op jit(solution)/shard_map/ppermute | solution.py:352
  38.4 17.0 %collective-permute-start.9 = (bf16[16,16,256]{2,1,0:T(8,128)(2,1)}, bf16[16,16,256]{2,1,0:T(8,128)(2,1)}, u32[]{:S(2)}, u32[]{:S(2)}) collective-permute-start(bf16[16,16,256]{2,1,0:T(8,128)(2,1)} %get-tuple-element.114), channel_id=1, source_target_pairs={{0,12},{2,14},{4,8},{6,10},{8,4},{10,6},{12,0},{14,2},{1,13},{3,15... | collective-permute-start | bytes 393224 | tf_op jit(solution)/shard_map/ppermute | solution.py:352
  50.9 9.1 %collective-permute-start.10 = (bf16[16,16,256]{2,1,0:T(8,128)(2,1)}, bf16[16,16,256]{2,1,0:T(8,128)(2,1)}, u32[]{:S(2)}, u32[]{:S(2)}) collective-permute-start(bf16[16,16,256]{2,1,0:T(8,128)(2,1)} %get-tuple-element.115), channel_id=1, source_target_pairs={{0,14},{2,12},{4,10},{6,8},{8,6},{10,4},{12,2},{14,0},{1,15},{3,13... | collective-permute-start | bytes 393224 | tf_op jit(solution)/shard_map/ppermute | solution.py:352
  54.1 12.7 %collective-permute-start.4 = (bf16[32,16,256]{2,1,0:T(8,128)(2,1)}, bf16[32,16,256]{2,1,0:T(8,128)(2,1)S(1)}, u32[]{:S(2)}, u32[]{:S(2)}) collective-permute-start(bf16[32,16,256]{2,1,0:T(8,128)(2,1)} %get-tuple-element.109), channel_id=1, source_target_pairs={{0,2},{2,0},{4,6},{6,4},{8,10},{10,8},{12,14},{14,12},{1,3},{3,1},... | collective-permute-start | bytes 786440 | tf_op jit(solution)/shard_map/ppermute | solution.py:352
  55.4 15.3 %collective-permute-start.5 = (bf16[32,16,256]{2,1,0:T(8,128)(2,1)}, bf16[32,16,256]{2,1,0:T(8,128)(2,1)S(1)}, u32[]{:S(2)}, u32[]{:S(2)}) collective-permute-start(bf16[32,16,256]{2,1,0:T(8,128)(2,1)} %get-tuple-element.110), channel_id=1, source_target_pairs={{0,4},{2,6},{4,0},{6,2},{8,12},{10,14},{12,8},{14,10},{1,5},{3,7},... | collective-permute-start | bytes 786440 | tf_op jit(solution)/shard_map/ppermute | solution.py:352
  60.0 14.9 %collective-permute-start.6 = (bf16[32,16,256]{2,1,0:T(8,128)(2,1)}, bf16[32,16,256]{2,1,0:T(8,128)(2,1)S(1)}, u32[]{:S(2)}, u32[]{:S(2)}) collective-permute-start(bf16[32,16,256]{2,1,0:T(8,128)(2,1)} %get-tuple-element.111), channel_id=1, source_target_pairs={{0,6},{2,4},{4,2},{6,0},{8,14},{10,12},{12,10},{14,8},{1,7},{3,5},... | collective-permute-start | bytes 786440 | tf_op jit(solution)/shard_map/ppermute | solution.py:352
  63.7 14.7 %collective-permute-start.11 = (bf16[32,16,256]{2,1,0:T(8,128)(2,1)}, bf16[32,16,256]{2,1,0:T(8,128)(2,1)S(1)}, u32[]{:S(2)}, u32[]{:S(2)}) collective-permute-start(bf16[32,16,256]{2,1,0:T(8,128)(2,1)} %get-tuple-element.116), channel_id=1, source_target_pairs={{0,8},{2,10},{4,12},{6,14},{8,0},{10,2},{12,4},{14,6},{1,9},{3,11}... | collective-permute-start | bytes 786440 | tf_op jit(solution)/shard_map/ppermute | solution.py:352
  82.5 2.2 %collective-permute-start.20 = (bf16[64,16,256]{2,1,0:T(8,128)(2,1)}, bf16[64,16,256]{2,1,0:T(8,128)(2,1)S(1)}, u32[]{:S(2)}, u32[]{:S(2)}) collective-permute-start(bf16[64,16,256]{2,1,0:T(8,128)(2,1)} %get-tuple-element.141), channel_id=1, source_target_pairs={{0,1},{1,0},{2,3},{3,2},{4,5},{5,4},{6,7},{7,6},{8,9},{9,8},{10,11... | collective-permute-start | bytes 1572872 | tf_op jit(solution)/shard_map/ppermute | solution.py:349
  101.5 1.3 %collective-permute-start.21 = (bf16[64,512]{1,0:T(8,128)(2,1)S(1)}, bf16[64,512]{1,0:T(8,128)(2,1)S(1)}, u32[]{:S(2)}, u32[]{:S(2)}) collective-permute-start(bf16[64,512]{1,0:T(8,128)(2,1)S(1)} %shard_map.124), channel_id=1, source_target_pairs={{0,1},{1,0},{2,3},{3,2},{4,5},{5,4},{6,7},{7,6},{8,9},{9,8},{10,11... | collective-permute-start | bytes 196616 | tf_op jit(solution)/shard_map/ppermute | solution.py:349
  (15 other events, 221.5 us)

commit v2 on v1

--- a/solution.py
+++ b/solution.py
@@ -34,8 +34,8 @@
         self.base = self.capacity // 2 if split else self.capacity
         self.extra = self.capacity - self.base
         self.part = self.half * self.extra // 2
-        self.far_at = self.half * self.capacity
-        self.rest_at = self.far_at + self.half * self.base
+        self.near_at = owner_count * self.base
+        self.rest_at = self.near_at + self.half * self.extra
         self.slots = self.rest_at + 2 * self.part
         self.row = self.capacity + (self.half if split else 0)
 
@@ -69,11 +69,10 @@
         for index in range(owners - 1):
             before = before + jnp.where(row > index, far_over[index : index + 1], 0)
         before = jnp.sum(jnp.where(named, before, 0), axis=0, keepdims=True)
-        distance = (owner % half) ^ (me % half)
-        rest = plan.rest_at + before + rank - plan.base
-        direct = plan.far_at + distance * plan.base + rank
-        far = jnp.where(rank < plan.base, direct, rest)
-        where = jnp.where(owner // half != me // half, far, distance * plan.capacity + rank)
+        rest = rank - plan.base
+        near = plan.near_at + ((owner % half) ^ (me % half)) * plan.extra + rest
+        late = jnp.where(owner // half == me // half, near, plan.rest_at + before + rest)
+        where = jnp.where(rest < 0, where, late)
         told = place(1, owners) == plan.capacity + row % half
         wanted = wanted + jnp.sum(jnp.where(told, far_over, 0), axis=0, keepdims=True)
     for index in range(owners):
@@ -100,11 +99,16 @@
     lax.fori_loop(0, count, copy, 0, unroll=min(16, count))
 
 
-def serve_relays_kernel(plan, shard_ref, incoming_ref, tokens_ref, *served_refs):
-    *served_refs, crowded_ref = served_refs
-    for distance, served_ref in enumerate(served_refs):
-        requester = shard_ref[0] ^ (distance + plan.half)
-        serve(tokens_ref, incoming_ref, requester, plan.base, served_ref)
+def serve_kernel(plan, shard_ref, incoming_ref, tokens_ref, *refs):
+    relay_refs, near_refs = refs[: plan.half], refs[plan.half + 1 : -1]
+    served_ref, crowded_ref = refs[plan.half], refs[-1]
+    me = shard_ref[0]
+    for distance, relay_ref in enumerate(relay_refs):
+        serve(tokens_ref, incoming_ref, me ^ (distance + plan.half), plan.base, relay_ref)
+    for requester in range(plan.owners):
+        serve(tokens_ref, incoming_ref, requester, 0, served_ref.at[requester])
+    for distance, near_ref in enumerate(near_refs):
+        serve(tokens_ref, incoming_ref, me ^ distance, plan.base, near_ref)
     most = 0
     for requester in range(plan.owners):
         total = 0
@@ -112,11 +116,6 @@
             total = total + incoming_ref[requester, 0, plan.capacity + index]
         most = jnp.maximum(most, total)
     crowded_ref[0] = jnp.where(most > plan.part, 1, 0)
-
-
-def serve_direct_kernel(plan, shard_ref, incoming_ref, tokens_ref, *served_refs):
-    for distance, served_ref in enumerate(served_refs):
-        serve(tokens_ref, incoming_ref, shard_ref[0] ^ distance, 0, served_ref)
 
 
 def serve_all_kernel(plan, incoming_ref, tokens_ref, served_ref):
@@ -379,34 +378,36 @@
         returned = lax.all_to_all(served, "shard", split_axis=0, concat_axis=0, tiled=True)
         sources = [returned.reshape(-1, length, features)]
     else:
-        *chunks, crowded = pl.pallas_call(
-            functools.partial(serve_relays_kernel, plan),
-            out_shape=[images(plan.extra)] * plan.half + [jax.ShapeDtypeStruct((1,), jnp.int32)],
+        outs = pl.pallas_call(
+            functools.partial(serve_kernel, plan),
+            out_shape=[images(plan.extra)] * plan.half
+            + [images(owner_count, plan.base)]
+            + [images(plan.extra)] * plan.half
+            + [jax.ShapeDtypeStruct((1,), jnp.int32)],
             in_specs=[smem, smem, vmem],
-            out_specs=[vmem] * plan.half + [smem],
+            out_specs=[vmem] * (2 * plan.half + 1) + [smem],
         )(shard, incoming, image_tokens)
-        incoming, chunks = lax.optimization_barrier((incoming, chunks))
+        chunks, near, crowded = outs[: plan.half], outs[plan.half + 1 : -1], outs[-1]
         chunks = [chunks[0]] + [across(chunks[k], k) for k in range(1, plan.half)]
-        served = pl.pallas_call(
-            functools.partial(serve_direct_kernel, plan),
-            out_shape=[images(plan.capacity)] * plan.half + [images(plan.base)] * plan.half,
-            in_specs=[smem, smem, vmem],
-        )(shard, incoming, image_tokens)
-        served, chunks = lax.optimization_barrier((served, chunks))
-        direct = [across(served[k], k) for k in range(plan.half, owner_count)]
+        returned = lax.all_to_all(
+            outs[plan.half], "shard", split_axis=0, concat_axis=0, tiled=True
+        ).reshape(-1, length, features)
         first, second = pl.pallas_call(
             functools.partial(relay_kernel, plan),
             out_shape=[images(plan.part)] * 2,
             in_specs=[smem, smem] + [vmem] * plan.half,
+            cost_estimate=pl.CostEstimate(
+                flops=2 * 10**11, bytes_accessed=2**20, transcendentals=0
+            ),
         )(shard, incoming, *chunks)
-        near, first, crowded = lax.optimization_barrier((served[: plan.half], first, crowded))
+        near, first, crowded = lax.optimization_barrier((near, first, crowded))
         first = across(first, plan.half)
         near = [near[0]] + [across(near[k], k) for k in range(1, plan.half)]
         passed = crowded
         for _ in range(groups - 1):
             passed = lax.ppermute(passed, "groups", [(k, (k + 1) % groups) for k in range(groups)])
             crowded = jnp.maximum(crowded, passed)
-        sources = [*near, *direct, first]
+        sources = [returned, *near, first]
     weights = (w_qk, w_value, w_out, w_in, w_back, bias_in, logit_scale)
     far_qk, far_value, far_out, far_in, far_back, far_bias, far_scale = [swap(w) for w in weights]
     all_in = jnp.concatenate([w_in, far_in], axis=1)
@@ -437,7 +438,7 @@
             jax.ShapeDtypeStruct((token_count, width), jnp.bfloat16),
             jax.ShapeDtypeStruct((mine, width), jnp.float32),
         ),
-        in_specs=[smem] * 3 + [vmem] * 2 + [hbm] * 8,
+        in_specs=[smem] * 3 + [vmem] * 4 + [hbm] * 6,
         scratch_shapes=[
             pltpu.VMEM((width, 2 * width), jnp.bfloat16),
             pltpu.VMEM((width, width), jnp.bfloat16),

time: 104 us -> 90.9 us (0.87)
  waiting for transfers between devices: 31.6 us -> 25.2 us
  starting transfers between devices: 21.4 us -> 17.1 us
    ppermute x11 -> x7, starting transfers between devices: 18.2 us -> 9.86 us  [across(): lax.ppermute(values, 'shard', [(k, k ^ distance) for k in range(owner_cou...]
    ppermute x11 -> x7, waiting for transfers between devices: 26.3 us -> 19.5 us  [across(): lax.ppermute(values, 'shard', [(k, k ^ distance) for k in range(owner_cou...]
    all_to_all x0 -> x1, starting transfers between devices: none -> 4.24 us  [on_device(): lax.all_to_all(outs[plan.half], 'shard', split_axis=0, concat_axis=0, til...]
    pallas_call x2 -> x1, Pallas kernels: 5.67 us -> 3.22 us  [on_device(): pl.pallas_call(functools.partial(serve_kernel, plan), out_shape=[images(p...]
    pallas_call x1, Pallas kernels: 0.47 us -> 2.03 us  [on_device(): pl.pallas_call(functools.partial(back_kernel, length), out_shape=jax.Shap...]
    concatenate x1, other arithmetic: 3.12 us -> 1.74 us  [on_device(): all_in = jnp.concatenate([w_in, far_in], axis=1)]
    unnamed x36 -> x22, local copies, waits for them, and re-layouts: 2.31 us -> 1.61 us
  transfers between devices with their start and end apart: 21 -> 18, of which waited for: 8 -> 7; matrix products, arithmetic and copies ran while one was open for 4% -> 3% of each run, Pallas kernels for 9% -> 2%
where the time goes in v2:
time: 90.9 us; the launch traced here: 90.4 us
  waiting for transfers between devices  25.2 us (28%)
  Pallas kernels  21.6 us (24%)
  starting transfers between devices  17.1 us (19%)
  blocking collectives  13.8 us (15%)
  other arithmetic  4.87 us (5%)
  matrix products  4.85 us (5%)
  local copies, waits for them, and re-layouts  1.61 us (2%)
  between operations  1.39 us (2%)
    ppermute x7, waiting for transfers between devices, across(): lax.ppermute(values, 'shard', [(k, k ^ distance) for k in range(owner_cou...  19.5 us
    all_to_all x1, blocking collectives, on_device(): lax.all_to_all(wanted, 'shard', split_axis=0, concat_axis=0, tiled=True)  13.8 us
    ppermute x7, starting transfers between devices, across(): lax.ppermute(values, 'shard', [(k, k ^ distance) for k in range(owner_cou...  9.86 us
    pallas_call x1, Pallas kernels, on_device(): pl.pallas_call(functools.partial(attention_kernel, length, head_dim), out...  9.18 us
    dot_general x1, matrix products, dot(): return jnp.dot(a, b, preferred_element_type=jnp.float32)  4.85 us
    all_to_all x1, starting transfers between devices, on_device(): lax.all_to_all(outs[plan.half], 'shard', split_axis=0, concat_axis=0, til...  4.24 us
    pallas_call x1, Pallas kernels, on_device(): pl.pallas_call(functools.partial(pick_kernel, plan), out_shape=[images(pa...  3.33 us
    ppermute x9, waiting for transfers between devices, swap(): return lax.ppermute(values, 'mp', [(0, 1), (1, 0)])  3.23 us
  transfers between devices with their start and end apart: 18, of which 7 were waited for; matrix products, arithmetic and copies ran while one was open for 3% of the time, Pallas kernels for 2%

profile of v2, /device:TPU:0, one launch (start us, length us, event | category | flops | bytes accessed | tf_op | source)
XLA Modules:
  0.0 90.4 jit_solution(5398854134967145537)
XLA Ops:
  0.0 1.8 %shard_map.118 = (s32[8,1,36]{2,1,0:T(1,128)}, s32[1,128]{1,0:T(1,128)}) custom-call(s32[1]{0:T(128)} %bitcast.1.shard_ref, s32[2,64]{1,0:T(2,128)} %bitcast.17, s32[2,64]{1,0:T(2,128)} %bitcast.18), custom_call_target="tpu_custom_call" | custom-call | tf_op jit(solution)/shard_map/pallas_call | solution.py:363
  1.8 13.8 %all_to_all.10.incoming_ref = s32[8,1,36]{2,1,0:T(1,128)} all-to-all(s32[8,1,36]{2,1,0:T(1,128)} %get-tuple-element.54), channel_id=1, replica_groups=mesh['groups'=2,'shard'=8,'mp'=2] {'shard'}, dimensions={0} | all-to-all | bytes 2304 | tf_op jit(solution)/shard_map/all_to_all | solution.py:371
  15.5 3.2 %shard_map.119 = (bf16[16,16,256]{2,1,0:T(8,128)(2,1)}, bf16[16,16,256]{2,1,0:T(8,128)(2,1)}, bf16[16,16,256]{2,1,0:T(8,128)(2,1)}, bf16[16,16,256]{2,1,0:T(8,12...) custom-call(s32[1]{0:T(128)} %bitcast.1.shard_ref, ...), custom_call_target="tpu_custom_call" | custom-call | tf_op jit(solution)/shard_map/pallas_call | solution.py:381
  20.0 2.4 %collective-permute-start.3 = (bf16[16,16,256]{2,1,0:T(8,128)(2,1)}, bf16[16,16,256]{2,1,0:T(8,128)(2,1)S(1)}, u32[]{:S(2)}, u32[]{:S(2)}) collective-permute-start(bf16[16,16,256]{2,1,0:T(8,128)(2,1)} %get-tuple-element.63), channel_id=1, source_target_pairs={{0,6},{2,4},{4,2},{6,0},{8,14},{10,12},{12,10},{14,8},{1,7},{3,5},... | collective-permute-start | bytes 393224 | tf_op jit(solution)/shard_map/ppermute | solution.py:351
  22.8 4.2 %all-to-all-start.1 = ((bf16[8,16,16,256]{3,2,1,0:T(8,128)(2,1)}), bf16[8,16,16,256]{3,2,1,0:T(8,128)(2,1)}, u32[]{:S(2)}, u32[]{:S(2)}) async-start(bf16[8,16,16,256]{3,2,1,0:T(8,128)(2,1)} %get-tuple-element.55), calls=%async_computation.1 | async-start | bytes 2097152 | tf_op jit(solution)/shard_map/all_to_all | solution.py:392
  28.3 2.1 %shard_map.120 = (bf16[32,16,256]{2,1,0:T(8,128)(2,1)}, bf16[32,16,256]{2,1,0:T(8,128)(2,1)S(1)}) custom-call(s32[1]{0:T(128)} %bitcast.1.shard_ref, s32[8,1,36]{2,1,0:T(1,128)} %all_to_all.10.incoming_ref, bf16[16,16,256]{2,1,0:T(8,128)(2,1)} %get-tuple-element.60.refs_0_, bf16[16,16,256]{2,1,0:T(8,128)(2,1)} %copy-done.8, bf16[16,16,256]{2,1,0:T(8,128)(2,1)} %copy-done.9, ...), custom_call_target="tpu_custom_call" | custom-call | flops 199999995904 | bytes 1048576 | tf_op jit(solution)/shard_map/pallas_call | solution.py:395
  30.6 1.4 %collective-permute-start.15 = (s32[1]{0:T(128)}, s32[1]{0:T(128)}, u32[]{:S(2)}, u32[]{:S(2)}) collective-permute-start(s32[1]{0:T(128)} %get-tuple-element.86), channel_id=1, source_target_pairs={{0,16},{16,0},{1,17},{17,1},{2,18},{18,2},{3,19},{19,3},{4,20},{20... | collective-permute-start | bytes 20 | tf_op jit(solution)/shard_map/ppermute | solution.py:408
  32.0 2.5 %collective-permute-done.15 = s32[1]{0:T(128)} collective-permute-done((s32[1]{0:T(128)}, s32[1]{0:T(128)}, u32[]{:S(2)}, u32[]{:S(2)}) %collective-permute-start.15) | collective-permute-done | bytes 36 | tf_op jit(solution)/shard_map/ppermute | solution.py:408
  34.5 1.3 %pad_maximum_fusion.1 = f32[2048]{0:T(1024)} fusion(f32[1024]{0:T(1024)} %collective-permute-done.13, f32[1024]{0:T(1024)S(1)} %copy-done.7), kind=kLoop, calls=%fused_computation.11 | loop fusion | flops 2048 | bytes 16384 | tf_op jit(solution)/shard_map/concatenate | solution.py:414
  37.0 2.0 %collective-permute-start.4 = (bf16[16,16,256]{2,1,0:T(8,128)(2,1)}, bf16[16,16,256]{2,1,0:T(8,128)(2,1)S(1)}, u32[]{:S(2)}, u32[]{:S(2)}) collective-permute-start(bf16[16,16,256]{2,1,0:T(8,128)(2,1)} %get-tuple-element.67), channel_id=1, source_target_pairs={{0,2},{2,0},{4,6},{6,4},{8,10},{10,8},{12,14},{14,12},{1,3},{3,1},... | collective-permute-start | bytes 393224 | tf_op jit(solution)/shard_map/ppermute | solution.py:351
  39.0 1.4 %collective-permute-start.5 = (bf16[16,16,256]{2,1,0:T(8,128)(2,1)}, bf16[16,16,256]{2,1,0:T(8,128)(2,1)}, u32[]{:S(2)}, u32[]{:S(2)}) collective-permute-start(bf16[16,16,256]{2,1,0:T(8,128)(2,1)} %get-tuple-element.68), channel_id=1, source_target_pairs={{0,4},{2,6},{4,0},{6,2},{8,12},{10,14},{12,8},{14,10},{1,5},{3,7},... | collective-permute-start | bytes 393224 | tf_op jit(solution)/shard_map/ppermute | solution.py:351
  40.6 2.7 %collective-permute-start.7 = (bf16[32,16,256]{2,1,0:T(8,128)(2,1)}, bf16[32,16,256]{2,1,0:T(8,128)(2,1)}, u32[]{:S(2)}, u32[]{:S(2)}) collective-permute-start(bf16[32,16,256]{2,1,0:T(8,128)(2,1)} %get-tuple-element.70), channel_id=1, source_target_pairs={{0,8},{2,10},{4,12},{6,14},{8,0},{10,2},{12,4},{14,6},{1,9},{3,11}... | collective-permute-start | bytes 786440 | tf_op jit(solution)/shard_map/ppermute | solution.py:351
  43.3 1.7 %pad_maximum_fusion = bf16[512,2048]{1,0:T(8,128)(2,1)S(1)} fusion(bf16[512,1024]{1,0:T(8,128)(2,1)} %collective-permute-done.11, bf16[512,1024]{1,0:T(8,128)(2,1)} %param.23), kind=kLoop, calls=%fused_computation.10 | loop fusion | flops 4194304 | bytes 4194304 | tf_op jit(solution)/shard_map/concatenate | solution.py:413
  46.0 2.8 %collective-permute-done.5.refs_3_ = bf16[16,16,256]{2,1,0:T(8,128)(2,1)} collective-permute-done((bf16[16,16,256]{2,1,0:T(8,128)(2,1)}, bf16[16,16,256]{2,1,0:T(8,128)(2,1)}, u32[]{:S(2)}, u32[]{:S(2)}) %collective-permute-start.5) | collective-permute-done | bytes 131104 | tf_op jit(solution)/shard_map/ppermute | solution.py:351
  48.8 2.8 %collective-permute-done.6.refs_4_ = bf16[16,16,256]{2,1,0:T(8,128)(2,1)} collective-permute-done((bf16[16,16,256]{2,1,0:T(8,128)(2,1)}, bf16[16,16,256]{2,1,0:T(8,128)(2,1)}, u32[]{:S(2)}, u32[]{:S(2)}) %collective-permute-start.6) | collective-permute-done | bytes 131104 | tf_op jit(solution)/shard_map/ppermute | solution.py:351
  51.6 12.9 %collective-permute-done.7.refs_5_ = bf16[32,16,256]{2,1,0:T(8,128)(2,1)} collective-permute-done((bf16[32,16,256]{2,1,0:T(8,128)(2,1)}, bf16[32,16,256]{2,1,0:T(8,128)(2,1)}, u32[]{:S(2)}, u32[]{:S(2)}) %collective-permute-start.7) | collective-permute-done | bytes 262176 | tf_op jit(solution)/shard_map/ppermute | solution.py:351
  64.5 3.3 %shard_map.121 = (bf16[64,16,256]{2,1,0:T(8,128)(2,1)}, bf16[64,16,256]{2,1,0:T(8,128)(2,1)}) custom-call(s32[1]{0:T(128)} %bitcast.core_ref, s32[1,128]{1,0:T(1,128)} %get-tuple-element.72.list_ref, bf16[128,16,256]{2,1,0:T(8,128)(2,1)} %bitcast.4.refs_0_, bf16[16,16,256]{2,1,0:T(8,128)(2,1)} %get-tuple-element.81.refs_1_, bf16[16,16,256]{2,1,0:T(8,128)(2,1)} %copy-done.6, ...), custom_call_target="tpu_custom_call" | custom-call | tf_op jit(solution)/shard_map/pallas_call | solution.py:424
  68.0 2.1 %collective-permute-done.16.refs_1_ = bf16[64,16,256]{2,1,0:T(8,128)(2,1)S(1)} collective-permute-done((bf16[64,16,256]{2,1,0:T(8,128)(2,1)}, bf16[64,16,256]{2,1,0:T(8,128)(2,1)S(1)}, u32[]{:S(2)}, u32[]{:S(2)}) %collective-permute-start.16) | collective-permute-done | bytes 524320 | tf_op jit(solution)/shard_map/ppermute | solution.py:348
  70.1 1.0 %copy-done = bf16[64,16,256]{2,1,0:T(8,128)(2,1)S(1)} copy-done((bf16[64,16,256]{2,1,0:T(8,128)(2,1)S(1)}, bf16[64,16,256]{2,1,0:T(8,128)(2,1)}, u32[]{:S(2)}) %copy-start) | copy-done | bytes 524312
  71.1 9.2 %shard_map.122 = (bf16[1024,512]{1,0:T(8,128)(2,1)S(1)}, f32[32,512]{1,0:T(8,128)S(1)}) custom-call(s32[1]{0:T(128)} %bitcast.core_ref, f32[4]{0:T(128)S(1)} %copy-done.5, f32[4]{0:T(128)} %collective-permute-done.14.scale_b_ref, f32[1,512]{1,0:T(1,128)S(1)} %bitcast.14, f32[1,512]{1,0:T(1,128)S(1)} %bitcast.15, bf16[64,16,256]{2,1,0:T(8,128)(2,1)S(1)} %copy-done, ...), custom_call_target="tpu_custom_call" | custom-call | flops 1610612736 | bytes 4194304 | tf_op jit(solution)/shard_map/pallas_call | solution.py:435
  80.3 4.8 %fusion.7 = bf16[1024,2048]{1,0:T(8,128)(2,1)S(1)} fusion(f32[2048]{0:T(1024)} %pad_maximum_fusion.1, bf16[1024,512]{1,0:T(8,128)(2,1)S(1)} %get-tuple-element.94, bf16[512,2048]{1,0:T(8,128)(2,1)S(1)} %pad_maximum_fusion), kind=kOutput, calls=%fused_computation.8 | convolution fusion | flops 2168455168 | bytes 7348224 | tf_op jit(solution)/shard_map/dot_general | solution.py:25
  85.2 1.2 %convert_reduce_fusion = f32[4,8,2048]{2,1,0:T(8,128)S(1)} fusion(bf16[4,2,8,16,2048]{4,3,2,1,0:T(8,128)(2,1)S(1)} %bitcast.16), kind=kLoop, calls=%fused_computation.9 | loop fusion | flops 4128768 | bytes 4456448 | tf_op jit(solution)/shard_map/reduce_sum | solution.py:318
  86.4 2.0 %shard_map.123 = bf16[64,512]{1,0:T(8,128)(2,1)S(1)} custom-call(s32[1]{0:T(128)} %bitcast.core_ref, f32[32,512]{1,0:T(8,128)S(1)} %get-tuple-element.93.mean_ref, f32[32,2048]{1,0:T(8,128)S(1)} %bitcast.13, bf16[1024,512]{1,0:T(8,128)(2,1)} %back_ref.1, bf16[1024,512]{1,0:T(8,128)(2,1)} %collective-permute-done.12.far_back_ref), custom_call_target="tpu_custom_call" | custom-call | tf_op jit(solution)/shard_map/pallas_call | solution.py:473
  88.6 1.1 %collective-permute-done.17 = bf16[64,512]{1,0:T(8,128)(2,1)S(1)} collective-permute-done((bf16[64,512]{1,0:T(8,128)(2,1)S(1)}, bf16[64,512]{1,0:T(8,128)(2,1)S(1)}, u32[]{:S(2)}, u32[]{:S(2)}) %collective-permute-start.17) | collective-permute-done | bytes 65568 | tf_op jit(solution)/shard_map/ppermute | solution.py:348
  (47 shorter events, 5.1 us)
Async XLA Ops:
  18.8 8.3 %collective-permute-start.1 = (bf16[16,16,256]{2,1,0:T(8,128)(2,1)}, bf16[16,16,256]{2,1,0:T(8,128)(2,1)S(1)}, u32[]{:S(2)}, u32[]{:S(2)}) collective-permute-start(bf16[16,16,256]{2,1,0:T(8,128)(2,1)} %get-tuple-element.61), channel_id=1, source_target_pairs={{0,2},{2,0},{4,6},{6,4},{8,10},{10,8},{12,14},{14,12},{1,3},{3,1},... | collective-permute-start | bytes 393224 | tf_op jit(solution)/shard_map/ppermute | solution.py:351
  19.4 7.8 %collective-permute-start.2 = (bf16[16,16,256]{2,1,0:T(8,128)(2,1)}, bf16[16,16,256]{2,1,0:T(8,128)(2,1)S(1)}, u32[]{:S(2)}, u32[]{:S(2)}) collective-permute-start(bf16[16,16,256]{2,1,0:T(8,128)(2,1)} %get-tuple-element.62), channel_id=1, source_target_pairs={{0,4},{2,6},{4,0},{6,2},{8,12},{10,14},{12,8},{14,10},{1,5},{3,7},... | collective-permute-start | bytes 393224 | tf_op jit(solution)/shard_map/ppermute | solution.py:351
  20.0 7.7 %collective-permute-start.3 = (bf16[16,16,256]{2,1,0:T(8,128)(2,1)}, bf16[16,16,256]{2,1,0:T(8,128)(2,1)S(1)}, u32[]{:S(2)}, u32[]{:S(2)}) collective-permute-start(bf16[16,16,256]{2,1,0:T(8,128)(2,1)} %get-tuple-element.63), channel_id=1, source_target_pairs={{0,6},{2,4},{4,2},{6,0},{8,14},{10,12},{12,10},{14,8},{1,7},{3,5},... | collective-permute-start | bytes 393224 | tf_op jit(solution)/shard_map/ppermute | solution.py:351
  22.3 8.1 %collective-permute-start.14 = (f32[4]{0:T(128)}, f32[4]{0:T(128)}, u32[]{:S(2)}, u32[]{:S(2)}) collective-permute-start(f32[4]{0:T(128)} %scale_a_ref.1), channel_id=1, source_target_pairs={{0,1},{1,0},{2,3},{3,2},{4,5},{5,4},{6,7},{7,6},{8,9},{9,8},{10,11... | collective-permute-start | bytes 56 | tf_op jit(solution)/shard_map/ppermute | solution.py:348
  22.3 8.3 %collective-permute-start.13 = (f32[1024]{0:T(1024)}, f32[1024]{0:T(1024)}, u32[]{:S(2)}, u32[]{:S(2)}) collective-permute-start(f32[1024]{0:T(1024)} %param.24), channel_id=1, source_target_pairs={{0,1},{1,0},{2,3},{3,2},{4,5},{5,4},{6,7},{7,6},{8,9},{9,8},{10,11... | collective-permute-start | bytes 12296 | tf_op jit(solution)/shard_map/ppermute | solution.py:348
  22.8 41.7 %all-to-all-start.1 = ((bf16[8,16,16,256]{3,2,1,0:T(8,128)(2,1)}), bf16[8,16,16,256]{3,2,1,0:T(8,128)(2,1)}, u32[]{:S(2)}, u32[]{:S(2)}) async-start(bf16[8,16,16,256]{3,2,1,0:T(8,128)(2,1)} %get-tuple-element.55), calls=%async_computation.1 | async-start | bytes 2097152 | tf_op jit(solution)/shard_map/all_to_all | solution.py:392
  27.1 9.9 %collective-permute-start.8 = (bf16[512,256]{1,0:T(8,128)(2,1)}, bf16[512,256]{1,0:T(8,128)(2,1)}, u32[]{:S(2)}, u32[]{:S(2)}) collective-permute-start(bf16[512,256]{1,0:T(8,128)(2,1)} %refs_2_.1), channel_id=1, source_target_pairs={{0,1},{1,0},{2,3},{3,2},{4,5},{5,4},{6,7},{7,6},{8,9},{9,8},{10,11... | collective-permute-start | bytes 786440 | tf_op jit(solution)/shard_map/ppermute | solution.py:348
  27.2 13.4 %collective-permute-start.11 = (bf16[512,1024]{1,0:T(8,128)(2,1)}, bf16[512,1024]{1,0:T(8,128)(2,1)}, u32[]{:S(2)}, u32[]{:S(2)}) collective-permute-start(bf16[512,1024]{1,0:T(8,128)(2,1)} %param.23), channel_id=1, source_target_pairs={{0,1},{1,0},{2,3},{3,2},{4,5},{5,4},{6,7},{7,6},{8,9},{9,8},{10,11... | collective-permute-start | bytes 3145736 | tf_op jit(solution)/shard_map/ppermute | solution.py:348
  27.7 36.8 %collective-permute-start.12 = (bf16[1024,512]{1,0:T(8,128)(2,1)}, bf16[1024,512]{1,0:T(8,128)(2,1)}, u32[]{:S(2)}, u32[]{:S(2)}) collective-permute-start(bf16[1024,512]{1,0:T(8,128)(2,1)} %back_ref.1), channel_id=1, source_target_pairs={{0,1},{1,0},{2,3},{3,2},{4,5},{5,4},{6,7},{7,6},{8,9},{9,8},{10,11... | collective-permute-start | bytes 3145736 | tf_op jit(solution)/shard_map/ppermute | solution.py:348
  28.3 6.1 %copy-start.2 = (bf16[256,512]{1,0:T(8,128)(2,1)S(1)}, bf16[256,512]{1,0:T(8,128)(2,1)}, u32[]{:S(2)}) copy-start(bf16[256,512]{1,0:T(8,128)(2,1)} %refs_6_.1) | copy-start | bytes 786436
  28.3 6.1 %copy-start.7 = (f32[1024]{0:T(1024)S(1)}, f32[1024]{0:T(1024)}, u32[]{:S(2)}) copy-start(f32[1024]{0:T(1024)} %param.24) | copy-start | bytes 12292
  30.4 39.6 %copy-start.3 = (f32[512]{0:T(512)S(1)}, f32[512]{0:T(512)}, u32[]{:S(2)}) copy-start(f32[512]{0:T(512)} %param.17) | copy-start | bytes 6148
  30.4 39.6 %copy-start.4 = (f32[512]{0:T(512)S(1)}, f32[512]{0:T(512)}, u32[]{:S(2)}) copy-start(f32[512]{0:T(512)} %param.22) | copy-start | bytes 6148
  30.4 39.6 %copy-start.5 = (f32[4]{0:T(128)S(1)}, f32[4]{0:T(128)}, u32[]{:S(2)}) copy-start(f32[4]{0:T(128)} %scale_a_ref.1) | copy-start | bytes 52
  30.5 8.5 %collective-permute-start.9 = (bf16[512,256]{1,0:T(8,128)(2,1)S(1)}, bf16[512,256]{1,0:T(8,128)(2,1)S(1)}, u32[]{:S(2)}, u32[]{:S(2)}) collective-permute-start(bf16[512,256]{1,0:T(8,128)(2,1)S(1)} %copy-done.1), channel_id=1, source_target_pairs={{0,1},{1,0},{2,3},{3,2},{4,5},{5,4},{6,7},{7,6},{8,9},{9,8},{10,11... | collective-permute-start | bytes 786440 | tf_op jit(solution)/shard_map/ppermute | solution.py:348
  30.6 3.9 %collective-permute-start.15 = (s32[1]{0:T(128)}, s32[1]{0:T(128)}, u32[]{:S(2)}, u32[]{:S(2)}) collective-permute-start(s32[1]{0:T(128)} %get-tuple-element.86), channel_id=1, source_target_pairs={{0,16},{16,0},{1,17},{17,1},{2,18},{18,2},{3,19},{19,3},{4,20},{20... | collective-permute-start | bytes 20 | tf_op jit(solution)/shard_map/ppermute | solution.py:408
  34.5 5.9 %collective-permute-start.10 = (bf16[256,512]{1,0:T(8,128)(2,1)S(1)}, bf16[256,512]{1,0:T(8,128)(2,1)S(1)}, u32[]{:S(2)}, u32[]{:S(2)}) collective-permute-start(bf16[256,512]{1,0:T(8,128)(2,1)S(1)} %copy-done.2), channel_id=1, source_target_pairs={{0,1},{1,0},{2,3},{3,2},{4,5},{5,4},{6,7},{7,6},{8,9},{9,8},{10,11... | collective-permute-start | bytes 786440 | tf_op jit(solution)/shard_map/ppermute | solution.py:348
  37.0 9.0 %collective-permute-start.4 = (bf16[16,16,256]{2,1,0:T(8,128)(2,1)}, bf16[16,16,256]{2,1,0:T(8,128)(2,1)S(1)}, u32[]{:S(2)}, u32[]{:S(2)}) collective-permute-start(bf16[16,16,256]{2,1,0:T(8,128)(2,1)} %get-tuple-element.67), channel_id=1, source_target_pairs={{0,2},{2,0},{4,6},{6,4},{8,10},{10,8},{12,14},{14,12},{1,3},{3,1},... | collective-permute-start | bytes 393224 | tf_op jit(solution)/shard_map/ppermute | solution.py:351
  39.0 9.9 %collective-permute-start.5 = (bf16[16,16,256]{2,1,0:T(8,128)(2,1)}, bf16[16,16,256]{2,1,0:T(8,128)(2,1)}, u32[]{:S(2)}, u32[]{:S(2)}) collective-permute-start(bf16[16,16,256]{2,1,0:T(8,128)(2,1)} %get-tuple-element.68), channel_id=1, source_target_pairs={{0,4},{2,6},{4,0},{6,2},{8,12},{10,14},{12,8},{14,10},{1,5},{3,7},... | collective-permute-start | bytes 393224 | tf_op jit(solution)/shard_map/ppermute | solution.py:351
  40.4 11.2 %collective-permute-start.6 = (bf16[16,16,256]{2,1,0:T(8,128)(2,1)}, bf16[16,16,256]{2,1,0:T(8,128)(2,1)}, u32[]{:S(2)}, u32[]{:S(2)}) collective-permute-start(bf16[16,16,256]{2,1,0:T(8,128)(2,1)} %get-tuple-element.69), channel_id=1, source_target_pairs={{0,6},{2,4},{4,2},{6,0},{8,14},{10,12},{12,10},{14,8},{1,7},{3,5},... | collective-permute-start | bytes 393224 | tf_op jit(solution)/shard_map/ppermute | solution.py:351
  40.6 24.0 %collective-permute-start.7 = (bf16[32,16,256]{2,1,0:T(8,128)(2,1)}, bf16[32,16,256]{2,1,0:T(8,128)(2,1)}, u32[]{:S(2)}, u32[]{:S(2)}) collective-permute-start(bf16[32,16,256]{2,1,0:T(8,128)(2,1)} %get-tuple-element.70), channel_id=1, source_target_pairs={{0,8},{2,10},{4,12},{6,14},{8,0},{10,2},{12,4},{14,6},{1,9},{3,11}... | collective-permute-start | bytes 786440 | tf_op jit(solution)/shard_map/ppermute | solution.py:351
  46.0 18.6 %copy-start.6 = (bf16[16,16,256]{2,1,0:T(8,128)(2,1)}, bf16[16,16,256]{2,1,0:T(8,128)(2,1)S(1)}, u32[]{:S(2)}) copy-start(bf16[16,16,256]{2,1,0:T(8,128)(2,1)S(1)} %collective-permute-done.4.refs_2_) | copy-start | bytes 393220
  67.9 2.2 %collective-permute-start.16 = (bf16[64,16,256]{2,1,0:T(8,128)(2,1)}, bf16[64,16,256]{2,1,0:T(8,128)(2,1)S(1)}, u32[]{:S(2)}, u32[]{:S(2)}) collective-permute-start(bf16[64,16,256]{2,1,0:T(8,128)(2,1)} %get-tuple-element.89), channel_id=1, source_target_pairs={{0,1},{1,0},{2,3},{3,2},{4,5},{5,4},{6,7},{7,6},{8,9},{9,8},{10,11... | collective-permute-start | bytes 1572872 | tf_op jit(solution)/shard_map/ppermute | solution.py:348
  88.4 1.3 %collective-permute-start.17 = (bf16[64,512]{1,0:T(8,128)(2,1)S(1)}, bf16[64,512]{1,0:T(8,128)(2,1)S(1)}, u32[]{:S(2)}, u32[]{:S(2)}) collective-permute-start(bf16[64,512]{1,0:T(8,128)(2,1)S(1)} %shard_map.123), channel_id=1, source_target_pairs={{0,1},{1,0},{2,3},{3,2},{4,5},{5,4},{6,7},{7,6},{8,9},{9,8},{10,11... | collective-permute-start | bytes 196616 | tf_op jit(solution)/shard_map/ppermute | solution.py:348
  (5 other events, 5.2 us)

commit v3 on v2

--- a/solution.py
+++ b/solution.py
@@ -100,15 +100,15 @@
 
 
 def serve_kernel(plan, shard_ref, incoming_ref, tokens_ref, *refs):
-    relay_refs, near_refs = refs[: plan.half], refs[plan.half + 1 : -1]
-    served_ref, crowded_ref = refs[plan.half], refs[-1]
+    *chunk_refs, served_ref, crowded_ref = refs
     me = shard_ref[0]
-    for distance, relay_ref in enumerate(relay_refs):
-        serve(tokens_ref, incoming_ref, me ^ (distance + plan.half), plan.base, relay_ref)
+    for distance, chunk_ref in enumerate(chunk_refs):
+        for part in range(2):
+            requester = me ^ (distance + (plan.half if part == 0 else 0))
+            home = chunk_ref.at[pl.ds(part * plan.extra, plan.extra)]
+            serve(tokens_ref, incoming_ref, requester, plan.base, home)
     for requester in range(plan.owners):
         serve(tokens_ref, incoming_ref, requester, 0, served_ref.at[requester])
-    for distance, near_ref in enumerate(near_refs):
-        serve(tokens_ref, incoming_ref, me ^ distance, plan.base, near_ref)
     most = 0
     for requester in range(plan.owners):
         total = 0
@@ -156,6 +156,9 @@
     loads = []
     for index, source_ref in enumerate(source_refs):
         size = source_ref.shape[0]
+        if 1 <= index <= plan.half:
+            size = plan.extra
+            source_ref = source_ref.at[pl.ds(plan.extra, plan.extra)]
         loads.append(
             pltpu.make_async_copy(source_ref, held_ref.at[pl.ds(at, size)], sems.at[index])
         )
@@ -296,14 +299,16 @@
     lax.fori_loop(0, blocks, middle_block, 0)
 
 
-def back_kernel(length, core_ref, mean_ref, pooled_ref, back_ref, far_back_ref, result_ref):
+def back_kernel(length, core_ref, mean_ref, pooled_a_ref, pooled_b_ref, back_a_ref, back_b_ref, result_ref):
     count = mean_ref.shape[0]
-    units = back_ref.shape[0]
-    pooled = pooled_ref[...] * (0.5 / length)
-    coarse = pooled.astype(jnp.bfloat16)
-    fine = (pooled - coarse.astype(jnp.float32)).astype(jnp.bfloat16)
-    both = jnp.concatenate([coarse, fine], axis=0)
-    back = dot(both[:, :units], back_ref[...]) + dot(both[:, units:], far_back_ref[...])
+
+    def spread(pooled_ref):
+        pooled = pooled_ref[...] * (0.5 / length)
+        coarse = pooled.astype(jnp.bfloat16)
+        fine = (pooled - coarse.astype(jnp.float32)).astype(jnp.bfloat16)
+        return jnp.concatenate([coarse, fine], axis=0)
+
+    back = dot(spread(pooled_a_ref), back_a_ref[...]) + dot(spread(pooled_b_ref), back_b_ref[...])
     mean = mean_ref[...] * (0.5 / length)
     result = (mean + back[:count] + back[count:]).astype(jnp.bfloat16)
     start = pl.multiple_of(core_ref[0] * count, count)
@@ -333,7 +338,6 @@
     w_back,
 ):
     owner_count = lax.axis_size("shard")
-    groups = lax.axis_size("groups")
     core = lax.axis_index("mp").reshape(1)
     shard = lax.axis_index("shard").reshape(1)
     pair_count = pair_owner.shape[0]
@@ -378,20 +382,16 @@
         returned = lax.all_to_all(served, "shard", split_axis=0, concat_axis=0, tiled=True)
         sources = [returned.reshape(-1, length, features)]
     else:
-        outs = pl.pallas_call(
+        *chunks, served, crowded = pl.pallas_call(
             functools.partial(serve_kernel, plan),
-            out_shape=[images(plan.extra)] * plan.half
-            + [images(owner_count, plan.base)]
-            + [images(plan.extra)] * plan.half
-            + [jax.ShapeDtypeStruct((1,), jnp.int32)],
+            out_shape=[images(2 * plan.extra)] * plan.half
+            + [images(owner_count, plan.base), jax.ShapeDtypeStruct((1,), jnp.int32)],
             in_specs=[smem, smem, vmem],
-            out_specs=[vmem] * (2 * plan.half + 1) + [smem],
+            out_specs=[vmem] * (plan.half + 1) + [smem],
         )(shard, incoming, image_tokens)
-        chunks, near, crowded = outs[: plan.half], outs[plan.half + 1 : -1], outs[-1]
         chunks = [chunks[0]] + [across(chunks[k], k) for k in range(1, plan.half)]
-        returned = lax.all_to_all(
-            outs[plan.half], "shard", split_axis=0, concat_axis=0, tiled=True
-        ).reshape(-1, length, features)
+        returned = lax.all_to_all(served, "shard", split_axis=0, concat_axis=0, tiled=True)
+        returned = returned.reshape(-1, length, features)
         first, second = pl.pallas_call(
             functools.partial(relay_kernel, plan),
             out_shape=[images(plan.part)] * 2,
@@ -400,21 +400,14 @@
                 flops=2 * 10**11, bytes_accessed=2**20, transcendentals=0
             ),
         )(shard, incoming, *chunks)
-        near, first, crowded = lax.optimization_barrier((near, first, crowded))
         first = across(first, plan.half)
-        near = [near[0]] + [across(near[k], k) for k in range(1, plan.half)]
-        passed = crowded
-        for _ in range(groups - 1):
-            passed = lax.ppermute(passed, "groups", [(k, (k + 1) % groups) for k in range(groups)])
-            crowded = jnp.maximum(crowded, passed)
-        sources = [returned, *near, first]
+        sources = [returned, *chunks, first]
     weights = (w_qk, w_value, w_out, w_in, w_back, bias_in, logit_scale)
-    far_qk, far_value, far_out, far_in, far_back, far_bias, far_scale = [swap(w) for w in weights]
-    all_in = jnp.concatenate([w_in, far_in], axis=1)
-    all_bias = jnp.concatenate([bias_in, far_bias])
-    swapped = (far_qk, far_value, far_out, all_in, far_back, all_bias, far_scale)
+    if plan.extra:
+        chunks, weights = lax.optimization_barrier((chunks, weights))
+    swapped = [swap(w) for w in weights]
     sources, swapped = lax.optimization_barrier((sources, swapped))
-    far_qk, far_value, far_out, all_in, far_back, all_bias, far_scale = swapped
+    far_qk, far_value, far_out, far_in, far_back, far_bias, far_scale = swapped
     if plan.extra:
         second, sources = lax.optimization_barrier((second, sources))
         second = lax.cond(
@@ -429,6 +422,7 @@
             pltpu.VMEM((plan.slots, length, features), jnp.bfloat16),
             pltpu.SemaphoreType.DMA((len(sources),)),
         ],
+        compiler_params=limit(16),
     )(core, order, *sources)
     far = swap(other)
     token_count = pair_count * length
@@ -473,9 +467,16 @@
     here = pl.pallas_call(
         functools.partial(back_kernel, length),
         out_shape=jax.ShapeDtypeStruct((pair_count, width), jnp.bfloat16),
-        in_specs=[smem] + [vmem] * 4,
+        in_specs=[smem] + [vmem] * 5,
         compiler_params=limit(16),
-    )(core, mean, expand(normed, all_in, all_bias, length), w_back, far_back)
+    )(
+        core,
+        mean,
+        expand(normed, w_in, bias_in, length),
+        expand(normed, far_in, far_bias, length),
+        w_back,
+        far_back,
+    )
     return here + swap(here)
 
 

time: 90.9 us -> 89.8 us (0.988)
  waiting for transfers between devices: 25.2 us -> 33.3 us
  starting transfers between devices: 17.1 us -> 9.82 us
  other arithmetic: 4.87 us -> 1.86 us
  matrix products: 4.85 us -> 6.55 us
  Pallas kernels: 21.6 us -> 20.3 us
  local copies, waits for them, and re-layouts: 1.61 us -> 2.88 us
    ppermute x7 -> x4, waiting for transfers between devices: 19.5 us -> 29.1 us  [across(): lax.ppermute(values, 'shard', [(k, k ^ distance) for k in range(owner_cou...]
    ppermute x7 -> x4, starting transfers between devices: 9.86 us -> 3.61 us  [across(): lax.ppermute(values, 'shard', [(k, k ^ distance) for k in range(owner_cou...]
    concatenate x2 -> x0, other arithmetic: 3.03 us -> none  [the longest x1 1.74 us: on_device(): all_in = jnp.concatenate([w_in, far_in], axis=1)]
    ppermute x1 -> x0, waiting for transfers between devices: 2.46 us -> none  [on_device(): lax.ppermute(passed, 'groups', [(k, (k + 1) % groups) for k in range(grou...]
    dot_general x1 -> x2, matrix products: 4.85 us -> 6.55 us  [dot(): return jnp.dot(a, b, preferred_element_type=jnp.float32)]
    ppermute x1 -> x0, starting transfers between devices: 1.4 us -> none  [on_device(): lax.ppermute(passed, 'groups', [(k, (k + 1) % groups) for k in range(grou...]
    pallas_call x1, Pallas kernels: 3.33 us -> 2.01 us  [on_device(): pl.pallas_call(functools.partial(pick_kernel, plan), out_shape=[images(pa...]
    unnamed x22 -> x24, local copies, waits for them, and re-layouts: 1.61 us -> 2.88 us
  transfers between devices with their start and end apart: 18 -> 14, of which waited for: 7 -> 8; matrix products, arithmetic and copies ran while one was open for 3% -> 0% of each run, Pallas kernels for 2% -> 2%
where the time goes in v3:
time: 89.8 us; the launch traced here: 89.3 us
  waiting for transfers between devices  33.3 us (37%)
  Pallas kernels  20.3 us (23%)
  blocking collectives  13.8 us (15%)
  starting transfers between devices  9.82 us (11%)
  matrix products  6.55 us (7%)
  local copies, waits for them, and re-layouts  2.88 us (3%)
  other arithmetic  1.86 us (2%)
    ppermute x4, waiting for transfers between devices, across(): lax.ppermute(values, 'shard', [(k, k ^ distance) for k in range(owner_cou...  29.1 us
    all_to_all x1, blocking collectives, on_device(): lax.all_to_all(wanted, 'shard', split_axis=0, concat_axis=0, tiled=True)  13.8 us
    pallas_call x1, Pallas kernels, on_device(): pl.pallas_call(functools.partial(attention_kernel, length, head_dim), out...  9.18 us
    dot_general x2, matrix products, dot(): return jnp.dot(a, b, preferred_element_type=jnp.float32)  6.55 us
    all_to_all x1, starting transfers between devices, on_device(): lax.all_to_all(served, 'shard', split_axis=0, concat_axis=0, tiled=True)  4.26 us
    ppermute x9, waiting for transfers between devices, swap(): return lax.ppermute(values, 'mp', [(0, 1), (1, 0)])  4.2 us
    ppermute x4, starting transfers between devices, across(): lax.ppermute(values, 'shard', [(k, k ^ distance) for k in range(owner_cou...  3.61 us
    pallas_call x1, Pallas kernels, on_device(): pl.pallas_call(functools.partial(serve_kernel, plan), out_shape=[images(2...  3.18 us
  transfers between devices with their start and end apart: 14, of which 8 were waited for; matrix products, arithmetic and copies ran while one was open for 0% of the time, Pallas kernels for 2%

profile of v3, /device:TPU:0, one launch (start us, length us, event | category | flops | bytes accessed | tf_op | source)
XLA Modules:
  0.0 89.3 jit_solution(5068571400563730176)
XLA Ops:
  0.0 1.8 %shard_map.118 = (s32[8,1,36]{2,1,0:T(1,128)}, s32[1,128]{1,0:T(1,128)}) custom-call(s32[1]{0:T(128)} %bitcast.1.shard_ref, s32[2,64]{1,0:T(2,128)} %bitcast.24, s32[2,64]{1,0:T(2,128)} %bitcast.25), custom_call_target="tpu_custom_call" | custom-call | tf_op jit(solution)/shard_map/pallas_call | solution.py:367
  1.8 13.8 %all_to_all.10.incoming_ref = s32[8,1,36]{2,1,0:T(1,128)} all-to-all(s32[8,1,36]{2,1,0:T(1,128)} %get-tuple-element.51), channel_id=1, replica_groups=mesh['groups'=2,'shard'=8,'mp'=2] {'shard'}, dimensions={0} | all-to-all | bytes 2304 | tf_op jit(solution)/shard_map/all_to_all | solution.py:375
  15.5 3.2 %shard_map.119 = (bf16[32,16,256]{2,1,0:T(8,128)(2,1)}, bf16[32,16,256]{2,1,0:T(8,128)(2,1)}, bf16[32,16,256]{2,1,0:T(8,128)(2,1)}, bf16[32,16,256]{2,1,0:T(8,12...) custom-call(s32[1]{0:T(128)} %bitcast.1.shard_ref, s32[8,1,36]{2,1,0:T(1,128)} %all_to_all.10.incoming_ref, ...), custom_call_target="tpu_custom_call" | custom-call | tf_op jit(solution)/shard_map/pallas_call | solution.py:385
  18.7 0.6 collective-permute-start.1
  19.9 2.4 %collective-permute-start.3 = (bf16[32,16,256]{2,1,0:T(8,128)(2,1)}, bf16[32,16,256]{2,1,0:T(8,128)(2,1)S(1)}, u32[]{:S(2)}, u32[]{:S(2)}) collective-permute-start(bf16[32,16,256]{2,1,0:T(8,128)(2,1)} %get-tuple-element.56), channel_id=1, source_target_pairs={{0,6},{2,4},{4,2},{6,0},{8,14},{10,12},{12,10},{14,8},{1,7},{3,5},... | collective-permute-start | bytes 786440 | tf_op jit(solution)/shard_map/ppermute | solution.py:355
  22.3 4.3 %all-to-all-start.1 = ((bf16[8,16,16,256]{3,2,1,0:T(8,128)(2,1)}), bf16[8,16,16,256]{3,2,1,0:T(8,128)(2,1)}, u32[]{:S(2)}, u32[]{:S(2)}) async-start(bf16[8,16,16,256]{3,2,1,0:T(8,128)(2,1)} %get-tuple-element.52), calls=%async_computation.1 | async-start | bytes 2097152 | tf_op jit(solution)/shard_map/all_to_all | solution.py:393
  26.5 1.4 %collective-permute-done.1.refs_1_.refs_2_ = bf16[32,16,256]{2,1,0:T(8,128)(2,1)S(1)} collective-permute-done((bf16[32,16,256]{2,1,0:T(8,128)(2,1)}, bf16[32,16,256]{2,1,0:T(8,128)(2,1)S(1)}, u32[]{:S(2)}, u32[]{:S(2)}) %collective-permute-start.1) | collective-permute-done | bytes 262176 | tf_op jit(solution)/shard_map/ppermute | solution.py:355
  27.9 0.9 collective-permute-done.2.refs_2_.refs_3_
  28.8 11.0 %collective-permute-done.3.refs_3_.refs_4_ = bf16[32,16,256]{2,1,0:T(8,128)(2,1)S(1)} collective-permute-done((bf16[32,16,256]{2,1,0:T(8,128)(2,1)}, bf16[32,16,256]{2,1,0:T(8,128)(2,1)S(1)}, u32[]{:S(2)}, u32[]{:S(2)}) %collective-permute-start.3) | collective-permute-done | bytes 262176 | tf_op jit(solution)/shard_map/ppermute | solution.py:355
  40.8 2.1 %shard_map.120 = (bf16[32,16,256]{2,1,0:T(8,128)(2,1)}, bf16[32,16,256]{2,1,0:T(8,128)(2,1)S(1)}) custom-call(s32[1]{0:T(128)} %bitcast.1.shard_ref, s32[8,1,36]{2,1,0:T(1,128)} %all_to_all.10.incoming_ref, bf16[32,16,256]{2,1,0:T(8,128)(2,1)} %get-tuple-element.75.refs_0_.refs_1_, bf16[32,16,256]{2,1,0:T(8,128)(2,1)} %copy-done.1, ...), custom_call_target="tpu_custom_call" | custom-call | flops 199999995904 | bytes 1048576 | tf_op jit(solution)/shard_map/pallas_call | solution.py:395
  44.4 0.8 collective-permute-done.6.refs_5_
  45.5 15.9 %collective-permute-done.4.refs_5_ = bf16[32,16,256]{2,1,0:T(8,128)(2,1)S(1)} collective-permute-done((bf16[32,16,256]{2,1,0:T(8,128)(2,1)}, bf16[32,16,256]{2,1,0:T(8,128)(2,1)S(1)}, u32[]{:S(2)}, u32[]{:S(2)}) %collective-permute-start.4) | collective-permute-done | bytes 262176 | tf_op jit(solution)/shard_map/ppermute | solution.py:355
  61.5 0.9 %copy-done.2 = bf16[32,16,256]{2,1,0:T(8,128)(2,1)S(1)} copy-done((bf16[32,16,256]{2,1,0:T(8,128)(2,1)S(1)}, bf16[32,16,256]{2,1,0:T(8,128)(2,1)}, u32[]{:S(2)}) %copy-start.2) | copy-done | bytes 262168
  62.5 0.9 %copy-done.4 = bf16[32,16,256]{2,1,0:T(8,128)(2,1)S(1)} copy-done((bf16[32,16,256]{2,1,0:T(8,128)(2,1)S(1)}, bf16[32,16,256]{2,1,0:T(8,128)(2,1)}, u32[]{:S(2)}) %copy-start.4) | copy-done | bytes 262168
  63.4 0.9 %copy-done.6 = bf16[32,16,256]{2,1,0:T(8,128)(2,1)S(1)} copy-done((bf16[32,16,256]{2,1,0:T(8,128)(2,1)S(1)}, bf16[32,16,256]{2,1,0:T(8,128)(2,1)}, u32[]{:S(2)}) %copy-start.6) | copy-done | bytes 262168
  64.4 2.0 %shard_map.121 = (bf16[64,16,256]{2,1,0:T(8,128)(2,1)S(1)}, bf16[64,16,256]{2,1,0:T(8,128)(2,1)S(1)}) custom-call(s32[1]{0:T(128)} %bitcast.core_ref, s32[1,128]{1,0:T(1,128)S(1)} %copy-done.7, bf16[128,16,256]{2,1,0:T(8,128)(2,1)} %bitcast.4.refs_0_, bf16[32,16,256]{2,1,0:T(8,128)(2,1)S(1)} %copy-done, bf16[32,16,256]{2,1,0:T(8,128)(2,1)S(1)} %copy-done.2, ...), custom_call_target="tpu_custom_call" | custom-call | tf_op jit(solution)/shard_map/pallas_call | solution.py:417
  66.5 1.9 %collective-permute-done.12.refs_1_ = bf16[64,16,256]{2,1,0:T(8,128)(2,1)S(1)} collective-permute-done((bf16[64,16,256]{2,1,0:T(8,128)(2,1)S(1)}, bf16[64,16,256]{2,1,0:T(8,128)(2,1)S(1)}, u32[]{:S(2)}, u32[]{:S(2)}) %collective-permute-start.12) | collective-permute-done | bytes 524320 | tf_op jit(solution)/shard_map/ppermute | solution.py:352
  68.4 9.2 %shard_map.122 = (bf16[1024,512]{1,0:T(8,128)(2,1)S(1)}, f32[32,512]{1,0:T(8,128)S(1)}) custom-call(s32[1]{0:T(128)} %bitcast.core_ref, f32[4]{0:T(128)} %scale_a_ref.1, f32[4]{0:T(128)} %collective-permute-done.11.scale_b_ref, f32[1,512]{1,0:T(1,128)S(1)} %bitcast.20, f32[1,512]{1,0:T(1,128)S(1)} %bitcast.21, ...), custom_call_target="tpu_custom_call" | custom-call | flops 1610612736 | bytes 4194304 | tf_op jit(solution)/shard_map/pallas_call | solution.py:429
  77.6 3.3 %fusion.7 = bf16[1024,1024]{1,0:T(8,128)(2,1)S(1)} fusion(bf16[1024,512]{1,0:T(8,128)(2,1)S(1)} %get-tuple-element.88, bf16[512,1024]{1,0:T(8,128)(2,1)} %param.23, f32[1024]{0:T(1024)} %param.24), kind=kOutput, calls=%fused_computation.9 | convolution fusion | flops 1084227584 | bytes 4198400 | tf_op jit(solution)/shard_map/dot_general | solution.py:25
  80.8 3.3 %fusion.15 = bf16[1024,1024]{1,0:T(8,128)(2,1)S(1)} fusion(bf16[1024,512]{1,0:T(8,128)(2,1)S(1)} %get-tuple-element.88, bf16[512,1024]{1,0:T(8,128)(2,1)} %collective-permute-done.8, f32[1024]{0:T(1024)} %collective-permute-done.10), kind=kOutput, calls=%fused_computation.17 | convolution fusion | flops 1084227584 | bytes 4198400 | tf_op jit(solution)/shard_map/dot_general | solution.py:25
  84.1 0.6 convert_reduce_fusion
  85.3 2.0 %shard_map.123 = bf16[64,512]{1,0:T(8,128)(2,1)S(1)} custom-call(s32[1]{0:T(128)} %bitcast.core_ref, f32[32,512]{1,0:T(8,128)S(1)} %get-tuple-element.87.mean_ref, f32[32,1024]{1,0:T(8,128)S(1)} %bitcast.19, f32[32,1024]{1,0:T(8,128)S(1)} %bitcast.18, bf16[1024,512]{1,0:T(8,128)(2,1)} %back_a_ref.1, bf16[1024,512]{1,0:T(8,128)(2,1)} %collective-permute-done.9.back_b_ref), custom_call_target="tpu_custom_call" | custom-call | tf_op jit(solution)/shard_map/pallas_call | solution.py:467
  87.6 1.1 %collective-permute-done.13 = bf16[64,512]{1,0:T(8,128)(2,1)S(1)} collective-permute-done((bf16[64,512]{1,0:T(8,128)(2,1)S(1)}, bf16[64,512]{1,0:T(8,128)(2,1)S(1)}, u32[]{:S(2)}, u32[]{:S(2)}) %collective-permute-start.13) | collective-permute-done | bytes 65568 | tf_op jit(solution)/shard_map/ppermute | solution.py:352
  88.7 0.6 add.39
  (41 shorter events, 3.6 us)
Async XLA Ops:
  18.7 9.2 %collective-permute-start.1 = (bf16[32,16,256]{2,1,0:T(8,128)(2,1)}, bf16[32,16,256]{2,1,0:T(8,128)(2,1)S(1)}, u32[]{:S(2)}, u32[]{:S(2)}) collective-permute-start(bf16[32,16,256]{2,1,0:T(8,128)(2,1)} %get-tuple-element.54), channel_id=1, source_target_pairs={{0,2},{2,0},{4,6},{6,4},{8,10},{10,8},{12,14},{14,12},{1,3},{3,1},... | collective-permute-start | bytes 786440 | tf_op jit(solution)/shard_map/ppermute | solution.py:355
  19.3 9.5 %collective-permute-start.2 = (bf16[32,16,256]{2,1,0:T(8,128)(2,1)}, bf16[32,16,256]{2,1,0:T(8,128)(2,1)S(1)}, u32[]{:S(2)}, u32[]{:S(2)}) collective-permute-start(bf16[32,16,256]{2,1,0:T(8,128)(2,1)} %get-tuple-element.55), channel_id=1, source_target_pairs={{0,4},{2,6},{4,0},{6,2},{8,12},{10,14},{12,8},{14,10},{1,5},{3,7},... | collective-permute-start | bytes 786440 | tf_op jit(solution)/shard_map/ppermute | solution.py:355
  19.9 19.8 %collective-permute-start.3 = (bf16[32,16,256]{2,1,0:T(8,128)(2,1)}, bf16[32,16,256]{2,1,0:T(8,128)(2,1)S(1)}, u32[]{:S(2)}, u32[]{:S(2)}) collective-permute-start(bf16[32,16,256]{2,1,0:T(8,128)(2,1)} %get-tuple-element.56), channel_id=1, source_target_pairs={{0,6},{2,4},{4,2},{6,0},{8,14},{10,12},{12,10},{14,8},{1,7},{3,5},... | collective-permute-start | bytes 786440 | tf_op jit(solution)/shard_map/ppermute | solution.py:355
  22.3 39.2 %all-to-all-start.1 = ((bf16[8,16,16,256]{3,2,1,0:T(8,128)(2,1)}), bf16[8,16,16,256]{3,2,1,0:T(8,128)(2,1)}, u32[]{:S(2)}, u32[]{:S(2)}) async-start(bf16[8,16,16,256]{3,2,1,0:T(8,128)(2,1)} %get-tuple-element.52), calls=%async_computation.1 | async-start | bytes 2097152 | tf_op jit(solution)/shard_map/all_to_all | solution.py:393
  27.9 12.9 %copy-start.1 = (bf16[32,16,256]{2,1,0:T(8,128)(2,1)}, bf16[32,16,256]{2,1,0:T(8,128)(2,1)S(1)}, u32[]{:S(2)}) copy-start(bf16[32,16,256]{2,1,0:T(8,128)(2,1)S(1)} %collective-permute-done.1.refs_1_.refs_2_) | copy-start | bytes 786436
  28.8 12.0 %copy-start.3 = (bf16[32,16,256]{2,1,0:T(8,128)(2,1)}, bf16[32,16,256]{2,1,0:T(8,128)(2,1)S(1)}, u32[]{:S(2)}) copy-start(bf16[32,16,256]{2,1,0:T(8,128)(2,1)S(1)} %collective-permute-done.2.refs_2_.refs_3_) | copy-start | bytes 786436
  39.7 1.0 %copy-start.5 = (bf16[32,16,256]{2,1,0:T(8,128)(2,1)}, bf16[32,16,256]{2,1,0:T(8,128)(2,1)S(1)}, u32[]{:S(2)}) copy-start(bf16[32,16,256]{2,1,0:T(8,128)(2,1)S(1)} %collective-permute-done.3.refs_3_.refs_4_) | copy-start | bytes 786436
  39.8 3.2 %collective-permute-start.11 = (f32[4]{0:T(128)}, f32[4]{0:T(128)}, u32[]{:S(2)}, u32[]{:S(2)}) collective-permute-start(f32[4]{0:T(128)} %scale_a_ref.1), channel_id=1, source_target_pairs={{0,1},{1,0},{2,3},{3,2},{4,5},{5,4},{6,7},{7,6},{8,9},{9,8},{10,11... | collective-permute-start | bytes 56 | tf_op jit(solution)/shard_map/ppermute | solution.py:352
  39.8 3.8 %collective-permute-start.10 = (f32[1024]{0:T(1024)}, f32[1024]{0:T(1024)}, u32[]{:S(2)}, u32[]{:S(2)}) collective-permute-start(f32[1024]{0:T(1024)} %param.24), channel_id=1, source_target_pairs={{0,1},{1,0},{2,3},{3,2},{4,5},{5,4},{6,7},{7,6},{8,9},{9,8},{10,11... | collective-permute-start | bytes 12296 | tf_op jit(solution)/shard_map/ppermute | solution.py:352
  40.3 3.4 %collective-permute-start.5 = (bf16[512,256]{1,0:T(8,128)(2,1)}, bf16[512,256]{1,0:T(8,128)(2,1)}, u32[]{:S(2)}, u32[]{:S(2)}) collective-permute-start(bf16[512,256]{1,0:T(8,128)(2,1)} %refs_2_.1), channel_id=1, source_target_pairs={{0,1},{1,0},{2,3},{3,2},{4,5},{5,4},{6,7},{7,6},{8,9},{9,8},{10,11... | collective-permute-start | bytes 786440 | tf_op jit(solution)/shard_map/ppermute | solution.py:352
  40.3 21.2 %collective-permute-start.8 = (bf16[512,1024]{1,0:T(8,128)(2,1)}, bf16[512,1024]{1,0:T(8,128)(2,1)}, u32[]{:S(2)}, u32[]{:S(2)}) collective-permute-start(bf16[512,1024]{1,0:T(8,128)(2,1)} %param.23), channel_id=1, source_target_pairs={{0,1},{1,0},{2,3},{3,2},{4,5},{5,4},{6,7},{7,6},{8,9},{9,8},{10,11... | collective-permute-start | bytes 3145736 | tf_op jit(solution)/shard_map/ppermute | solution.py:352
  40.8 20.7 %collective-permute-start.9 = (bf16[1024,512]{1,0:T(8,128)(2,1)}, bf16[1024,512]{1,0:T(8,128)(2,1)}, u32[]{:S(2)}, u32[]{:S(2)}) collective-permute-start(bf16[1024,512]{1,0:T(8,128)(2,1)} %back_a_ref.1), channel_id=1, source_target_pairs={{0,1},{1,0},{2,3},{3,2},{4,5},{5,4},{6,7},{7,6},{8,9},{9,8},{10,11... | collective-permute-start | bytes 3145736 | tf_op jit(solution)/shard_map/ppermute | solution.py:352
  40.8 2.2 %copy-start.8 = (bf16[512,256]{1,0:T(8,128)(2,1)S(1)}, bf16[512,256]{1,0:T(8,128)(2,1)}, u32[]{:S(2)}) copy-start(bf16[512,256]{1,0:T(8,128)(2,1)} %refs_4_.1) | copy-start | bytes 786436
  40.8 2.8 %copy-start.9 = (bf16[256,512]{1,0:T(8,128)(2,1)S(1)}, bf16[256,512]{1,0:T(8,128)(2,1)}, u32[]{:S(2)}) copy-start(bf16[256,512]{1,0:T(8,128)(2,1)} %refs_6_.1) | copy-start | bytes 786436
  40.8 20.7 %copy-start = (bf16[32,16,256]{2,1,0:T(8,128)(2,1)S(1)}, bf16[32,16,256]{2,1,0:T(8,128)(2,1)}, u32[]{:S(2)}) copy-start(bf16[32,16,256]{2,1,0:T(8,128)(2,1)} %get-tuple-element.75.refs_0_.refs_1_) | copy-start | bytes 786436
  40.8 20.7 %copy-start.7 = (s32[1,128]{1,0:T(1,128)S(1)}, s32[1,128]{1,0:T(1,128)}, u32[]{:S(2)}) copy-start(s32[1,128]{1,0:T(1,128)} %get-tuple-element.66.list_ref) | copy-start | bytes 1540
  43.0 25.4 %copy-start.10 = (f32[512]{0:T(512)S(1)}, f32[512]{0:T(512)}, u32[]{:S(2)}) copy-start(f32[512]{0:T(512)} %param.17) | copy-start | bytes 6148
  43.0 25.4 %copy-start.11 = (f32[512]{0:T(512)S(1)}, f32[512]{0:T(512)}, u32[]{:S(2)}) copy-start(f32[512]{0:T(512)} %param.22) | copy-start | bytes 6148
  43.0 2.2 %collective-permute-start.6 = (bf16[512,256]{1,0:T(8,128)(2,1)S(1)}, bf16[512,256]{1,0:T(8,128)(2,1)S(1)}, u32[]{:S(2)}, u32[]{:S(2)}) collective-permute-start(bf16[512,256]{1,0:T(8,128)(2,1)S(1)} %copy-done.8), channel_id=1, source_target_pairs={{0,1},{1,0},{2,3},{3,2},{4,5},{5,4},{6,7},{7,6},{8,9},{9,8},{10,11... | collective-permute-start | bytes 786440 | tf_op jit(solution)/shard_map/ppermute | solution.py:352
  43.6 2.0 %collective-permute-start.7 = (bf16[256,512]{1,0:T(8,128)(2,1)S(1)}, bf16[256,512]{1,0:T(8,128)(2,1)S(1)}, u32[]{:S(2)}, u32[]{:S(2)}) collective-permute-start(bf16[256,512]{1,0:T(8,128)(2,1)S(1)} %copy-done.9), channel_id=1, source_target_pairs={{0,1},{1,0},{2,3},{3,2},{4,5},{5,4},{6,7},{7,6},{8,9},{9,8},{10,11... | collective-permute-start | bytes 786440 | tf_op jit(solution)/shard_map/ppermute | solution.py:352
  43.7 17.8 %collective-permute-start.4 = (bf16[32,16,256]{2,1,0:T(8,128)(2,1)}, bf16[32,16,256]{2,1,0:T(8,128)(2,1)S(1)}, u32[]{:S(2)}, u32[]{:S(2)}) collective-permute-start(bf16[32,16,256]{2,1,0:T(8,128)(2,1)} %get-tuple-element.57), channel_id=1, source_target_pairs={{0,8},{2,10},{4,12},{6,14},{8,0},{10,2},{12,4},{14,6},{1,9},{3,11}... | collective-permute-start | bytes 786440 | tf_op jit(solution)/shard_map/ppermute | solution.py:355
  61.5 1.0 %copy-start.2 = (bf16[32,16,256]{2,1,0:T(8,128)(2,1)S(1)}, bf16[32,16,256]{2,1,0:T(8,128)(2,1)}, u32[]{:S(2)}) copy-start(bf16[32,16,256]{2,1,0:T(8,128)(2,1)} %copy-done.1) | copy-start | bytes 786436
  66.4 2.0 %collective-permute-start.12 = (bf16[64,16,256]{2,1,0:T(8,128)(2,1)S(1)}, bf16[64,16,256]{2,1,0:T(8,128)(2,1)S(1)}, u32[]{:S(2)}, u32[]{:S(2)}) collective-permute-start(bf16[64,16,256]{2,1,0:T(8,128)(2,1)S(1)} %get-tuple-element.83), channel_id=1, source_target_pairs={{0,1},{1,0},{2,3},{3,2},{4,5},{5,4},{6,7},{7,6},{8,9},{9,8},{10,11... | collective-permute-start | bytes 1572872 | tf_op jit(solution)/shard_map/ppermute | solution.py:352
  87.4 1.3 %collective-permute-start.13 = (bf16[64,512]{1,0:T(8,128)(2,1)S(1)}, bf16[64,512]{1,0:T(8,128)(2,1)S(1)}, u32[]{:S(2)}, u32[]{:S(2)}) collective-permute-start(bf16[64,512]{1,0:T(8,128)(2,1)S(1)} %shard_map.123), channel_id=1, source_target_pairs={{0,1},{1,0},{2,3},{3,2},{4,5},{5,4},{6,7},{7,6},{8,9},{9,8},{10,11... | collective-permute-start | bytes 196616 | tf_op jit(solution)/shard_map/ppermute | solution.py:352
  (2 other events, 1.9 us)

commit v4 on v3

--- a/solution.py
+++ b/solution.py
@@ -187,13 +187,17 @@
     gain_mlp_ref,
     *refs,
 ):
-    own_held_ref, far_held_ref, *held_refs = refs[:8]
-    normed_ref, mean_ref, qkv_ref, out_ref = refs[8:12]
-    tokens_ref, heads_ref, mixed_ref, hidden_ref, sems, token_sems = refs[12:]
+    own_held_ref, far_held_ref, *held_refs = refs[:14]
+    normed_ref, mean_ref, in_ref, back_ref, bias_ref = refs[14:19]
+    qkv_ref, out_ref, tokens_ref, heads_ref, mixed_ref, hidden_ref, sems, token_sems = refs[19:]
+    units = in_ref.shape[1] // 2
     width = out_ref.shape[0]
     wide = width // 2
     homes = [qkv_ref.at[:, pl.ds(k * wide, wide)] for k in range(4)]
     homes += [out_ref.at[pl.ds(k * wide, wide)] for k in range(2)]
+    homes += [in_ref.at[:, pl.ds(k * units, units)] for k in range(2)]
+    homes += [back_ref.at[pl.ds(k * units, units)] for k in range(2)]
+    homes += [bias_ref.at[:, pl.ds(k * units, units)] for k in range(2)]
     loads = [
         pltpu.make_async_copy(held, home, sems.at[k])
         for k, (held, home) in enumerate(zip(held_refs, homes))
@@ -293,22 +297,18 @@
         load.wait()
     lax.fori_loop(0, blocks // 2 * 4, project, 0)
     lax.fori_loop(0, blocks, attend, 0)
-    for load in loads[4:6]:
+    for load in loads[4:]:
         load.wait()
     lax.fori_loop(0, blocks // 2 * 2, join, 0)
     lax.fori_loop(0, blocks, middle_block, 0)
 
 
-def back_kernel(length, core_ref, mean_ref, pooled_a_ref, pooled_b_ref, back_a_ref, back_b_ref, result_ref):
+def back_kernel(length, core_ref, mean_ref, pooled_ref, back_ref, result_ref):
     count = mean_ref.shape[0]
-
-    def spread(pooled_ref):
-        pooled = pooled_ref[...] * (0.5 / length)
-        coarse = pooled.astype(jnp.bfloat16)
-        fine = (pooled - coarse.astype(jnp.float32)).astype(jnp.bfloat16)
-        return jnp.concatenate([coarse, fine], axis=0)
-
-    back = dot(spread(pooled_a_ref), back_a_ref[...]) + dot(spread(pooled_b_ref), back_b_ref[...])
+    pooled = pooled_ref[...] * (0.5 / length)
+    coarse = pooled.astype(jnp.bfloat16)
+    fine = (pooled - coarse.astype(jnp.float32)).astype(jnp.bfloat16)
+    back = dot(jnp.concatenate([coarse, fine], axis=0), back_ref[...])
     mean = mean_ref[...] * (0.5 / length)
     result = (mean + back[:count] + back[count:]).astype(jnp.bfloat16)
     start = pl.multiple_of(core_ref[0] * count, count)
@@ -422,17 +422,20 @@
             pltpu.VMEM((plan.slots, length, features), jnp.bfloat16),
             pltpu.SemaphoreType.DMA((len(sources),)),
         ],
-        compiler_params=limit(16),
     )(core, order, *sources)
     far = swap(other)
     token_count = pair_count * length
-    normed, mean = pl.pallas_call(
+    units = 2 * w_in.shape[1]
+    normed, mean, all_in, all_back, all_bias = pl.pallas_call(
         functools.partial(attention_kernel, length, head_dim),
         out_shape=(
             jax.ShapeDtypeStruct((token_count, width), jnp.bfloat16),
             jax.ShapeDtypeStruct((mine, width), jnp.float32),
+            jax.ShapeDtypeStruct((width, units), jnp.bfloat16),
+            jax.ShapeDtypeStruct((units, width), jnp.bfloat16),
+            jax.ShapeDtypeStruct((1, units), jnp.float32),
         ),
-        in_specs=[smem] * 3 + [vmem] * 4 + [hbm] * 6,
+        in_specs=[smem] * 3 + [vmem] * 4 + [hbm] * 12,
         scratch_shapes=[
             pltpu.VMEM((width, 2 * width), jnp.bfloat16),
             pltpu.VMEM((width, width), jnp.bfloat16),
@@ -440,10 +443,10 @@
             pltpu.VMEM((token_count, 2 * width), jnp.bfloat16),
             pltpu.VMEM((token_count, width), jnp.bfloat16),
             pltpu.VMEM((token_count, width), jnp.float32),
-            pltpu.SemaphoreType.DMA((6,)),
+            pltpu.SemaphoreType.DMA((12,)),
             pltpu.SemaphoreType.DMA((2,)),
         ],
-        compiler_params=limit(24),
+        compiler_params=limit(32),
         cost_estimate=pl.CostEstimate(
             flops=6 * token_count * width * width,
             bytes_accessed=4 * 2**20,
@@ -463,20 +466,19 @@
         far_value,
         w_out,
         far_out,
+        w_in,
+        far_in,
+        w_back,
+        far_back,
+        bias_in.reshape(1, -1),
+        far_bias.reshape(1, -1),
     )
     here = pl.pallas_call(
         functools.partial(back_kernel, length),
         out_shape=jax.ShapeDtypeStruct((pair_count, width), jnp.bfloat16),
-        in_specs=[smem] + [vmem] * 5,
+        in_specs=[smem] + [vmem] * 3,
         compiler_params=limit(16),
-    )(
-        core,
-        mean,
-        expand(normed, w_in, bias_in, length),
-        expand(normed, far_in, far_bias, length),
-        w_back,
-        far_back,
-    )
+    )(core, mean, expand(normed, all_in, all_bias, length), all_back)
     return here + swap(here)
 
 

time: 89.8 us -> 86.3 us (0.961)
  matrix products: 6.55 us -> 4.15 us
  local copies, waits for them, and re-layouts: 2.88 us -> 1.75 us
    dot_general x2 -> x1, matrix products: 6.55 us -> 4.15 us  [dot(): return jnp.dot(a, b, preferred_element_type=jnp.float32)]
    pallas_call x1, Pallas kernels: 2.02 us -> 0.47 us  [on_device(): pl.pallas_call(functools.partial(back_kernel, length), out_shape=jax.Shap...]
    pallas_call x1, Pallas kernels: 2.01 us -> 3.29 us  [on_device(): pl.pallas_call(functools.partial(pick_kernel, plan), out_shape=[images(pa...]
    unnamed x24 -> x18, local copies, waits for them, and re-layouts: 2.88 us -> 1.75 us
where the time goes in v4:
time: 86.3 us; the launch traced here: 85.9 us
  waiting for transfers between devices  33.9 us (39%)
  Pallas kernels  20.1 us (23%)
  blocking collectives  13.6 us (16%)
  starting transfers between devices  9.75 us (11%)
  matrix products  4.15 us (5%)
  other arithmetic  1.84 us (2%)
  local copies, waits for them, and re-layouts  1.75 us (2%)
    ppermute x4, waiting for transfers between devices, across(): lax.ppermute(values, 'shard', [(k, k ^ distance) for k in range(owner_cou...  29.4 us
    all_to_all x1, blocking collectives, on_device(): lax.all_to_all(wanted, 'shard', split_axis=0, concat_axis=0, tiled=True)  13.6 us
    pallas_call x1, Pallas kernels, on_device(): pl.pallas_call(functools.partial(attention_kernel, length, head_dim), out...  9.25 us
    ppermute x9, waiting for transfers between devices, swap(): return lax.ppermute(values, 'mp', [(0, 1), (1, 0)])  4.55 us
    all_to_all x1, starting transfers between devices, on_device(): lax.all_to_all(served, 'shard', split_axis=0, concat_axis=0, tiled=True)  4.26 us
    dot_general x1, matrix products, dot(): return jnp.dot(a, b, preferred_element_type=jnp.float32)  4.15 us
    ppermute x4, starting transfers between devices, across(): lax.ppermute(values, 'shard', [(k, k ^ distance) for k in range(owner_cou...  3.56 us
    pallas_call x1, Pallas kernels, on_device(): pl.pallas_call(functools.partial(pick_kernel, plan), out_shape=[images(pa...  3.29 us
  transfers between devices with their start and end apart: 14, of which 8 were waited for; matrix products, arithmetic and copies ran while one was open for 0% of the time, Pallas kernels for 2%

profile of v4, /device:TPU:0, one launch (start us, length us, event | category | flops | bytes accessed | tf_op | source)
XLA Modules:
  0.0 85.9 jit_solution(16813996618719966092)
XLA Ops:
  0.0 1.8 %shard_map.118 = (s32[8,1,36]{2,1,0:T(1,128)}, s32[1,128]{1,0:T(1,128)}) custom-call(s32[1]{0:T(128)} %bitcast.1.shard_ref, s32[2,64]{1,0:T(2,128)} %bitcast.21, s32[2,64]{1,0:T(2,128)} %bitcast.22), custom_call_target="tpu_custom_call" | custom-call | tf_op jit(solution)/shard_map/pallas_call | solution.py:367
  1.8 13.6 %all_to_all.10.incoming_ref = s32[8,1,36]{2,1,0:T(1,128)} all-to-all(s32[8,1,36]{2,1,0:T(1,128)} %get-tuple-element.54), channel_id=1, replica_groups=mesh['groups'=2,'shard'=8,'mp'=2] {'shard'}, dimensions={0} | all-to-all | bytes 2304 | tf_op jit(solution)/shard_map/all_to_all | solution.py:375
  15.4 3.2 %shard_map.119 = (bf16[32,16,256]{2,1,0:T(8,128)(2,1)}, bf16[32,16,256]{2,1,0:T(8,128)(2,1)}, bf16[32,16,256]{2,1,0:T(8,128)(2,1)}, bf16[32,16,256]{2,1,0:T(8,12...) custom-call(s32[1]{0:T(128)} %bitcast.1.shard_ref, s32[8,1,36]{2,1,0:T(1,128)} %all_to_all.10.incoming_ref, ...), custom_call_target="tpu_custom_call" | custom-call | tf_op jit(solution)/shard_map/pallas_call | solution.py:385
  18.6 0.8 collective-permute-start.1
  19.4 0.6 collective-permute-start.2
  20.0 2.2 %collective-permute-start.3 = (bf16[32,16,256]{2,1,0:T(8,128)(2,1)}, bf16[32,16,256]{2,1,0:T(8,128)(2,1)S(1)}, u32[]{:S(2)}, u32[]{:S(2)}) collective-permute-start(bf16[32,16,256]{2,1,0:T(8,128)(2,1)} %get-tuple-element.59), channel_id=1, source_target_pairs={{0,6},{2,4},{4,2},{6,0},{8,14},{10,12},{12,10},{14,8},{1,7},{3,5},... | collective-permute-start | bytes 786440 | tf_op jit(solution)/shard_map/ppermute | solution.py:355
  22.2 4.3 %all-to-all-start.1 = ((bf16[8,16,16,256]{3,2,1,0:T(8,128)(2,1)}), bf16[8,16,16,256]{3,2,1,0:T(8,128)(2,1)}, u32[]{:S(2)}, u32[]{:S(2)}) async-start(bf16[8,16,16,256]{3,2,1,0:T(8,128)(2,1)} %get-tuple-element.55), calls=%async_computation.1 | async-start | bytes 2097152 | tf_op jit(solution)/shard_map/all_to_all | solution.py:393
  26.5 1.1 %collective-permute-done.1.refs_1_.refs_2_ = bf16[32,16,256]{2,1,0:T(8,128)(2,1)S(1)} collective-permute-done((bf16[32,16,256]{2,1,0:T(8,128)(2,1)}, bf16[32,16,256]{2,1,0:T(8,128)(2,1)S(1)}, u32[]{:S(2)}, u32[]{:S(2)}) %collective-permute-start.1) | collective-permute-done | bytes 262176 | tf_op jit(solution)/shard_map/ppermute | solution.py:355
  27.5 1.3 %collective-permute-done.2.refs_2_.refs_3_ = bf16[32,16,256]{2,1,0:T(8,128)(2,1)S(1)} collective-permute-done((bf16[32,16,256]{2,1,0:T(8,128)(2,1)}, bf16[32,16,256]{2,1,0:T(8,128)(2,1)S(1)}, u32[]{:S(2)}, u32[]{:S(2)}) %collective-permute-start.2) | collective-permute-done | bytes 262176 | tf_op jit(solution)/shard_map/ppermute | solution.py:355
  28.9 10.9 %collective-permute-done.3.refs_3_.refs_4_ = bf16[32,16,256]{2,1,0:T(8,128)(2,1)S(1)} collective-permute-done((bf16[32,16,256]{2,1,0:T(8,128)(2,1)}, bf16[32,16,256]{2,1,0:T(8,128)(2,1)S(1)}, u32[]{:S(2)}, u32[]{:S(2)}) %collective-permute-start.3) | collective-permute-done | bytes 262176 | tf_op jit(solution)/shard_map/ppermute | solution.py:355
  39.7 0.5 collective-permute-start.10
  40.8 2.1 %shard_map.120 = (bf16[32,16,256]{2,1,0:T(8,128)(2,1)}, bf16[32,16,256]{2,1,0:T(8,128)(2,1)S(1)}) custom-call(s32[1]{0:T(128)} %bitcast.1.shard_ref, s32[8,1,36]{2,1,0:T(1,128)} %all_to_all.10.incoming_ref, bf16[32,16,256]{2,1,0:T(8,128)(2,1)} %get-tuple-element.78.refs_0_.refs_1_, bf16[32,16,256]{2,1,0:T(8,128)(2,1)} %copy-done.5, ...), custom_call_target="tpu_custom_call" | custom-call | flops 199999995904 | bytes 1048576 | tf_op jit(solution)/shard_map/pallas_call | solution.py:395
  42.9 0.6 collective-permute-start.6
  44.2 0.9 %collective-permute-done.6.refs_5_ = bf16[512,256]{1,0:T(8,128)(2,1)S(1)} collective-permute-done((bf16[512,256]{1,0:T(8,128)(2,1)S(1)}, bf16[512,256]{1,0:T(8,128)(2,1)S(1)}, u32[]{:S(2)}, u32[]{:S(2)}) %collective-permute-start.6) | collective-permute-done | bytes 262176 | tf_op jit(solution)/shard_map/ppermute | solution.py:352
  45.5 16.1 %collective-permute-done.4.refs_5_ = bf16[32,16,256]{2,1,0:T(8,128)(2,1)S(1)} collective-permute-done((bf16[32,16,256]{2,1,0:T(8,128)(2,1)}, bf16[32,16,256]{2,1,0:T(8,128)(2,1)S(1)}, u32[]{:S(2)}, u32[]{:S(2)}) %collective-permute-start.4) | collective-permute-done | bytes 262176 | tf_op jit(solution)/shard_map/ppermute | solution.py:355
  61.7 0.7 copy-done.8
  62.3 3.3 %shard_map.121 = (bf16[64,16,256]{2,1,0:T(8,128)(2,1)}, bf16[64,16,256]{2,1,0:T(8,128)(2,1)}) custom-call(s32[1]{0:T(128)} %bitcast.core_ref, s32[1,128]{1,0:T(1,128)} %get-tuple-element.69.list_ref, bf16[128,16,256]{2,1,0:T(8,128)(2,1)} %bitcast.4.refs_0_, bf16[32,16,256]{2,1,0:T(8,128)(2,1)} %get-tuple-element.78.refs_0_.refs_1_, ...), custom_call_target="tpu_custom_call" | custom-call | tf_op jit(solution)/shard_map/pallas_call | solution.py:417
  65.7 2.1 %collective-permute-done.12.refs_1_ = bf16[64,16,256]{2,1,0:T(8,128)(2,1)S(1)} collective-permute-done((bf16[64,16,256]{2,1,0:T(8,128)(2,1)}, bf16[64,16,256]{2,1,0:T(8,128)(2,1)S(1)}, u32[]{:S(2)}, u32[]{:S(2)}) %collective-permute-start.12) | collective-permute-done | bytes 524320 | tf_op jit(solution)/shard_map/ppermute | solution.py:352
  67.8 1.0 %copy-done = bf16[64,16,256]{2,1,0:T(8,128)(2,1)S(1)} copy-done((bf16[64,16,256]{2,1,0:T(8,128)(2,1)S(1)}, bf16[64,16,256]{2,1,0:T(8,128)(2,1)}, u32[]{:S(2)}) %copy-start) | copy-done | bytes 524312
  68.9 9.3 %shard_map.122 = (bf16[1024,512]{1,0:T(8,128)(2,1)S(1)}, f32[32,512]{1,0:T(8,128)S(1)}, bf16[512,2048]{1,0:T(8,128)(2,1)S(1)}, bf16[2048,512]{1,0:T(8,128)(2,1)S(1)}, f32[1,2048]{1,0:T(1,128)S(1)}) custom-call(s32[1]{0:T(128)} %bitcast.core_ref, f32[4]{0:T(128)} %scale_a_ref.1, f32[4]{0:T(128)} %collective-permute-done.11.scale_b_ref, ...), custom_call_target="tpu_custom_call" | custom-call | flops 1610612736 | bytes 4194304 | tf_op jit(solution)/shard_map/pallas_call | solution.py:429
  78.1 4.1 %fusion.7 = bf16[1024,2048]{1,0:T(8,128)(2,1)S(1)} fusion(f32[2048]{0:T(1024)S(1)} %bitcast.19, bf16[1024,512]{1,0:T(8,128)(2,1)S(1)} %get-tuple-element.94, bf16[512,2048]{1,0:T(8,128)(2,1)S(1)} %get-tuple-element.95), kind=kOutput, calls=%fused_computation.8 | convolution fusion | flops 2168455168 | bytes 7348224 | tf_op jit(solution)/shard_map/dot_general | solution.py:25
  82.3 1.2 %convert_reduce_fusion = f32[4,8,2048]{2,1,0:T(8,128)S(1)} fusion(bf16[4,2,8,16,2048]{4,3,2,1,0:T(8,128)(2,1)S(1)} %bitcast.20), kind=kLoop, calls=%fused_computation.9 | loop fusion | flops 4128768 | bytes 4456448 | tf_op jit(solution)/shard_map/reduce_sum | solution.py:323
  84.2 1.1 %collective-permute-done.13 = bf16[64,512]{1,0:T(8,128)(2,1)S(1)} collective-permute-done((bf16[64,512]{1,0:T(8,128)(2,1)S(1)}, bf16[64,512]{1,0:T(8,128)(2,1)S(1)}, u32[]{:S(2)}, u32[]{:S(2)}) %collective-permute-start.13) | collective-permute-done | bytes 65568 | tf_op jit(solution)/shard_map/ppermute | solution.py:352
  85.3 0.6 add.28
  (33 shorter events, 1.8 us)
Async XLA Ops:
  18.6 8.9 %collective-permute-start.1 = (bf16[32,16,256]{2,1,0:T(8,128)(2,1)}, bf16[32,16,256]{2,1,0:T(8,128)(2,1)S(1)}, u32[]{:S(2)}, u32[]{:S(2)}) collective-permute-start(bf16[32,16,256]{2,1,0:T(8,128)(2,1)} %get-tuple-element.57), channel_id=1, source_target_pairs={{0,2},{2,0},{4,6},{6,4},{8,10},{10,8},{12,14},{14,12},{1,3},{3,1},... | collective-permute-start | bytes 786440 | tf_op jit(solution)/shard_map/ppermute | solution.py:355
  19.4 9.5 %collective-permute-start.2 = (bf16[32,16,256]{2,1,0:T(8,128)(2,1)}, bf16[32,16,256]{2,1,0:T(8,128)(2,1)S(1)}, u32[]{:S(2)}, u32[]{:S(2)}) collective-permute-start(bf16[32,16,256]{2,1,0:T(8,128)(2,1)} %get-tuple-element.58), channel_id=1, source_target_pairs={{0,4},{2,6},{4,0},{6,2},{8,12},{10,14},{12,8},{14,10},{1,5},{3,7},... | collective-permute-start | bytes 786440 | tf_op jit(solution)/shard_map/ppermute | solution.py:355
  20.0 19.7 %collective-permute-start.3 = (bf16[32,16,256]{2,1,0:T(8,128)(2,1)}, bf16[32,16,256]{2,1,0:T(8,128)(2,1)S(1)}, u32[]{:S(2)}, u32[]{:S(2)}) collective-permute-start(bf16[32,16,256]{2,1,0:T(8,128)(2,1)} %get-tuple-element.59), channel_id=1, source_target_pairs={{0,6},{2,4},{4,2},{6,0},{8,14},{10,12},{12,10},{14,8},{1,7},{3,5},... | collective-permute-start | bytes 786440 | tf_op jit(solution)/shard_map/ppermute | solution.py:355
  22.2 39.5 %all-to-all-start.1 = ((bf16[8,16,16,256]{3,2,1,0:T(8,128)(2,1)}), bf16[8,16,16,256]{3,2,1,0:T(8,128)(2,1)}, u32[]{:S(2)}, u32[]{:S(2)}) async-start(bf16[8,16,16,256]{3,2,1,0:T(8,128)(2,1)} %get-tuple-element.55), calls=%async_computation.1 | async-start | bytes 2097152 | tf_op jit(solution)/shard_map/all_to_all | solution.py:393
  27.5 13.2 %copy-start.5 = (bf16[32,16,256]{2,1,0:T(8,128)(2,1)}, bf16[32,16,256]{2,1,0:T(8,128)(2,1)S(1)}, u32[]{:S(2)}) copy-start(bf16[32,16,256]{2,1,0:T(8,128)(2,1)S(1)} %collective-permute-done.1.refs_1_.refs_2_) | copy-start | bytes 786436
  28.9 11.9 %copy-start.6 = (bf16[32,16,256]{2,1,0:T(8,128)(2,1)}, bf16[32,16,256]{2,1,0:T(8,128)(2,1)S(1)}, u32[]{:S(2)}) copy-start(bf16[32,16,256]{2,1,0:T(8,128)(2,1)S(1)} %collective-permute-done.2.refs_2_.refs_3_) | copy-start | bytes 786436
  39.7 1.0 %copy-start.7 = (bf16[32,16,256]{2,1,0:T(8,128)(2,1)}, bf16[32,16,256]{2,1,0:T(8,128)(2,1)S(1)}, u32[]{:S(2)}) copy-start(bf16[32,16,256]{2,1,0:T(8,128)(2,1)S(1)} %collective-permute-done.3.refs_3_.refs_4_) | copy-start | bytes 786436
  39.7 3.2 %collective-permute-start.11 = (f32[4]{0:T(128)}, f32[4]{0:T(128)}, u32[]{:S(2)}, u32[]{:S(2)}) collective-permute-start(f32[4]{0:T(128)} %scale_a_ref.1), channel_id=1, source_target_pairs={{0,1},{1,0},{2,3},{3,2},{4,5},{5,4},{6,7},{7,6},{8,9},{9,8},{10,11... | collective-permute-start | bytes 56 | tf_op jit(solution)/shard_map/ppermute | solution.py:352
  39.7 3.7 %collective-permute-start.10 = (f32[1024]{0:T(1024)}, f32[1024]{0:T(1024)}, u32[]{:S(2)}, u32[]{:S(2)}) collective-permute-start(f32[1024]{0:T(1024)} %param.24), channel_id=1, source_target_pairs={{0,1},{1,0},{2,3},{3,2},{4,5},{5,4},{6,7},{7,6},{8,9},{9,8},{10,11... | collective-permute-start | bytes 12296 | tf_op jit(solution)/shard_map/ppermute | solution.py:352
  40.2 3.3 %collective-permute-start.5 = (bf16[512,256]{1,0:T(8,128)(2,1)}, bf16[512,256]{1,0:T(8,128)(2,1)}, u32[]{:S(2)}, u32[]{:S(2)}) collective-permute-start(bf16[512,256]{1,0:T(8,128)(2,1)} %refs_2_.1), channel_id=1, source_target_pairs={{0,1},{1,0},{2,3},{3,2},{4,5},{5,4},{6,7},{7,6},{8,9},{9,8},{10,11... | collective-permute-start | bytes 786440 | tf_op jit(solution)/shard_map/ppermute | solution.py:352
  40.2 21.4 %collective-permute-start.8 = (bf16[512,1024]{1,0:T(8,128)(2,1)}, bf16[512,1024]{1,0:T(8,128)(2,1)}, u32[]{:S(2)}, u32[]{:S(2)}) collective-permute-start(bf16[512,1024]{1,0:T(8,128)(2,1)} %refs_8_.1), channel_id=1, source_target_pairs={{0,1},{1,0},{2,3},{3,2},{4,5},{5,4},{6,7},{7,6},{8,9},{9,8},{10,11... | collective-permute-start | bytes 3145736 | tf_op jit(solution)/shard_map/ppermute | solution.py:352
  40.7 20.9 %collective-permute-start.9 = (bf16[1024,512]{1,0:T(8,128)(2,1)}, bf16[1024,512]{1,0:T(8,128)(2,1)}, u32[]{:S(2)}, u32[]{:S(2)}) collective-permute-start(bf16[1024,512]{1,0:T(8,128)(2,1)} %refs_10_.1), channel_id=1, source_target_pairs={{0,1},{1,0},{2,3},{3,2},{4,5},{5,4},{6,7},{7,6},{8,9},{9,8},{10,11... | collective-permute-start | bytes 3145736 | tf_op jit(solution)/shard_map/ppermute | solution.py:352
  40.8 2.1 %copy-start.1 = (bf16[512,256]{1,0:T(8,128)(2,1)S(1)}, bf16[512,256]{1,0:T(8,128)(2,1)}, u32[]{:S(2)}) copy-start(bf16[512,256]{1,0:T(8,128)(2,1)} %refs_4_.1) | copy-start | bytes 786436
  40.8 2.7 %copy-start.2 = (bf16[256,512]{1,0:T(8,128)(2,1)S(1)}, bf16[256,512]{1,0:T(8,128)(2,1)}, u32[]{:S(2)}) copy-start(bf16[256,512]{1,0:T(8,128)(2,1)} %refs_6_.1) | copy-start | bytes 786436
  40.8 27.0 %copy-start.3 = (f32[512]{0:T(512)S(1)}, f32[512]{0:T(512)}, u32[]{:S(2)}) copy-start(f32[512]{0:T(512)} %param.17) | copy-start | bytes 6148
  40.8 27.0 %copy-start.4 = (f32[512]{0:T(512)S(1)}, f32[512]{0:T(512)}, u32[]{:S(2)}) copy-start(f32[512]{0:T(512)} %param.22) | copy-start | bytes 6148
  42.9 2.2 %collective-permute-start.6 = (bf16[512,256]{1,0:T(8,128)(2,1)S(1)}, bf16[512,256]{1,0:T(8,128)(2,1)S(1)}, u32[]{:S(2)}, u32[]{:S(2)}) collective-permute-start(bf16[512,256]{1,0:T(8,128)(2,1)S(1)} %copy-done.1), channel_id=1, source_target_pairs={{0,1},{1,0},{2,3},{3,2},{4,5},{5,4},{6,7},{7,6},{8,9},{9,8},{10,11... | collective-permute-start | bytes 786440 | tf_op jit(solution)/shard_map/ppermute | solution.py:352
  43.5 2.1 %collective-permute-start.7 = (bf16[256,512]{1,0:T(8,128)(2,1)S(1)}, bf16[256,512]{1,0:T(8,128)(2,1)S(1)}, u32[]{:S(2)}, u32[]{:S(2)}) collective-permute-start(bf16[256,512]{1,0:T(8,128)(2,1)S(1)} %copy-done.2), channel_id=1, source_target_pairs={{0,1},{1,0},{2,3},{3,2},{4,5},{5,4},{6,7},{7,6},{8,9},{9,8},{10,11... | collective-permute-start | bytes 786440 | tf_op jit(solution)/shard_map/ppermute | solution.py:352
  43.6 18.1 %collective-permute-start.4 = (bf16[32,16,256]{2,1,0:T(8,128)(2,1)}, bf16[32,16,256]{2,1,0:T(8,128)(2,1)S(1)}, u32[]{:S(2)}, u32[]{:S(2)}) collective-permute-start(bf16[32,16,256]{2,1,0:T(8,128)(2,1)} %get-tuple-element.60), channel_id=1, source_target_pairs={{0,8},{2,10},{4,12},{6,14},{8,0},{10,2},{12,4},{14,6},{1,9},{3,11}... | collective-permute-start | bytes 786440 | tf_op jit(solution)/shard_map/ppermute | solution.py:355
  61.6 0.7 copy-start.8
  65.6 2.2 %collective-permute-start.12 = (bf16[64,16,256]{2,1,0:T(8,128)(2,1)}, bf16[64,16,256]{2,1,0:T(8,128)(2,1)S(1)}, u32[]{:S(2)}, u32[]{:S(2)}) collective-permute-start(bf16[64,16,256]{2,1,0:T(8,128)(2,1)} %get-tuple-element.86), channel_id=1, source_target_pairs={{0,1},{1,0},{2,3},{3,2},{4,5},{5,4},{6,7},{7,6},{8,9},{9,8},{10,11... | collective-permute-start | bytes 1572872 | tf_op jit(solution)/shard_map/ppermute | solution.py:352
  67.8 1.0 %copy-start = (bf16[64,16,256]{2,1,0:T(8,128)(2,1)S(1)}, bf16[64,16,256]{2,1,0:T(8,128)(2,1)}, u32[]{:S(2)}) copy-start(bf16[64,16,256]{2,1,0:T(8,128)(2,1)} %get-tuple-element.85.refs_0_) | copy-start | bytes 1572868
  84.0 1.3 %collective-permute-start.13 = (bf16[64,512]{1,0:T(8,128)(2,1)S(1)}, bf16[64,512]{1,0:T(8,128)(2,1)S(1)}, u32[]{:S(2)}, u32[]{:S(2)}) collective-permute-start(bf16[64,512]{1,0:T(8,128)(2,1)S(1)} %shard_map.123), channel_id=1, source_target_pairs={{0,1},{1,0},{2,3},{3,2},{4,5},{5,4},{6,7},{7,6},{8,9},{9,8},{10,11... | collective-permute-start | bytes 196616 | tf_op jit(solution)/shard_map/ppermute | solution.py:352

commit v5 on v4

--- a/solution.py
+++ b/solution.py
@@ -178,15 +178,21 @@
 
 
 def attention_kernel(
+    plan,
     length,
     head_dim,
     core_ref,
+    list_ref,
+    crowded_ref,
     scale_a_ref,
     scale_b_ref,
     gain_attn_ref,
     gain_mlp_ref,
     *refs,
 ):
+    if plan.extra:
+        rest_held_refs, refs = refs[:4], refs[4:]
+        *refs, rest_ref, rest_sems = refs
     own_held_ref, far_held_ref, *held_refs = refs[:14]
     normed_ref, mean_ref, in_ref, back_ref, bias_ref = refs[14:19]
     qkv_ref, out_ref, tokens_ref, heads_ref, mixed_ref, hidden_ref, sems, token_sems = refs[19:]
@@ -207,7 +213,26 @@
         pltpu.make_async_copy(own_held_ref, tokens_ref.at[core], token_sems.at[0]),
         pltpu.make_async_copy(far_held_ref, tokens_ref.at[1 - core], token_sems.at[1]),
     ]
-    for load in token_loads + loads:
+    for load in token_loads:
+        load.start()
+    if plan.extra:
+        rest_loads = [
+            pltpu.make_async_copy(
+                held, rest_ref.at[side, pl.ds(at * plan.part, plan.part)], rest_sems.at[index]
+            )
+            for index, (held, side, at) in enumerate(
+                zip(rest_held_refs, (core, 1 - core, core, 1 - core), (0, 0, 1, 1))
+            )
+        ]
+        for load in rest_loads[:2]:
+            load.start()
+
+        @pl.when(crowded_ref[0] > 0)
+        def _():
+            for load in rest_loads[2:]:
+                load.start()
+
+    for load in loads:
         load.start()
     half = BLOCK * length
     rows = 2 * half
@@ -292,6 +317,26 @@
 
     for load in token_loads:
         load.wait()
+    if plan.extra:
+        for load in rest_loads[:2]:
+            load.wait()
+
+        @pl.when(crowded_ref[0] > 0)
+        def _():
+            for load in rest_loads[2:]:
+                load.wait()
+
+        def put(index, carry):
+            where = list_ref[0, core * tokens_ref.shape[1] + index] - plan.rest_at
+
+            @pl.when(where >= 0)
+            def _():
+                for side in range(2):
+                    tokens_ref[side, index] = rest_ref[side, where]
+
+            return carry
+
+        lax.fori_loop(0, tokens_ref.shape[1], put, 0, unroll=4)
     lax.fori_loop(0, blocks, start_block, 0)
     for load in loads[:4]:
         load.wait()
@@ -401,19 +446,11 @@
             ),
         )(shard, incoming, *chunks)
         first = across(first, plan.half)
-        sources = [returned, *chunks, first]
+        sources = [returned, *chunks]
     weights = (w_qk, w_value, w_out, w_in, w_back, bias_in, logit_scale)
     if plan.extra:
         chunks, weights = lax.optimization_barrier((chunks, weights))
     swapped = [swap(w) for w in weights]
-    sources, swapped = lax.optimization_barrier((sources, swapped))
-    far_qk, far_value, far_out, far_in, far_back, far_bias, far_scale = swapped
-    if plan.extra:
-        second, sources = lax.optimization_barrier((second, sources))
-        second = lax.cond(
-            crowded[0] > 0, lambda part: across(part, plan.half), lambda part: part, second
-        )
-        sources = [*sources, second]
     own, other = pl.pallas_call(
         functools.partial(pick_kernel, plan),
         out_shape=[images(pair_count)] * 2,
@@ -424,10 +461,26 @@
         ],
     )(core, order, *sources)
     far = swap(other)
+    rest = []
+    if plan.extra:
+        first, second, swapped = lax.optimization_barrier((first, second, swapped))
+        far_first = swap(first)
+
+        def fetch_second(part):
+            part = across(part, plan.half)
+            return part, swap(part)
+
+        second, far_second = lax.cond(
+            crowded[0] > 0, fetch_second, lambda part: (part, part), second
+        )
+        rest = [first, far_first, second, far_second]
+    else:
+        crowded = jnp.zeros((1,), jnp.int32)
+    far_qk, far_value, far_out, far_in, far_back, far_bias, far_scale = swapped
     token_count = pair_count * length
     units = 2 * w_in.shape[1]
     normed, mean, all_in, all_back, all_bias = pl.pallas_call(
-        functools.partial(attention_kernel, length, head_dim),
+        functools.partial(attention_kernel, plan, length, head_dim),
         out_shape=(
             jax.ShapeDtypeStruct((token_count, width), jnp.bfloat16),
             jax.ShapeDtypeStruct((mine, width), jnp.float32),
@@ -435,7 +488,7 @@
             jax.ShapeDtypeStruct((units, width), jnp.bfloat16),
             jax.ShapeDtypeStruct((1, units), jnp.float32),
         ),
-        in_specs=[smem] * 3 + [vmem] * 4 + [hbm] * 12,
+        in_specs=[smem] * 5 + [vmem] * 2 + [hbm] * len(rest) + [vmem] * 2 + [hbm] * 12,
         scratch_shapes=[
             pltpu.VMEM((width, 2 * width), jnp.bfloat16),
             pltpu.VMEM((width, width), jnp.bfloat16),
@@ -445,7 +498,15 @@
             pltpu.VMEM((token_count, width), jnp.float32),
             pltpu.SemaphoreType.DMA((12,)),
             pltpu.SemaphoreType.DMA((2,)),
-        ],
+        ]
+        + (
+            [
+                pltpu.VMEM((2, 2 * plan.part, length, features), jnp.bfloat16),
+                pltpu.SemaphoreType.DMA((4,)),
+            ]
+            if rest
+            else []
+        ),
         compiler_params=limit(32),
         cost_estimate=pl.CostEstimate(
             flops=6 * token_count * width * width,
@@ -454,10 +515,13 @@
         ),
     )(
         core,
+        order,
+        crowded,
         logit_scale,
         far_scale,
         gain_attn.reshape(1, -1),
         gain_mlp.reshape(1, -1),
+        *rest,
         own,
         far,
         w_qk,

time: 86.3 us -> 82.8 us (0.959)
  waiting for transfers between devices: 33.9 us -> 28.2 us
  Pallas kernels: 20.1 us -> 21.3 us
    ppermute x4, waiting for transfers between devices: 29.4 us -> 14.5 us  [across(): lax.ppermute(values, 'shard', [(k, k ^ distance) for k in range(owner_cou...]
    all_to_all x1, waiting for transfers between devices: 0.01 us -> 12.5 us  [on_device(): lax.all_to_all(served, 'shard', split_axis=0, concat_axis=0, tiled=True)]
    ppermute x9 -> x10, waiting for transfers between devices: 4.55 us -> 1.14 us  [swap(): return lax.ppermute(values, 'mp', [(0, 1), (1, 0)])]
    pallas_call x1, Pallas kernels: 9.25 us -> 10.5 us  [on_device(): pl.pallas_call(functools.partial(attention_kernel, plan, length, head_dim...]
    ppermute x9 -> x10, starting transfers between devices: 1.93 us -> 2.12 us  [swap(): return lax.ppermute(values, 'mp', [(0, 1), (1, 0)])]
    unnamed x18 -> x24, local copies, waits for them, and re-layouts: 1.75 us -> 1.66 us
  transfers between devices with their start and end apart: 14 -> 15, of which waited for: 8 -> 7; matrix products, arithmetic and copies ran while one was open for 0% -> 1% of each run, Pallas kernels for 2% -> 6%
where the time goes in v5:
time: 82.8 us; the launch traced here: 82.4 us
  waiting for transfers between devices  28.2 us (34%)
  Pallas kernels  21.3 us (26%)
  blocking collectives  13.8 us (17%)
  starting transfers between devices  10 us (12%)
  matrix products  4.15 us (5%)
  local copies, waits for them, and re-layouts  2.37 us (3%)
  other arithmetic  1.84 us (2%)
    ppermute x4, waiting for transfers between devices, across(): lax.ppermute(values, 'shard', [(k, k ^ distance) for k in range(owner_cou...  14.5 us
    all_to_all x1, blocking collectives, on_device(): lax.all_to_all(wanted, 'shard', split_axis=0, concat_axis=0, tiled=True)  13.8 us
    all_to_all x1, waiting for transfers between devices, on_device(): lax.all_to_all(served, 'shard', split_axis=0, concat_axis=0, tiled=True)  12.5 us
    pallas_call x1, Pallas kernels, on_device(): pl.pallas_call(functools.partial(attention_kernel, plan, length, head_dim...  10.5 us
    all_to_all x1, starting transfers between devices, on_device(): lax.all_to_all(served, 'shard', split_axis=0, concat_axis=0, tiled=True)  4.24 us
    dot_general x1, matrix products, dot(): return jnp.dot(a, b, preferred_element_type=jnp.float32)  4.15 us
    ppermute x4, starting transfers between devices, across(): lax.ppermute(values, 'shard', [(k, k ^ distance) for k in range(owner_cou...  3.66 us
    pallas_call x1, Pallas kernels, on_device(): pl.pallas_call(functools.partial(pick_kernel, plan), out_shape=[images(pa...  3.19 us
  transfers between devices with their start and end apart: 15, of which 7 were waited for; matrix products, arithmetic and copies ran while one was open for 1% of the time, Pallas kernels for 6%

profile of v5, /device:TPU:0, one launch (start us, length us, event | category | flops | bytes accessed | tf_op | source)
XLA Modules:
  0.0 82.4 jit_solution(17900606075043087256)
XLA Ops:
  0.0 1.8 %shard_map.118 = (s32[8,1,36]{2,1,0:T(1,128)}, s32[1,128]{1,0:T(1,128)}) custom-call(s32[1]{0:T(128)} %bitcast.1.shard_ref, s32[2,64]{1,0:T(2,128)} %bitcast.21, s32[2,64]{1,0:T(2,128)} %bitcast.22), custom_call_target="tpu_custom_call" | custom-call | tf_op jit(solution)/shard_map/pallas_call | solution.py:412
  1.8 13.8 %all_to_all.10.incoming_ref = s32[8,1,36]{2,1,0:T(1,128)} all-to-all(s32[8,1,36]{2,1,0:T(1,128)} %get-tuple-element.43), channel_id=1, replica_groups=mesh['groups'=2,'shard'=8,'mp'=2] {'shard'}, dimensions={0} | all-to-all | bytes 2304 | tf_op jit(solution)/shard_map/all_to_all | solution.py:420
  15.5 3.2 %shard_map.119 = (bf16[32,16,256]{2,1,0:T(8,128)(2,1)}, bf16[32,16,256]{2,1,0:T(8,128)(2,1)}, bf16[32,16,256]{2,1,0:T(8,128)(2,1)}, bf16[32,16,256]{2,1,0:T(8,12...) custom-call(s32[1]{0:T(128)} %bitcast.1.shard_ref, s32[8,1,36]{2,1,0:T(1,128)} %all_to_all.10.incoming_ref, ...), custom_call_target="tpu_custom_call" | custom-call | tf_op jit(solution)/shard_map/pallas_call | solution.py:430
  18.7 0.6 collective-permute-start.2
  19.3 0.6 collective-permute-start.3
  19.9 2.4 %collective-permute-start.4 = (bf16[32,16,256]{2,1,0:T(8,128)(2,1)}, bf16[32,16,256]{2,1,0:T(8,128)(2,1)S(1)}, u32[]{:S(2)}, u32[]{:S(2)}) collective-permute-start(bf16[32,16,256]{2,1,0:T(8,128)(2,1)} %get-tuple-element.48), channel_id=1, source_target_pairs={{0,6},{2,4},{4,2},{6,0},{8,14},{10,12},{12,10},{14,8},{1,7},{3,5},... | collective-permute-start | bytes 786440 | tf_op jit(solution)/shard_map/ppermute | solution.py:400
  22.3 4.2 %all-to-all-start.1 = ((bf16[8,16,16,256]{3,2,1,0:T(8,128)(2,1)}), bf16[8,16,16,256]{3,2,1,0:T(8,128)(2,1)}, u32[]{:S(2)}, u32[]{:S(2)}) async-start(bf16[8,16,16,256]{3,2,1,0:T(8,128)(2,1)} %get-tuple-element.63), calls=%async_computation.1 | async-start | bytes 2097152 | tf_op jit(solution)/shard_map/all_to_all | solution.py:438
  26.5 1.4 %collective-permute-done.2.refs_1_.refs_2_ = bf16[32,16,256]{2,1,0:T(8,128)(2,1)S(1)} collective-permute-done((bf16[32,16,256]{2,1,0:T(8,128)(2,1)}, bf16[32,16,256]{2,1,0:T(8,128)(2,1)S(1)}, u32[]{:S(2)}, u32[]{:S(2)}) %collective-permute-start.2) | collective-permute-done | bytes 262176 | tf_op jit(solution)/shard_map/ppermute | solution.py:400
  27.9 0.8 %collective-permute-done.3.refs_2_.refs_3_ = bf16[32,16,256]{2,1,0:T(8,128)(2,1)S(1)} collective-permute-done((bf16[32,16,256]{2,1,0:T(8,128)(2,1)}, bf16[32,16,256]{2,1,0:T(8,128)(2,1)S(1)}, u32[]{:S(2)}, u32[]{:S(2)}) %collective-permute-start.3) | collective-permute-done | bytes 262176 | tf_op jit(solution)/shard_map/ppermute | solution.py:400
  28.8 11.0 %collective-permute-done.4.refs_3_.refs_4_ = bf16[32,16,256]{2,1,0:T(8,128)(2,1)S(1)} collective-permute-done((bf16[32,16,256]{2,1,0:T(8,128)(2,1)}, bf16[32,16,256]{2,1,0:T(8,128)(2,1)S(1)}, u32[]{:S(2)}, u32[]{:S(2)}) %collective-permute-start.4) | collective-permute-done | bytes 262176 | tf_op jit(solution)/shard_map/ppermute | solution.py:400
  39.8 0.5 collective-permute-start.11
  40.9 0.6 copy-done.7
  42.0 2.1 %shard_map.120 = (bf16[32,16,256]{2,1,0:T(8,128)(2,1)}, bf16[32,16,256]{2,1,0:T(8,128)(2,1)S(1)}) custom-call(s32[1]{0:T(128)} %bitcast.1.shard_ref, s32[8,1,36]{2,1,0:T(1,128)} %all_to_all.10.incoming_ref, bf16[32,16,256]{2,1,0:T(8,128)(2,1)} %get-tuple-element.45.refs_0_.refs_1_, bf16[32,16,256]{2,1,0:T(8,128)(2,1)} %copy-done.9, ...), custom_call_target="tpu_custom_call" | custom-call | flops 199999995904 | bytes 1048576 | tf_op jit(solution)/shard_map/pallas_call | solution.py:440
  44.4 12.5 %all-to-all-done.1 = bf16[8,16,16,256]{3,2,1,0:T(8,128)(2,1)} async-done(((bf16[8,16,16,256]{3,2,1,0:T(8,128)(2,1)}), bf16[8,16,16,256]{3,2,1,0:T(8,128)(2,1)}, u32[]{:S(2)}, u32[]{:S(2)}) %all-to-all-start.1) | async-done | bytes 1048608 | tf_op jit(solution)/shard_map/all_to_all | solution.py:438
  56.9 3.2 %shard_map.121 = (bf16[64,16,256]{2,1,0:T(8,128)(2,1)}, bf16[64,16,256]{2,1,0:T(8,128)(2,1)}) custom-call(s32[1]{0:T(128)} %bitcast.core_ref, s32[1,128]{1,0:T(1,128)} %get-tuple-element.42.list_ref, bf16[128,16,256]{2,1,0:T(8,128)(2,1)} %bitcast.7.refs_0_, bf16[32,16,256]{2,1,0:T(8,128)(2,1)} %get-tuple-element.45.refs_0_.refs_1_, ...), custom_call_target="tpu_custom_call" | custom-call | tf_op jit(solution)/shard_map/pallas_call | solution.py:454
  60.2 1.2 %collective-permute-done.5.refs_0_ = bf16[32,16,256]{2,1,0:T(8,128)(2,1)S(1)} collective-permute-done((bf16[32,16,256]{2,1,0:T(8,128)(2,1)}, bf16[32,16,256]{2,1,0:T(8,128)(2,1)S(1)}, u32[]{:S(2)}, u32[]{:S(2)}) %collective-permute-start.5) | collective-permute-done | bytes 262176 | tf_op jit(solution)/shard_map/ppermute | solution.py:400
  62.1 0.7 conditional.1
  62.1 0.7 copy.14
  63.0 1.0 %copy-done = bf16[64,16,256]{2,1,0:T(8,128)(2,1)S(1)} copy-done((bf16[64,16,256]{2,1,0:T(8,128)(2,1)S(1)}, bf16[64,16,256]{2,1,0:T(8,128)(2,1)}, u32[]{:S(2)}) %copy-start) | copy-done | bytes 524312
  64.1 10.5 %shard_map.122 = (bf16[1024,512]{1,0:T(8,128)(2,1)S(1)}, f32[32,512]{1,0:T(8,128)S(1)}, bf16[512,2048]{1,0:T(8,128)(2,1)S(1)}, bf16[2048,512]{1,0:T(8,128)(2,1)S(1)}, f32[1,2048]{1,0:T(1,128)S(1)}) custom-call(s32[1]{0:T(128)} %bitcast.core_ref, s32[1,128]{1,0:T(1,128)S(1)} %copy-done.4, s32[1]{0:T(128)} %get-tuple-element.44.crowded_ref, f32[4]{0:T(128)S(1)} %copy-done.6, ...), custom_call_target="tpu_custom_call" | custom-call | flops 1610612736 | bytes 4194304 | tf_op jit(solution)/shard_map/pallas_call | solution.py:482
  74.6 4.1 %fusion.7 = bf16[1024,2048]{1,0:T(8,128)(2,1)S(1)} fusion(f32[2048]{0:T(1024)S(1)} %bitcast.19, bf16[1024,512]{1,0:T(8,128)(2,1)S(1)} %get-tuple-element.73, bf16[512,2048]{1,0:T(8,128)(2,1)S(1)} %get-tuple-element.74), kind=kOutput, calls=%fused_computation.8 | convolution fusion | flops 2168455168 | bytes 7348224 | tf_op jit(solution)/shard_map/dot_general | solution.py:25
  78.8 1.2 %convert_reduce_fusion = f32[4,8,2048]{2,1,0:T(8,128)S(1)} fusion(bf16[4,2,8,16,2048]{4,3,2,1,0:T(8,128)(2,1)S(1)} %bitcast.20), kind=kLoop, calls=%fused_computation.9 | loop fusion | flops 4128768 | bytes 4456448 | tf_op jit(solution)/shard_map/reduce_sum | solution.py:368
  80.8 0.9 %collective-permute-done.15 = bf16[64,512]{1,0:T(8,128)(2,1)S(1)} collective-permute-done((bf16[64,512]{1,0:T(8,128)(2,1)S(1)}, bf16[64,512]{1,0:T(8,128)(2,1)S(1)}, u32[]{:S(2)}, u32[]{:S(2)}) %collective-permute-start.15) | collective-permute-done | bytes 65568 | tf_op jit(solution)/shard_map/ppermute | solution.py:397
  81.8 0.6 add.28
  (42 shorter events, 2.5 us)
Async XLA Ops:
  0.0 39.8 %copy-start.5 = (f32[4]{0:T(128)S(1)}, f32[4]{0:T(128)}, u32[]{:S(2)}) copy-start(f32[4]{0:T(128)} %scale_a_ref.1) | copy-start | bytes 52
  18.7 9.2 %collective-permute-start.2 = (bf16[32,16,256]{2,1,0:T(8,128)(2,1)}, bf16[32,16,256]{2,1,0:T(8,128)(2,1)S(1)}, u32[]{:S(2)}, u32[]{:S(2)}) collective-permute-start(bf16[32,16,256]{2,1,0:T(8,128)(2,1)} %get-tuple-element.46), channel_id=1, source_target_pairs={{0,2},{2,0},{4,6},{6,4},{8,10},{10,8},{12,14},{14,12},{1,3},{3,1},... | collective-permute-start | bytes 786440 | tf_op jit(solution)/shard_map/ppermute | solution.py:400
  19.3 9.5 %collective-permute-start.3 = (bf16[32,16,256]{2,1,0:T(8,128)(2,1)}, bf16[32,16,256]{2,1,0:T(8,128)(2,1)S(1)}, u32[]{:S(2)}, u32[]{:S(2)}) collective-permute-start(bf16[32,16,256]{2,1,0:T(8,128)(2,1)} %get-tuple-element.47), channel_id=1, source_target_pairs={{0,4},{2,6},{4,0},{6,2},{8,12},{10,14},{12,8},{14,10},{1,5},{3,7},... | collective-permute-start | bytes 786440 | tf_op jit(solution)/shard_map/ppermute | solution.py:400
  19.9 19.9 %collective-permute-start.4 = (bf16[32,16,256]{2,1,0:T(8,128)(2,1)}, bf16[32,16,256]{2,1,0:T(8,128)(2,1)S(1)}, u32[]{:S(2)}, u32[]{:S(2)}) collective-permute-start(bf16[32,16,256]{2,1,0:T(8,128)(2,1)} %get-tuple-element.48), channel_id=1, source_target_pairs={{0,6},{2,4},{4,2},{6,0},{8,14},{10,12},{12,10},{14,8},{1,7},{3,5},... | collective-permute-start | bytes 786440 | tf_op jit(solution)/shard_map/ppermute | solution.py:400
  22.3 34.6 %all-to-all-start.1 = ((bf16[8,16,16,256]{3,2,1,0:T(8,128)(2,1)}), bf16[8,16,16,256]{3,2,1,0:T(8,128)(2,1)}, u32[]{:S(2)}, u32[]{:S(2)}) async-start(bf16[8,16,16,256]{3,2,1,0:T(8,128)(2,1)} %get-tuple-element.63), calls=%async_computation.1 | async-start | bytes 2097152 | tf_op jit(solution)/shard_map/all_to_all | solution.py:438
  27.9 14.0 %copy-start.9 = (bf16[32,16,256]{2,1,0:T(8,128)(2,1)}, bf16[32,16,256]{2,1,0:T(8,128)(2,1)S(1)}, u32[]{:S(2)}) copy-start(bf16[32,16,256]{2,1,0:T(8,128)(2,1)S(1)} %collective-permute-done.2.refs_1_.refs_2_) | copy-start | bytes 786436
  28.8 13.1 %copy-start.10 = (bf16[32,16,256]{2,1,0:T(8,128)(2,1)}, bf16[32,16,256]{2,1,0:T(8,128)(2,1)S(1)}, u32[]{:S(2)}) copy-start(bf16[32,16,256]{2,1,0:T(8,128)(2,1)S(1)} %collective-permute-done.3.refs_2_.refs_3_) | copy-start | bytes 786436
  39.8 1.1 %collective-permute-start.12 = (f32[4]{0:T(128)S(1)}, f32[4]{0:T(128)S(1)}, u32[]{:S(2)}, u32[]{:S(2)}) collective-permute-start(f32[4]{0:T(128)S(1)} %copy-done.5), channel_id=1, source_target_pairs={{0,1},{1,0},{2,3},{3,2},{4,5},{5,4},{6,7},{7,6},{8,9},{9,8},{10,11... | collective-permute-start | bytes 56 | tf_op jit(solution)/shard_map/ppermute | solution.py:397
  39.8 4.3 %collective-permute-start.11 = (f32[1024]{0:T(1024)}, f32[1024]{0:T(1024)}, u32[]{:S(2)}, u32[]{:S(2)}) collective-permute-start(f32[1024]{0:T(1024)} %param.24), channel_id=1, source_target_pairs={{0,1},{1,0},{2,3},{3,2},{4,5},{5,4},{6,7},{7,6},{8,9},{9,8},{10,11... | collective-permute-start | bytes 12296 | tf_op jit(solution)/shard_map/ppermute | solution.py:397
  40.3 4.0 %collective-permute-start.6 = (bf16[512,256]{1,0:T(8,128)(2,1)}, bf16[512,256]{1,0:T(8,128)(2,1)}, u32[]{:S(2)}, u32[]{:S(2)}) collective-permute-start(bf16[512,256]{1,0:T(8,128)(2,1)} %refs_6_.1), channel_id=1, source_target_pairs={{0,1},{1,0},{2,3},{3,2},{4,5},{5,4},{6,7},{7,6},{8,9},{9,8},{10,11... | collective-permute-start | bytes 786440 | tf_op jit(solution)/shard_map/ppermute | solution.py:397
  40.4 19.8 %collective-permute-start.7 = (bf16[512,256]{1,0:T(8,128)(2,1)}, bf16[512,256]{1,0:T(8,128)(2,1)}, u32[]{:S(2)}, u32[]{:S(2)}) collective-permute-start(bf16[512,256]{1,0:T(8,128)(2,1)} %refs_8_.1), channel_id=1, source_target_pairs={{0,1},{1,0},{2,3},{3,2},{4,5},{5,4},{6,7},{7,6},{8,9},{9,8},{10,11... | collective-permute-start | bytes 786440 | tf_op jit(solution)/shard_map/ppermute | solution.py:397
  40.8 20.6 %collective-permute-start.9 = (bf16[512,1024]{1,0:T(8,128)(2,1)}, bf16[512,1024]{1,0:T(8,128)(2,1)}, u32[]{:S(2)}, u32[]{:S(2)}) collective-permute-start(bf16[512,1024]{1,0:T(8,128)(2,1)} %refs_12_.1), channel_id=1, source_target_pairs={{0,1},{1,0},{2,3},{3,2},{4,5},{5,4},{6,7},{7,6},{8,9},{9,8},{10,11... | collective-permute-start | bytes 3145736 | tf_op jit(solution)/shard_map/ppermute | solution.py:397
  41.5 20.0 %collective-permute-start.10 = (bf16[1024,512]{1,0:T(8,128)(2,1)}, bf16[1024,512]{1,0:T(8,128)(2,1)}, u32[]{:S(2)}, u32[]{:S(2)}) collective-permute-start(bf16[1024,512]{1,0:T(8,128)(2,1)} %refs_14_.1), channel_id=1, source_target_pairs={{0,1},{1,0},{2,3},{3,2},{4,5},{5,4},{6,7},{7,6},{8,9},{9,8},{10,11... | collective-permute-start | bytes 3145736 | tf_op jit(solution)/shard_map/ppermute | solution.py:397
  41.9 2.2 %copy-start.1 = (bf16[256,512]{1,0:T(8,128)(2,1)S(1)}, bf16[256,512]{1,0:T(8,128)(2,1)}, u32[]{:S(2)}) copy-start(bf16[256,512]{1,0:T(8,128)(2,1)} %refs_10_.1) | copy-start | bytes 786436
  41.9 21.1 %copy-start.2 = (f32[512]{0:T(512)S(1)}, f32[512]{0:T(512)}, u32[]{:S(2)}) copy-start(f32[512]{0:T(512)} %param.17) | copy-start | bytes 6148
  41.9 21.1 %copy-start.3 = (f32[512]{0:T(512)S(1)}, f32[512]{0:T(512)}, u32[]{:S(2)}) copy-start(f32[512]{0:T(512)} %param.22) | copy-start | bytes 6148
  41.9 21.1 %copy-start.4 = (s32[1,128]{1,0:T(1,128)S(1)}, s32[1,128]{1,0:T(1,128)}, u32[]{:S(2)}) copy-start(s32[1,128]{1,0:T(1,128)} %get-tuple-element.42.list_ref) | copy-start | bytes 1540
  41.9 21.1 %copy-start.6 = (f32[4]{0:T(128)S(1)}, f32[4]{0:T(128)}, u32[]{:S(2)}) copy-start(f32[4]{0:T(128)} %scale_a_ref.1) | copy-start | bytes 52
  42.0 21.1 %copy-start.8 = (f32[4]{0:T(128)S(1)}, f32[4]{0:T(128)}, u32[]{:S(2)}) copy-start(f32[4]{0:T(128)} %copy-done.7) | copy-start | bytes 52
  44.1 16.1 %collective-permute-start.8 = (bf16[256,512]{1,0:T(8,128)(2,1)S(1)}, bf16[256,512]{1,0:T(8,128)(2,1)S(1)}, u32[]{:S(2)}, u32[]{:S(2)}) collective-permute-start(bf16[256,512]{1,0:T(8,128)(2,1)S(1)} %copy-done.1), channel_id=1, source_target_pairs={{0,1},{1,0},{2,3},{3,2},{4,5},{5,4},{6,7},{7,6},{8,9},{9,8},{10,11... | collective-permute-start | bytes 786440 | tf_op jit(solution)/shard_map/ppermute | solution.py:397
  44.3 17.2 %collective-permute-start.5 = (bf16[32,16,256]{2,1,0:T(8,128)(2,1)}, bf16[32,16,256]{2,1,0:T(8,128)(2,1)S(1)}, u32[]{:S(2)}, u32[]{:S(2)}) collective-permute-start(bf16[32,16,256]{2,1,0:T(8,128)(2,1)} %get-tuple-element.49), channel_id=1, source_target_pairs={{0,8},{2,10},{4,12},{6,14},{8,0},{10,2},{12,4},{14,6},{1,9},{3,11}... | collective-permute-start | bytes 786440 | tf_op jit(solution)/shard_map/ppermute | solution.py:400
  60.1 2.9 %collective-permute-start.14 = (bf16[64,16,256]{2,1,0:T(8,128)(2,1)}, bf16[64,16,256]{2,1,0:T(8,128)(2,1)S(1)}, u32[]{:S(2)}, u32[]{:S(2)}) collective-permute-start(bf16[64,16,256]{2,1,0:T(8,128)(2,1)} %get-tuple-element.65), channel_id=1, source_target_pairs={{0,1},{1,0},{2,3},{3,2},{4,5},{5,4},{6,7},{7,6},{8,9},{9,8},{10,11... | collective-permute-start | bytes 1572872 | tf_op jit(solution)/shard_map/ppermute | solution.py:397
  61.4 1.5 %collective-permute-start.13 = (bf16[32,16,256]{2,1,0:T(8,128)(2,1)S(1)}, bf16[32,16,256]{2,1,0:T(8,128)(2,1)S(1)}, u32[]{:S(2)}, u32[]{:S(2)}) collective-permute-start(bf16[32,16,256]{2,1,0:T(8,128)(2,1)S(1)} %collective-permute-done.5.refs_0_), channel_id=1, source_target_pairs={{0,1},{1,0},{2,3},{3,2},{4,5},{5,4},{6,7},{7,6},{8,9},{9,8},{10,11... | collective-permute-start | bytes 786440 | tf_op jit(solution)/shard_map/ppermute | solution.py:397
  80.4 1.3 %collective-permute-start.15 = (bf16[64,512]{1,0:T(8,128)(2,1)S(1)}, bf16[64,512]{1,0:T(8,128)(2,1)S(1)}, u32[]{:S(2)}, u32[]{:S(2)}) collective-permute-start(bf16[64,512]{1,0:T(8,128)(2,1)S(1)} %shard_map.123), channel_id=1, source_target_pairs={{0,1},{1,0},{2,3},{3,2},{4,5},{5,4},{6,7},{7,6},{8,9},{9,8},{10,11... | collective-permute-start | bytes 196616 | tf_op jit(solution)/shard_map/ppermute | solution.py:397
  (3 other events, 3.8 us)

commit v6 on v5

--- a/solution.py
+++ b/solution.py
@@ -141,7 +141,7 @@
             return carry
 
         def pack_more(index, carry, chunk_ref=chunk_ref, at=at):
-            second_ref[at + index - plan.part] = chunk_ref[index]
+            second_ref[0, at + index - plan.part] = chunk_ref[index]
             return carry
 
         lax.fori_loop(0, fit, pack, 0)
@@ -191,7 +191,7 @@
     *refs,
 ):
     if plan.extra:
-        rest_held_refs, refs = refs[:4], refs[4:]
+        first_held_ref, far_first_held_ref, second_held_ref, *refs = refs
         *refs, rest_ref, rest_sems = refs
     own_held_ref, far_held_ref, *held_refs = refs[:14]
     normed_ref, mean_ref, in_ref, back_ref, bias_ref = refs[14:19]
@@ -216,6 +216,8 @@
     for load in token_loads:
         load.start()
     if plan.extra:
+        rest_held_refs = [first_held_ref, far_first_held_ref]
+        rest_held_refs += [second_held_ref.at[0], second_held_ref.at[1]]
         rest_loads = [
             pltpu.make_async_copy(
                 held, rest_ref.at[side, pl.ds(at * plan.part, plan.part)], rest_sems.at[index]
@@ -434,12 +436,13 @@
             in_specs=[smem, smem, vmem],
             out_specs=[vmem] * (plan.half + 1) + [smem],
         )(shard, incoming, image_tokens)
-        chunks = [chunks[0]] + [across(chunks[k], k) for k in range(1, plan.half)]
+        passed = [across(chunks[k], k) for k in reversed(range(1, plan.half))]
+        chunks = [chunks[0], *reversed(passed)]
         returned = lax.all_to_all(served, "shard", split_axis=0, concat_axis=0, tiled=True)
         returned = returned.reshape(-1, length, features)
         first, second = pl.pallas_call(
             functools.partial(relay_kernel, plan),
-            out_shape=[images(plan.part)] * 2,
+            out_shape=[images(plan.part), images(2, plan.part)],
             in_specs=[smem, smem] + [vmem] * plan.half,
             cost_estimate=pl.CostEstimate(
                 flops=2 * 10**11, bytes_accessed=2**20, transcendentals=0
@@ -459,6 +462,7 @@
             pltpu.VMEM((plan.slots, length, features), jnp.bfloat16),
             pltpu.SemaphoreType.DMA((len(sources),)),
         ],
+        compiler_params=limit(16),
     )(core, order, *sources)
     far = swap(other)
     rest = []
@@ -466,14 +470,12 @@
         first, second, swapped = lax.optimization_barrier((first, second, swapped))
         far_first = swap(first)
 
-        def fetch_second(part):
-            part = across(part, plan.half)
-            return part, swap(part)
-
-        second, far_second = lax.cond(
-            crowded[0] > 0, fetch_second, lambda part: (part, part), second
-        )
-        rest = [first, far_first, second, far_second]
+        def fetch_second(parts):
+            part = across(parts[0], plan.half)
+            return jnp.stack([part, swap(part)])
+
+        second = lax.cond(crowded[0] > 0, fetch_second, lambda parts: parts, second)
+        rest = [first, far_first, second]
     else:
         crowded = jnp.zeros((1,), jnp.int32)
     far_qk, far_value, far_out, far_in, far_back, far_bias, far_scale = swapped

time: 82.8 us -> 83.7 us (1.011)
  local copies, waits for them, and re-layouts: 2.37 us -> 3.55 us
  Pallas kernels: 21.3 us -> 20.2 us
    unnamed x24 -> x30, local copies, waits for them, and re-layouts: 1.66 us -> 3.55 us
    ppermute x4, waiting for transfers between devices: 14.5 us -> 13.2 us  [across(): lax.ppermute(values, 'shard', [(k, k ^ distance) for k in range(owner_cou...]
    pallas_call x1, Pallas kernels: 3.19 us -> 1.99 us  [on_device(): pl.pallas_call(functools.partial(pick_kernel, plan), out_shape=[images(pa...]
    ppermute x10, waiting for transfers between devices: 1.14 us -> 2.16 us  [swap(): return lax.ppermute(values, 'mp', [(0, 1), (1, 0)])]
  transfers between devices with their start and end apart: 15 -> 15, of which waited for: 7 -> 6; matrix products, arithmetic and copies ran while one was open for 1% -> 0% of each run, Pallas kernels for 6% -> 5%
where the time goes in v6:
time: 83.7 us; the launch traced here: 83.3 us
  waiting for transfers between devices  28.6 us (34%)
  Pallas kernels  20.2 us (24%)
  blocking collectives  13.8 us (16%)
  starting transfers between devices  10.3 us (12%)
  matrix products  4.14 us (5%)
  local copies, waits for them, and re-layouts  3.55 us (4%)
  other arithmetic  1.83 us (2%)
  between operations  0.88 us (1%)
    all_to_all x1, blocking collectives, on_device(): lax.all_to_all(wanted, 'shard', split_axis=0, concat_axis=0, tiled=True)  13.8 us
    ppermute x4, waiting for transfers between devices, across(): lax.ppermute(values, 'shard', [(k, k ^ distance) for k in range(owner_cou...  13.2 us
    all_to_all x1, waiting for transfers between devices, on_device(): lax.all_to_all(served, 'shard', split_axis=0, concat_axis=0, tiled=True)  13.2 us
    pallas_call x1, Pallas kernels, on_device(): pl.pallas_call(functools.partial(attention_kernel, plan, length, head_dim...  10.6 us
    all_to_all x1, starting transfers between devices, on_device(): lax.all_to_all(served, 'shard', split_axis=0, concat_axis=0, tiled=True)  4.24 us
    dot_general x1, matrix products, dot(): return jnp.dot(a, b, preferred_element_type=jnp.float32)  4.14 us
    ppermute x4, starting transfers between devices, across(): lax.ppermute(values, 'shard', [(k, k ^ distance) for k in range(owner_cou...  3.56 us
    unnamed x30, local copies, waits for them, and re-layouts  3.55 us
  transfers between devices with their start and end apart: 15, of which 6 were waited for; matrix products, arithmetic and copies ran while one was open for 0% of the time, Pallas kernels for 5%

profile of v6, /device:TPU:0, one launch (start us, length us, event | category | flops | bytes accessed | tf_op | source)
XLA Modules:
  0.0 83.3 jit_solution(671863858437348907)
XLA Ops:
  0.0 1.8 %shard_map.118 = (s32[8,1,36]{2,1,0:T(1,128)}, s32[1,128]{1,0:T(1,128)}) custom-call(s32[1]{0:T(128)} %bitcast.4.shard_ref, s32[2,64]{1,0:T(2,128)} %bitcast.27, s32[2,64]{1,0:T(2,128)} %bitcast.28), custom_call_target="tpu_custom_call" | custom-call | tf_op jit(solution)/shard_map/pallas_call | solution.py:414
  1.8 13.8 %all_to_all.10.incoming_ref = s32[8,1,36]{2,1,0:T(1,128)} all-to-all(s32[8,1,36]{2,1,0:T(1,128)} %get-tuple-element.44), channel_id=1, replica_groups=mesh['groups'=2,'shard'=8,'mp'=2] {'shard'}, dimensions={0} | all-to-all | bytes 2304 | tf_op jit(solution)/shard_map/all_to_all | solution.py:422
  15.6 3.2 %shard_map.119 = (bf16[32,16,256]{2,1,0:T(8,128)(2,1)}, bf16[32,16,256]{2,1,0:T(8,128)(2,1)}, bf16[32,16,256]{2,1,0:T(8,128)(2,1)}, bf16[32,16,256]{2,1,0:T(8,12...) custom-call(s32[1]{0:T(128)} %bitcast.4.shard_ref, s32[8,1,36]{2,1,0:T(1,128)} %all_to_all.10.incoming_ref, ...), custom_call_target="tpu_custom_call" | custom-call | tf_op jit(solution)/shard_map/pallas_call | solution.py:432
  18.7 0.6 collective-permute-start.2
  19.4 0.6 collective-permute-start.3
  19.9 2.4 %collective-permute-start.4 = (bf16[32,16,256]{2,1,0:T(8,128)(2,1)}, bf16[32,16,256]{2,1,0:T(8,128)(2,1)S(1)}, u32[]{:S(2)}, u32[]{:S(2)}) collective-permute-start(bf16[32,16,256]{2,1,0:T(8,128)(2,1)} %get-tuple-element.49), channel_id=1, source_target_pairs={{0,6},{2,4},{4,2},{6,0},{8,14},{10,12},{12,10},{14,8},{1,7},{3,5},... | collective-permute-start | bytes 786440 | tf_op jit(solution)/shard_map/ppermute | solution.py:402
  22.3 4.2 %all-to-all-start.1 = ((bf16[8,16,16,256]{3,2,1,0:T(8,128)(2,1)}), bf16[8,16,16,256]{3,2,1,0:T(8,128)(2,1)}, u32[]{:S(2)}, u32[]{:S(2)}) async-start(bf16[8,16,16,256]{3,2,1,0:T(8,128)(2,1)} %get-tuple-element.62), calls=%async_computation.1 | async-start | bytes 2097152 | tf_op jit(solution)/shard_map/all_to_all | solution.py:441
  26.5 1.4 %collective-permute-done.2.refs_1_.refs_2_ = bf16[32,16,256]{2,1,0:T(8,128)(2,1)S(1)} collective-permute-done((bf16[32,16,256]{2,1,0:T(8,128)(2,1)}, bf16[32,16,256]{2,1,0:T(8,128)(2,1)S(1)}, u32[]{:S(2)}, u32[]{:S(2)}) %collective-permute-start.2) | collective-permute-done | bytes 262176 | tf_op jit(solution)/shard_map/ppermute | solution.py:402
  28.0 0.8 %collective-permute-done.3.refs_2_.refs_3_ = bf16[32,16,256]{2,1,0:T(8,128)(2,1)S(1)} collective-permute-done((bf16[32,16,256]{2,1,0:T(8,128)(2,1)}, bf16[32,16,256]{2,1,0:T(8,128)(2,1)S(1)}, u32[]{:S(2)}, u32[]{:S(2)}) %collective-permute-start.3) | collective-permute-done | bytes 262176 | tf_op jit(solution)/shard_map/ppermute | solution.py:402
  28.8 11.0 %collective-permute-done.4.refs_3_.refs_4_ = bf16[32,16,256]{2,1,0:T(8,128)(2,1)S(1)} collective-permute-done((bf16[32,16,256]{2,1,0:T(8,128)(2,1)}, bf16[32,16,256]{2,1,0:T(8,128)(2,1)S(1)}, u32[]{:S(2)}, u32[]{:S(2)}) %collective-permute-start.4) | collective-permute-done | bytes 262176 | tf_op jit(solution)/shard_map/ppermute | solution.py:402
  41.4 2.1 %shard_map.120 = (bf16[32,16,256]{2,1,0:T(8,128)(2,1)}, bf16[2,32,16,256]{3,2,1,0:T(8,128)(2,1)S(1)}) custom-call(s32[1]{0:T(128)} %bitcast.4.shard_ref, s32[8,1,36]{2,1,0:T(1,128)} %all_to_all.10.incoming_ref, bf16[32,16,256]{2,1,0:T(8,128)(2,1)} %get-tuple-element.46.refs_0_.refs_1_, bf16[32,16,256]{2,1,0:T(8,128)(2,1)} %copy-done.2, ...), custom_call_target="tpu_custom_call" | custom-call | flops 199999995904 | bytes 1048576 | tf_op jit(solution)/shard_map/pallas_call | solution.py:443
  43.7 13.2 %all-to-all-done.1 = bf16[8,16,16,256]{3,2,1,0:T(8,128)(2,1)} async-done(((bf16[8,16,16,256]{3,2,1,0:T(8,128)(2,1)}), bf16[8,16,16,256]{3,2,1,0:T(8,128)(2,1)}, u32[]{:S(2)}, u32[]{:S(2)}) %all-to-all-start.1) | async-done | bytes 1048608 | tf_op jit(solution)/shard_map/all_to_all | solution.py:441
  57.0 0.9 %copy-done.3 = bf16[32,16,256]{2,1,0:T(8,128)(2,1)S(1)} copy-done((bf16[32,16,256]{2,1,0:T(8,128)(2,1)S(1)}, bf16[32,16,256]{2,1,0:T(8,128)(2,1)}, u32[]{:S(2)}) %copy-start.3) | copy-done | bytes 262168
  57.9 0.9 %copy-done.5 = bf16[32,16,256]{2,1,0:T(8,128)(2,1)S(1)} copy-done((bf16[32,16,256]{2,1,0:T(8,128)(2,1)S(1)}, bf16[32,16,256]{2,1,0:T(8,128)(2,1)}, u32[]{:S(2)}) %copy-start.5) | copy-done | bytes 262168
  58.9 0.9 %copy-done.7 = bf16[32,16,256]{2,1,0:T(8,128)(2,1)S(1)} copy-done((bf16[32,16,256]{2,1,0:T(8,128)(2,1)S(1)}, bf16[32,16,256]{2,1,0:T(8,128)(2,1)}, u32[]{:S(2)}) %copy-start.7) | copy-done | bytes 262168
  59.8 2.0 %shard_map.121 = (bf16[64,16,256]{2,1,0:T(8,128)(2,1)S(1)}, bf16[64,16,256]{2,1,0:T(8,128)(2,1)S(1)}) custom-call(s32[1]{0:T(128)} %bitcast.3.core_ref, s32[1,128]{1,0:T(1,128)S(1)} %copy-done.10, bf16[128,16,256]{2,1,0:T(8,128)(2,1)} %bitcast.10.refs_0_, bf16[32,16,256]{2,1,0:T(8,128)(2,1)S(1)} %copy-done.1, bf16[32,16,256]{2,1,0:T(8,128)(2,1)S(1)} %copy-done.3, ...), custom_call_target="tpu_custom_call" | custom-call | tf_op jit(solution)/shard_map/pallas_call | solution.py:457
  61.9 0.5 collective-permute-start.13
  63.2 1.0 %collective-permute-done.13.refs_1_ = bf16[32,16,256]{2,1,0:T(8,128)(2,1)S(1)} collective-permute-done((bf16[32,16,256]{2,1,0:T(8,128)(2,1)S(1)}, bf16[32,16,256]{2,1,0:T(8,128)(2,1)S(1)}, u32[]{:S(2)}, u32[]{:S(2)}) %collective-permute-start.13) | collective-permute-done | bytes 262176 | tf_op jit(solution)/shard_map/ppermute | solution.py:399
  64.2 0.6 copy-done.14
  64.9 10.6 %shard_map.122 = (bf16[1024,512]{1,0:T(8,128)(2,1)S(1)}, f32[32,512]{1,0:T(8,128)S(1)}, bf16[512,2048]{1,0:T(8,128)(2,1)S(1)}, bf16[2048,512]{1,0:T(8,128)(2,1)S(1)}, f32[1,2048]{1,0:T(1,128)S(1)}) custom-call(s32[1]{0:T(128)} %bitcast.3.core_ref, s32[1,128]{1,0:T(1,128)S(1)} %copy-done.10, s32[1]{0:T(128)} %get-tuple-element.45.crowded_ref, ...), custom_call_target="tpu_custom_call" | custom-call | flops 1610612736 | bytes 4194304 | tf_op jit(solution)/shard_map/pallas_call | solution.py:484
  75.5 4.1 %fusion.7 = bf16[1024,2048]{1,0:T(8,128)(2,1)S(1)} fusion(f32[2048]{0:T(1024)S(1)} %bitcast.23, bf16[1024,512]{1,0:T(8,128)(2,1)S(1)} %get-tuple-element.72, bf16[512,2048]{1,0:T(8,128)(2,1)S(1)} %get-tuple-element.73), kind=kOutput, calls=%fused_computation.10 | convolution fusion | flops 2168455168 | bytes 7348224 | tf_op jit(solution)/shard_map/dot_general | solution.py:25
  79.6 1.2 %convert_reduce_fusion = f32[4,8,2048]{2,1,0:T(8,128)S(1)} fusion(bf16[4,2,8,16,2048]{4,3,2,1,0:T(8,128)(2,1)S(1)} %bitcast.24), kind=kLoop, calls=%fused_computation.11 | loop fusion | flops 4128768 | bytes 4456448 | tf_op jit(solution)/shard_map/reduce_sum | solution.py:370
  81.5 1.1 %collective-permute-done.15 = bf16[64,512]{1,0:T(8,128)(2,1)S(1)} collective-permute-done((bf16[64,512]{1,0:T(8,128)(2,1)S(1)}, bf16[64,512]{1,0:T(8,128)(2,1)S(1)}, u32[]{:S(2)}, u32[]{:S(2)}) %collective-permute-start.15) | collective-permute-done | bytes 65568 | tf_op jit(solution)/shard_map/ppermute | solution.py:399
  82.6 0.6 add.28
  (47 shorter events, 2.5 us)
Async XLA Ops:
  0.0 39.8 %copy-start.11 = (f32[4]{0:T(128)S(1)}, f32[4]{0:T(128)}, u32[]{:S(2)}) copy-start(f32[4]{0:T(128)} %scale_a_ref.1) | copy-start | bytes 52
  18.7 9.2 %collective-permute-start.2 = (bf16[32,16,256]{2,1,0:T(8,128)(2,1)}, bf16[32,16,256]{2,1,0:T(8,128)(2,1)S(1)}, u32[]{:S(2)}, u32[]{:S(2)}) collective-permute-start(bf16[32,16,256]{2,1,0:T(8,128)(2,1)} %get-tuple-element.47), channel_id=1, source_target_pairs={{0,2},{2,0},{4,6},{6,4},{8,10},{10,8},{12,14},{14,12},{1,3},{3,1},... | collective-permute-start | bytes 786440 | tf_op jit(solution)/shard_map/ppermute | solution.py:402
  19.4 9.5 %collective-permute-start.3 = (bf16[32,16,256]{2,1,0:T(8,128)(2,1)}, bf16[32,16,256]{2,1,0:T(8,128)(2,1)S(1)}, u32[]{:S(2)}, u32[]{:S(2)}) collective-permute-start(bf16[32,16,256]{2,1,0:T(8,128)(2,1)} %get-tuple-element.48), channel_id=1, source_target_pairs={{0,4},{2,6},{4,0},{6,2},{8,12},{10,14},{12,8},{14,10},{1,5},{3,7},... | collective-permute-start | bytes 786440 | tf_op jit(solution)/shard_map/ppermute | solution.py:402
  19.9 19.9 %collective-permute-start.4 = (bf16[32,16,256]{2,1,0:T(8,128)(2,1)}, bf16[32,16,256]{2,1,0:T(8,128)(2,1)S(1)}, u32[]{:S(2)}, u32[]{:S(2)}) collective-permute-start(bf16[32,16,256]{2,1,0:T(8,128)(2,1)} %get-tuple-element.49), channel_id=1, source_target_pairs={{0,6},{2,4},{4,2},{6,0},{8,14},{10,12},{12,10},{14,8},{1,7},{3,5},... | collective-permute-start | bytes 786440 | tf_op jit(solution)/shard_map/ppermute | solution.py:402
  22.3 34.7 %all-to-all-start.1 = ((bf16[8,16,16,256]{3,2,1,0:T(8,128)(2,1)}), bf16[8,16,16,256]{3,2,1,0:T(8,128)(2,1)}, u32[]{:S(2)}, u32[]{:S(2)}) async-start(bf16[8,16,16,256]{3,2,1,0:T(8,128)(2,1)} %get-tuple-element.62), calls=%async_computation.1 | async-start | bytes 2097152 | tf_op jit(solution)/shard_map/all_to_all | solution.py:441
  28.0 13.4 %copy-start.2 = (bf16[32,16,256]{2,1,0:T(8,128)(2,1)}, bf16[32,16,256]{2,1,0:T(8,128)(2,1)S(1)}, u32[]{:S(2)}) copy-start(bf16[32,16,256]{2,1,0:T(8,128)(2,1)S(1)} %collective-permute-done.2.refs_1_.refs_2_) | copy-start | bytes 786436
  28.8 12.5 %copy-start.4 = (bf16[32,16,256]{2,1,0:T(8,128)(2,1)}, bf16[32,16,256]{2,1,0:T(8,128)(2,1)S(1)}, u32[]{:S(2)}) copy-start(bf16[32,16,256]{2,1,0:T(8,128)(2,1)S(1)} %collective-permute-done.3.refs_2_.refs_3_) | copy-start | bytes 786436
  39.8 1.1 %collective-permute-start.12 = (f32[4]{0:T(128)S(1)}, f32[4]{0:T(128)S(1)}, u32[]{:S(2)}, u32[]{:S(2)}) collective-permute-start(f32[4]{0:T(128)S(1)} %copy-done.11), channel_id=1, source_target_pairs={{0,1},{1,0},{2,3},{3,2},{4,5},{5,4},{6,7},{7,6},{8,9},{9,8},{10,11... | collective-permute-start | bytes 56 | tf_op jit(solution)/shard_map/ppermute | solution.py:399
  39.8 3.7 %collective-permute-start.11 = (f32[1024]{0:T(1024)}, f32[1024]{0:T(1024)}, u32[]{:S(2)}, u32[]{:S(2)}) collective-permute-start(f32[1024]{0:T(1024)} %param.24), channel_id=1, source_target_pairs={{0,1},{1,0},{2,3},{3,2},{4,5},{5,4},{6,7},{7,6},{8,9},{9,8},{10,11... | collective-permute-start | bytes 12296 | tf_op jit(solution)/shard_map/ppermute | solution.py:399
  40.3 3.4 %collective-permute-start.6 = (bf16[512,256]{1,0:T(8,128)(2,1)}, bf16[512,256]{1,0:T(8,128)(2,1)}, u32[]{:S(2)}, u32[]{:S(2)}) collective-permute-start(bf16[512,256]{1,0:T(8,128)(2,1)} %refs_5_.1), channel_id=1, source_target_pairs={{0,1},{1,0},{2,3},{3,2},{4,5},{5,4},{6,7},{7,6},{8,9},{9,8},{10,11... | collective-permute-start | bytes 786440 | tf_op jit(solution)/shard_map/ppermute | solution.py:399
  40.4 21.4 %collective-permute-start.7 = (bf16[512,256]{1,0:T(8,128)(2,1)}, bf16[512,256]{1,0:T(8,128)(2,1)}, u32[]{:S(2)}, u32[]{:S(2)}) collective-permute-start(bf16[512,256]{1,0:T(8,128)(2,1)} %refs_7_.1), channel_id=1, source_target_pairs={{0,1},{1,0},{2,3},{3,2},{4,5},{5,4},{6,7},{7,6},{8,9},{9,8},{10,11... | collective-permute-start | bytes 786440 | tf_op jit(solution)/shard_map/ppermute | solution.py:399
  40.8 21.1 %collective-permute-start.9 = (bf16[512,1024]{1,0:T(8,128)(2,1)}, bf16[512,1024]{1,0:T(8,128)(2,1)}, u32[]{:S(2)}, u32[]{:S(2)}) collective-permute-start(bf16[512,1024]{1,0:T(8,128)(2,1)} %refs_11_.1), channel_id=1, source_target_pairs={{0,1},{1,0},{2,3},{3,2},{4,5},{5,4},{6,7},{7,6},{8,9},{9,8},{10,11... | collective-permute-start | bytes 3145736 | tf_op jit(solution)/shard_map/ppermute | solution.py:399
  40.9 2.6 %copy-start.13 = (f32[4]{0:T(128)}, f32[4]{0:T(128)S(1)}, u32[]{:S(2)}) copy-start(f32[4]{0:T(128)S(1)} %collective-permute-done.12.scale_b_ref) | copy-start | bytes 52
  40.9 21.0 %collective-permute-start.10 = (bf16[1024,512]{1,0:T(8,128)(2,1)}, bf16[1024,512]{1,0:T(8,128)(2,1)}, u32[]{:S(2)}, u32[]{:S(2)}) collective-permute-start(bf16[1024,512]{1,0:T(8,128)(2,1)} %refs_13_.1), channel_id=1, source_target_pairs={{0,1},{1,0},{2,3},{3,2},{4,5},{5,4},{6,7},{7,6},{8,9},{9,8},{10,11... | collective-permute-start | bytes 3145736 | tf_op jit(solution)/shard_map/ppermute | solution.py:399
  41.4 15.6 %copy-start.1 = (bf16[32,16,256]{2,1,0:T(8,128)(2,1)S(1)}, bf16[32,16,256]{2,1,0:T(8,128)(2,1)}, u32[]{:S(2)}) copy-start(bf16[32,16,256]{2,1,0:T(8,128)(2,1)} %get-tuple-element.46.refs_0_.refs_1_) | copy-start | bytes 786436
  41.4 15.6 %copy-start.10 = (s32[1,128]{1,0:T(1,128)S(1)}, s32[1,128]{1,0:T(1,128)}, u32[]{:S(2)}) copy-start(s32[1,128]{1,0:T(1,128)} %get-tuple-element.43.list_ref) | copy-start | bytes 1540
  41.4 22.8 %copy-start.8 = (f32[512]{0:T(512)S(1)}, f32[512]{0:T(512)}, u32[]{:S(2)}) copy-start(f32[512]{0:T(512)} %param.17) | copy-start | bytes 6148
  41.4 22.8 %copy-start.9 = (f32[512]{0:T(512)S(1)}, f32[512]{0:T(512)}, u32[]{:S(2)}) copy-start(f32[512]{0:T(512)} %param.22) | copy-start | bytes 6148
  41.4 22.8 %copy-start.12 = (f32[4]{0:T(128)S(1)}, f32[4]{0:T(128)}, u32[]{:S(2)}) copy-start(f32[4]{0:T(128)} %scale_a_ref.1) | copy-start | bytes 52
  43.6 18.4 %collective-permute-start.8 = (bf16[256,512]{1,0:T(8,128)(2,1)S(1)}, bf16[256,512]{1,0:T(8,128)(2,1)S(1)}, u32[]{:S(2)}, u32[]{:S(2)}) collective-permute-start(bf16[256,512]{1,0:T(8,128)(2,1)S(1)} %copy-done), channel_id=1, source_target_pairs={{0,1},{1,0},{2,3},{3,2},{4,5},{5,4},{6,7},{7,6},{8,9},{9,8},{10,11... | collective-permute-start | bytes 786440 | tf_op jit(solution)/shard_map/ppermute | solution.py:399
  43.7 18.2 %collective-permute-start.5 = (bf16[32,16,256]{2,1,0:T(8,128)(2,1)}, bf16[32,16,256]{2,1,0:T(8,128)(2,1)S(1)}, u32[]{:S(2)}, u32[]{:S(2)}) collective-permute-start(bf16[32,16,256]{2,1,0:T(8,128)(2,1)} %get-tuple-element.50), channel_id=1, source_target_pairs={{0,8},{2,10},{4,12},{6,14},{8,0},{10,2},{12,4},{14,6},{1,9},{3,11}... | collective-permute-start | bytes 786440 | tf_op jit(solution)/shard_map/ppermute | solution.py:402
  61.8 2.4 %collective-permute-start.14 = (bf16[64,16,256]{2,1,0:T(8,128)(2,1)S(1)}, bf16[64,16,256]{2,1,0:T(8,128)(2,1)S(1)}, u32[]{:S(2)}, u32[]{:S(2)}) collective-permute-start(bf16[64,16,256]{2,1,0:T(8,128)(2,1)S(1)} %get-tuple-element.64), channel_id=1, source_target_pairs={{0,1},{1,0},{2,3},{3,2},{4,5},{5,4},{6,7},{7,6},{8,9},{9,8},{10,11... | collective-permute-start | bytes 1572872 | tf_op jit(solution)/shard_map/ppermute | solution.py:399
  61.9 2.2 %collective-permute-start.13 = (bf16[32,16,256]{2,1,0:T(8,128)(2,1)S(1)}, bf16[32,16,256]{2,1,0:T(8,128)(2,1)S(1)}, u32[]{:S(2)}, u32[]{:S(2)}) collective-permute-start(bf16[32,16,256]{2,1,0:T(8,128)(2,1)S(1)} %collective-permute-done.5.refs_0_), channel_id=1, source_target_pairs={{0,1},{1,0},{2,3},{3,2},{4,5},{5,4},{6,7},{7,6},{8,9},{9,8},{10,11... | collective-permute-start | bytes 786440 | tf_op jit(solution)/shard_map/ppermute | solution.py:399
  81.3 1.3 %collective-permute-start.15 = (bf16[64,512]{1,0:T(8,128)(2,1)S(1)}, bf16[64,512]{1,0:T(8,128)(2,1)S(1)}, u32[]{:S(2)}, u32[]{:S(2)}) collective-permute-start(bf16[64,512]{1,0:T(8,128)(2,1)S(1)} %shard_map.123), channel_id=1, source_target_pairs={{0,1},{1,0},{2,3},{3,2},{4,5},{5,4},{6,7},{7,6},{8,9},{9,8},{10,11... | collective-permute-start | bytes 196616 | tf_op jit(solution)/shard_map/ppermute | solution.py:399
  (6 other events, 7.3 us)

commit v7 on v6

--- a/solution.py
+++ b/solution.py
@@ -239,7 +239,6 @@
     half = BLOCK * length
     rows = 2 * half
     blocks = tokens_ref.shape[1] // (2 * BLOCK)
-    long = 2 * rows
     pair_dim = 2 * head_dim
     scale_refs = (scale_a_ref, scale_b_ref)
     per_core = wide // head_dim
@@ -250,7 +249,7 @@
     )
 
     def span(step, size):
-        return pl.ds(pl.multiple_of(step * size, size), size)
+        return pl.ds(step * size, size)
 
     def split(values):
         zero = jnp.zeros_like(values)
@@ -260,20 +259,19 @@
 
     ones = split(jnp.ones((half, pair_dim), jnp.bfloat16))
 
-    def start_block(step, carry):
+    def begin(step):
         images = pl.ds(step * 2 * BLOCK, 2 * BLOCK)
         tokens = jnp.concatenate(
             [tokens_ref[k, images].reshape(rows, -1).astype(jnp.float32) for k in range(2)], axis=1
         )
         hidden_ref[span(step, rows), :] = tokens
         normed_ref[span(step, rows), :] = norm_rows(tokens, gain_attn_ref[...]).astype(jnp.bfloat16)
-        return carry
-
-    def project(step, carry):
-        here = span(step // 4, long)
-        cut = span(step % 4, 2 * width // 4)
-        heads_ref[here, cut] = dot(normed_ref[here, :], qkv_ref[:, cut]).astype(jnp.bfloat16)
-        return carry
+
+    def project(step):
+        here = span(step, rows)
+        for index in range(4):
+            cut = span(index, wide)
+            heads_ref[here, cut] = dot(normed_ref[here, :], qkv_ref[:, cut]).astype(jnp.bfloat16)
 
     def weigh(scores, factor):
         scores = jnp.where(same, scores, -1e30)
@@ -289,7 +287,7 @@
         inverse = inverse * (2.0 - total * inverse)
         return (mixed[:, :pair_dim] * inverse).astype(jnp.bfloat16)
 
-    def attend(step, carry):
+    def attend(step):
         for index in range(width // pair_dim):
             factors = [scale_refs[k // per_core][k % per_core] for k in (2 * index, 2 * index + 1)]
             factors = [factor * (LOG2E / head_dim**0.5) for factor in factors]
@@ -300,22 +298,20 @@
             value = [heads_ref[side, beyond] for side in sides]
             for k in range(2):
                 mixed_ref[sides[k], cut] = mix(query[k], query[1 - k], value[1 - k], factors)
-        return carry
-
-    def join(step, carry):
-        here = span(step // 2, long)
-        cut = span(step % 2, width // 2)
-        hidden_ref[here, cut] += dot(mixed_ref[here, :], out_ref[:, cut])
-        return carry
-
-    def middle_block(step, carry):
+
+    def join(step):
+        here = span(step, rows)
+        for index in range(2):
+            cut = span(index, wide)
+            hidden_ref[here, cut] += dot(mixed_ref[here, :], out_ref[:, cut])
+
+    def middle(step):
         here = span(step, rows)
         hidden = hidden_ref[here, :]
         mean_ref[span(step, BLOCK), :] = jnp.sum(
             hidden.reshape(2, BLOCK, length, -1), axis=(0, 2)
         )
         normed_ref[here, :] = norm_rows(hidden, gain_mlp_ref[...]).astype(jnp.bfloat16)
-        return carry
 
     for load in token_loads:
         load.wait()
@@ -339,15 +335,17 @@
             return carry
 
         lax.fori_loop(0, tokens_ref.shape[1], put, 0, unroll=4)
-    lax.fori_loop(0, blocks, start_block, 0)
-    for load in loads[:4]:
-        load.wait()
-    lax.fori_loop(0, blocks // 2 * 4, project, 0)
-    lax.fori_loop(0, blocks, attend, 0)
-    for load in loads[4:]:
-        load.wait()
-    lax.fori_loop(0, blocks // 2 * 2, join, 0)
-    lax.fori_loop(0, blocks, middle_block, 0)
+    stages = (begin, project, attend, join, middle)
+    for turn in range(blocks + len(stages) - 1):
+        if turn == 1:
+            for load in loads[:4]:
+                load.wait()
+        if turn == 3:
+            for load in loads[4:]:
+                load.wait()
+        for index, stage in enumerate(stages):
+            if 0 <= turn - index < blocks:
+                stage(turn - index)
 
 
 def back_kernel(length, core_ref, mean_ref, pooled_ref, back_ref, result_ref):
@@ -444,6 +442,7 @@
             functools.partial(relay_kernel, plan),
             out_shape=[images(plan.part), images(2, plan.part)],
             in_specs=[smem, smem] + [vmem] * plan.half,
+            compiler_params=limit(16),
             cost_estimate=pl.CostEstimate(
                 flops=2 * 10**11, bytes_accessed=2**20, transcendentals=0
             ),

time: 83.7 us -> 78.6 us (0.939)
  Pallas kernels: 20.2 us -> 15.8 us
  waiting for transfers between devices: 28.6 us -> 30.7 us
  local copies, waits for them, and re-layouts: 3.55 us -> 1.62 us
    pallas_call x1, Pallas kernels: 10.6 us -> 6.77 us  [on_device(): pl.pallas_call(functools.partial(attention_kernel, plan, length, head_dim...]
    ppermute x4, waiting for transfers between devices: 13.2 us -> 15.6 us  [across(): lax.ppermute(values, 'shard', [(k, k ^ distance) for k in range(owner_cou...]
    unnamed x30 -> x22, local copies, waits for them, and re-layouts: 3.55 us -> 1.62 us
  transfers between devices with their start and end apart: 15 -> 15, of which waited for: 6 -> 8; matrix products, arithmetic and copies ran while one was open for 0% -> 0% of each run, Pallas kernels for 5% -> 5%
where the time goes in v7:
time: 78.6 us; the launch traced here: 78.3 us
  waiting for transfers between devices  30.7 us (39%)
  Pallas kernels  15.8 us (20%)
  blocking collectives  13.8 us (18%)
  starting transfers between devices  9.66 us (12%)
  matrix products  4.13 us (5%)
  other arithmetic  1.83 us (2%)
  local copies, waits for them, and re-layouts  1.62 us (2%)
    ppermute x4, waiting for transfers between devices, across(): lax.ppermute(values, 'shard', [(k, k ^ distance) for k in range(owner_cou...  15.6 us
    all_to_all x1, blocking collectives, on_device(): lax.all_to_all(wanted, 'shard', split_axis=0, concat_axis=0, tiled=True)  13.8 us
    all_to_all x1, waiting for transfers between devices, on_device(): lax.all_to_all(served, 'shard', split_axis=0, concat_axis=0, tiled=True)  12.9 us
    pallas_call x1, Pallas kernels, on_device(): pl.pallas_call(functools.partial(attention_kernel, plan, length, head_dim...  6.77 us
    all_to_all x1, starting transfers between devices, on_device(): lax.all_to_all(served, 'shard', split_axis=0, concat_axis=0, tiled=True)  4.25 us
    dot_general x1, matrix products, dot(): return jnp.dot(a, b, preferred_element_type=jnp.float32)  4.13 us
    ppermute x4, starting transfers between devices, across(): lax.ppermute(values, 'shard', [(k, k ^ distance) for k in range(owner_cou...  3.56 us
    pallas_call x1, Pallas kernels, on_device(): pl.pallas_call(functools.partial(serve_kernel, plan), out_shape=[images(2...  3.22 us
  transfers between devices with their start and end apart: 15, of which 8 were waited for; matrix products, arithmetic and copies ran while one was open for 0% of the time, Pallas kernels for 5%

profile of v7, /device:TPU:0, one launch (start us, length us, event | category | flops | bytes accessed | tf_op | source)
XLA Modules:
  0.0 78.3 jit_solution(10148841440384292102)
XLA Ops:
  0.0 1.8 %shard_map.118 = (s32[8,1,36]{2,1,0:T(1,128)}, s32[1,128]{1,0:T(1,128)}) custom-call(s32[1]{0:T(128)} %bitcast.4.shard_ref, s32[2,64]{1,0:T(2,128)} %bitcast.27, s32[2,64]{1,0:T(2,128)} %bitcast.28), custom_call_target="tpu_custom_call" | custom-call | tf_op jit(solution)/shard_map/pallas_call | solution.py:412
  1.8 13.8 %all_to_all.10.incoming_ref = s32[8,1,36]{2,1,0:T(1,128)} all-to-all(s32[8,1,36]{2,1,0:T(1,128)} %get-tuple-element.44), channel_id=1, replica_groups=mesh['groups'=2,'shard'=8,'mp'=2] {'shard'}, dimensions={0} | all-to-all | bytes 2304 | tf_op jit(solution)/shard_map/all_to_all | solution.py:420
  15.6 3.2 %shard_map.119 = (bf16[32,16,256]{2,1,0:T(8,128)(2,1)}, bf16[32,16,256]{2,1,0:T(8,128)(2,1)}, bf16[32,16,256]{2,1,0:T(8,128)(2,1)}, bf16[32,16,256]{2,1,0:T(8,12...) custom-call(s32[1]{0:T(128)} %bitcast.4.shard_ref, s32[8,1,36]{2,1,0:T(1,128)} %all_to_all.10.incoming_ref, ...), custom_call_target="tpu_custom_call" | custom-call | tf_op jit(solution)/shard_map/pallas_call | solution.py:430
  18.8 0.6 collective-permute-start.2
  19.4 0.6 collective-permute-start.3
  20.0 2.4 %collective-permute-start.4 = (bf16[32,16,256]{2,1,0:T(8,128)(2,1)}, bf16[32,16,256]{2,1,0:T(8,128)(2,1)S(1)}, u32[]{:S(2)}, u32[]{:S(2)}) collective-permute-start(bf16[32,16,256]{2,1,0:T(8,128)(2,1)} %get-tuple-element.49), channel_id=1, source_target_pairs={{0,6},{2,4},{4,2},{6,0},{8,14},{10,12},{12,10},{14,8},{1,7},{3,5},... | collective-permute-start | bytes 786440 | tf_op jit(solution)/shard_map/ppermute | solution.py:400
  22.3 4.2 %all-to-all-start.1 = ((bf16[8,16,16,256]{3,2,1,0:T(8,128)(2,1)}), bf16[8,16,16,256]{3,2,1,0:T(8,128)(2,1)}, u32[]{:S(2)}, u32[]{:S(2)}) async-start(bf16[8,16,16,256]{3,2,1,0:T(8,128)(2,1)} %get-tuple-element.62), calls=%async_computation.1 | async-start | bytes 2097152 | tf_op jit(solution)/shard_map/all_to_all | solution.py:439
  26.6 1.4 %collective-permute-done.2.refs_1_.refs_2_ = bf16[32,16,256]{2,1,0:T(8,128)(2,1)S(1)} collective-permute-done((bf16[32,16,256]{2,1,0:T(8,128)(2,1)}, bf16[32,16,256]{2,1,0:T(8,128)(2,1)S(1)}, u32[]{:S(2)}, u32[]{:S(2)}) %collective-permute-start.2) | collective-permute-done | bytes 262176 | tf_op jit(solution)/shard_map/ppermute | solution.py:400
  28.0 0.9 %collective-permute-done.3.refs_2_.refs_3_ = bf16[32,16,256]{2,1,0:T(8,128)(2,1)S(1)} collective-permute-done((bf16[32,16,256]{2,1,0:T(8,128)(2,1)}, bf16[32,16,256]{2,1,0:T(8,128)(2,1)S(1)}, u32[]{:S(2)}, u32[]{:S(2)}) %collective-permute-start.3) | collective-permute-done | bytes 262176 | tf_op jit(solution)/shard_map/ppermute | solution.py:400
  28.9 11.0 %collective-permute-done.4.refs_3_.refs_4_ = bf16[32,16,256]{2,1,0:T(8,128)(2,1)S(1)} collective-permute-done((bf16[32,16,256]{2,1,0:T(8,128)(2,1)}, bf16[32,16,256]{2,1,0:T(8,128)(2,1)S(1)}, u32[]{:S(2)}, u32[]{:S(2)}) %collective-permute-start.4) | collective-permute-done | bytes 262176 | tf_op jit(solution)/shard_map/ppermute | solution.py:400
  39.8 0.5 collective-permute-start.11
  40.3 0.5 collective-permute-start.7
  41.4 0.9 %copy-done.1 = bf16[32,16,256]{2,1,0:T(8,128)(2,1)S(1)} copy-done((bf16[32,16,256]{2,1,0:T(8,128)(2,1)S(1)}, bf16[32,16,256]{2,1,0:T(8,128)(2,1)}, u32[]{:S(2)}) %copy-start.1) | copy-done | bytes 262168
  42.4 1.6 %shard_map.120 = (bf16[32,16,256]{2,1,0:T(8,128)(2,1)S(1)}, bf16[2,32,16,256]{3,2,1,0:T(8,128)(2,1)}) custom-call(s32[1]{0:T(128)} %bitcast.4.shard_ref, s32[8,1,36]{2,1,0:T(1,128)S(1)} %copy-done.3, bf16[32,16,256]{2,1,0:T(8,128)(2,1)S(1)} %copy-done.1, bf16[32,16,256]{2,1,0:T(8,128)(2,1)S(1)} %collective-permute-done.2.refs_1_.refs_2_, ...), custom_call_target="tpu_custom_call" | custom-call | flops 199999995904 | bytes 1048576 | tf_op jit(solution)/shard_map/pallas_call | solution.py:441
  44.2 12.9 %all-to-all-done.1 = bf16[8,16,16,256]{3,2,1,0:T(8,128)(2,1)} async-done(((bf16[8,16,16,256]{3,2,1,0:T(8,128)(2,1)}), bf16[8,16,16,256]{3,2,1,0:T(8,128)(2,1)}, u32[]{:S(2)}, u32[]{:S(2)}) %all-to-all-start.1) | async-done | bytes 1048608 | tf_op jit(solution)/shard_map/all_to_all | solution.py:439
  57.0 2.0 %shard_map.121 = (bf16[64,16,256]{2,1,0:T(8,128)(2,1)S(1)}, bf16[64,16,256]{2,1,0:T(8,128)(2,1)S(1)}) custom-call(s32[1]{0:T(128)} %bitcast.3.core_ref, s32[1,128]{1,0:T(1,128)S(1)} %copy-done.6, bf16[128,16,256]{2,1,0:T(8,128)(2,1)} %bitcast.10.refs_0_, bf16[32,16,256]{2,1,0:T(8,128)(2,1)S(1)} %copy-done.2, ...), custom_call_target="tpu_custom_call" | custom-call | tf_op jit(solution)/shard_map/pallas_call | solution.py:456
  59.1 2.4 %collective-permute-done.5.refs_0_ = bf16[32,16,256]{2,1,0:T(8,128)(2,1)S(1)} collective-permute-done((bf16[32,16,256]{2,1,0:T(8,128)(2,1)S(1)}, bf16[32,16,256]{2,1,0:T(8,128)(2,1)S(1)}, u32[]{:S(2)}, u32[]{:S(2)}) %collective-permute-start.5) | collective-permute-done | bytes 262176 | tf_op jit(solution)/shard_map/ppermute | solution.py:400
  62.1 0.9 %collective-permute-done.13.refs_1_ = bf16[32,16,256]{2,1,0:T(8,128)(2,1)S(1)} collective-permute-done((bf16[32,16,256]{2,1,0:T(8,128)(2,1)S(1)}, bf16[32,16,256]{2,1,0:T(8,128)(2,1)S(1)}, u32[]{:S(2)}, u32[]{:S(2)}) %collective-permute-start.13) | collective-permute-done | bytes 262176 | tf_op jit(solution)/shard_map/ppermute | solution.py:397
  63.1 0.6 copy-done.10
  63.7 6.8 %shard_map.122 = (bf16[1024,512]{1,0:T(8,128)(2,1)S(1)}, f32[32,512]{1,0:T(8,128)S(1)}, bf16[512,2048]{1,0:T(8,128)(2,1)S(1)}, bf16[2048,512]{1,0:T(8,128)(2,1)S(1)}, f32[1,2048]{1,0:T(1,128)S(1)}) custom-call(s32[1]{0:T(128)} %bitcast.3.core_ref, s32[1,128]{1,0:T(1,128)S(1)} %copy-done.6, s32[1]{0:T(128)} %get-tuple-element.45.crowded_ref, f32[4]{0:T(128)S(1)} %copy-done.8, ...), custom_call_target="tpu_custom_call" | custom-call | flops 1610612736 | bytes 4194304 | tf_op jit(solution)/shard_map/pallas_call | solution.py:483
  70.5 4.1 %fusion.7 = bf16[1024,2048]{1,0:T(8,128)(2,1)S(1)} fusion(f32[2048]{0:T(1024)S(1)} %bitcast.23, bf16[1024,512]{1,0:T(8,128)(2,1)S(1)} %get-tuple-element.72, bf16[512,2048]{1,0:T(8,128)(2,1)S(1)} %get-tuple-element.73), kind=kOutput, calls=%fused_computation.10 | convolution fusion | flops 2168455168 | bytes 7348224 | tf_op jit(solution)/shard_map/dot_general | solution.py:25
  74.6 1.2 %convert_reduce_fusion = f32[4,8,2048]{2,1,0:T(8,128)S(1)} fusion(bf16[4,2,8,16,2048]{4,3,2,1,0:T(8,128)(2,1)S(1)} %bitcast.24), kind=kLoop, calls=%fused_computation.11 | loop fusion | flops 4128768 | bytes 4456448 | tf_op jit(solution)/shard_map/reduce_sum | solution.py:368
  76.5 1.1 %collective-permute-done.15 = bf16[64,512]{1,0:T(8,128)(2,1)S(1)} collective-permute-done((bf16[64,512]{1,0:T(8,128)(2,1)S(1)}, bf16[64,512]{1,0:T(8,128)(2,1)S(1)}, u32[]{:S(2)}, u32[]{:S(2)}) %collective-permute-start.15) | collective-permute-done | bytes 65568 | tf_op jit(solution)/shard_map/ppermute | solution.py:397
  77.6 0.6 add.28
  (39 shorter events, 1.5 us)
Async XLA Ops:
  0.0 39.8 %copy-start.7 = (f32[4]{0:T(128)S(1)}, f32[4]{0:T(128)}, u32[]{:S(2)}) copy-start(f32[4]{0:T(128)} %scale_a_ref.1) | copy-start | bytes 52
  15.6 25.8 %copy-start.3 = (s32[8,1,36]{2,1,0:T(1,128)S(1)}, s32[8,1,36]{2,1,0:T(1,128)}, u32[]{:S(2)}) copy-start(s32[8,1,36]{2,1,0:T(1,128)} %all_to_all.10.incoming_ref) | copy-start | bytes 3460
  18.8 9.2 %collective-permute-start.2 = (bf16[32,16,256]{2,1,0:T(8,128)(2,1)}, bf16[32,16,256]{2,1,0:T(8,128)(2,1)S(1)}, u32[]{:S(2)}, u32[]{:S(2)}) collective-permute-start(bf16[32,16,256]{2,1,0:T(8,128)(2,1)} %get-tuple-element.47), channel_id=1, source_target_pairs={{0,2},{2,0},{4,6},{6,4},{8,10},{10,8},{12,14},{14,12},{1,3},{3,1},... | collective-permute-start | bytes 786440 | tf_op jit(solution)/shard_map/ppermute | solution.py:400
  19.4 9.5 %collective-permute-start.3 = (bf16[32,16,256]{2,1,0:T(8,128)(2,1)}, bf16[32,16,256]{2,1,0:T(8,128)(2,1)S(1)}, u32[]{:S(2)}, u32[]{:S(2)}) collective-permute-start(bf16[32,16,256]{2,1,0:T(8,128)(2,1)} %get-tuple-element.48), channel_id=1, source_target_pairs={{0,4},{2,6},{4,0},{6,2},{8,12},{10,14},{12,8},{14,10},{1,5},{3,7},... | collective-permute-start | bytes 786440 | tf_op jit(solution)/shard_map/ppermute | solution.py:400
  20.0 19.8 %collective-permute-start.4 = (bf16[32,16,256]{2,1,0:T(8,128)(2,1)}, bf16[32,16,256]{2,1,0:T(8,128)(2,1)S(1)}, u32[]{:S(2)}, u32[]{:S(2)}) collective-permute-start(bf16[32,16,256]{2,1,0:T(8,128)(2,1)} %get-tuple-element.49), channel_id=1, source_target_pairs={{0,6},{2,4},{4,2},{6,0},{8,14},{10,12},{12,10},{14,8},{1,7},{3,5},... | collective-permute-start | bytes 786440 | tf_op jit(solution)/shard_map/ppermute | solution.py:400
  22.3 34.7 %all-to-all-start.1 = ((bf16[8,16,16,256]{3,2,1,0:T(8,128)(2,1)}), bf16[8,16,16,256]{3,2,1,0:T(8,128)(2,1)}, u32[]{:S(2)}, u32[]{:S(2)}) async-start(bf16[8,16,16,256]{3,2,1,0:T(8,128)(2,1)} %get-tuple-element.62), calls=%async_computation.1 | async-start | bytes 2097152 | tf_op jit(solution)/shard_map/all_to_all | solution.py:439
  39.8 1.1 %collective-permute-start.12 = (f32[4]{0:T(128)S(1)}, f32[4]{0:T(128)S(1)}, u32[]{:S(2)}, u32[]{:S(2)}) collective-permute-start(f32[4]{0:T(128)S(1)} %copy-done.7), channel_id=1, source_target_pairs={{0,1},{1,0},{2,3},{3,2},{4,5},{5,4},{6,7},{7,6},{8,9},{9,8},{10,11... | collective-permute-start | bytes 56 | tf_op jit(solution)/shard_map/ppermute | solution.py:397
  39.8 4.1 %collective-permute-start.11 = (f32[1024]{0:T(1024)}, f32[1024]{0:T(1024)}, u32[]{:S(2)}, u32[]{:S(2)}) collective-permute-start(f32[1024]{0:T(1024)} %param.24), channel_id=1, source_target_pairs={{0,1},{1,0},{2,3},{3,2},{4,5},{5,4},{6,7},{7,6},{8,9},{9,8},{10,11... | collective-permute-start | bytes 12296 | tf_op jit(solution)/shard_map/ppermute | solution.py:397
  40.3 3.8 %collective-permute-start.6 = (bf16[512,256]{1,0:T(8,128)(2,1)}, bf16[512,256]{1,0:T(8,128)(2,1)}, u32[]{:S(2)}, u32[]{:S(2)}) collective-permute-start(bf16[512,256]{1,0:T(8,128)(2,1)} %refs_5_.1), channel_id=1, source_target_pairs={{0,1},{1,0},{2,3},{3,2},{4,5},{5,4},{6,7},{7,6},{8,9},{9,8},{10,11... | collective-permute-start | bytes 786440 | tf_op jit(solution)/shard_map/ppermute | solution.py:397
  40.3 18.7 %collective-permute-start.7 = (bf16[512,256]{1,0:T(8,128)(2,1)}, bf16[512,256]{1,0:T(8,128)(2,1)}, u32[]{:S(2)}, u32[]{:S(2)}) collective-permute-start(bf16[512,256]{1,0:T(8,128)(2,1)} %refs_7_.1), channel_id=1, source_target_pairs={{0,1},{1,0},{2,3},{3,2},{4,5},{5,4},{6,7},{7,6},{8,9},{9,8},{10,11... | collective-permute-start | bytes 786440 | tf_op jit(solution)/shard_map/ppermute | solution.py:397
  40.9 20.7 %collective-permute-start.9 = (bf16[512,1024]{1,0:T(8,128)(2,1)}, bf16[512,1024]{1,0:T(8,128)(2,1)}, u32[]{:S(2)}, u32[]{:S(2)}) collective-permute-start(bf16[512,1024]{1,0:T(8,128)(2,1)} %refs_11_.1), channel_id=1, source_target_pairs={{0,1},{1,0},{2,3},{3,2},{4,5},{5,4},{6,7},{7,6},{8,9},{9,8},{10,11... | collective-permute-start | bytes 3145736 | tf_op jit(solution)/shard_map/ppermute | solution.py:397
  41.0 3.0 %copy-start.9 = (f32[4]{0:T(128)}, f32[4]{0:T(128)S(1)}, u32[]{:S(2)}) copy-start(f32[4]{0:T(128)S(1)} %collective-permute-done.12.scale_b_ref) | copy-start | bytes 52
  41.0 20.6 %collective-permute-start.10 = (bf16[1024,512]{1,0:T(8,128)(2,1)}, bf16[1024,512]{1,0:T(8,128)(2,1)}, u32[]{:S(2)}, u32[]{:S(2)}) collective-permute-start(bf16[1024,512]{1,0:T(8,128)(2,1)} %refs_13_.1), channel_id=1, source_target_pairs={{0,1},{1,0},{2,3},{3,2},{4,5},{5,4},{6,7},{7,6},{8,9},{9,8},{10,11... | collective-permute-start | bytes 3145736 | tf_op jit(solution)/shard_map/ppermute | solution.py:397
  42.3 1.7 %copy-start = (bf16[256,512]{1,0:T(8,128)(2,1)S(1)}, bf16[256,512]{1,0:T(8,128)(2,1)}, u32[]{:S(2)}) copy-start(bf16[256,512]{1,0:T(8,128)(2,1)} %refs_9_.1) | copy-start | bytes 786436
  42.3 14.7 %copy-start.2 = (bf16[32,16,256]{2,1,0:T(8,128)(2,1)S(1)}, bf16[32,16,256]{2,1,0:T(8,128)(2,1)}, u32[]{:S(2)}) copy-start(bf16[32,16,256]{2,1,0:T(8,128)(2,1)} %get-tuple-element.46.refs_0_.refs_1_) | copy-start | bytes 786436
  42.3 14.7 %copy-start.6 = (s32[1,128]{1,0:T(1,128)S(1)}, s32[1,128]{1,0:T(1,128)}, u32[]{:S(2)}) copy-start(s32[1,128]{1,0:T(1,128)} %get-tuple-element.43.list_ref) | copy-start | bytes 1540
  42.3 20.7 %copy-start.4 = (f32[512]{0:T(512)S(1)}, f32[512]{0:T(512)}, u32[]{:S(2)}) copy-start(f32[512]{0:T(512)} %param.17) | copy-start | bytes 6148
  42.3 20.7 %copy-start.5 = (f32[512]{0:T(512)S(1)}, f32[512]{0:T(512)}, u32[]{:S(2)}) copy-start(f32[512]{0:T(512)} %param.22) | copy-start | bytes 6148
  42.3 20.7 %copy-start.8 = (f32[4]{0:T(128)S(1)}, f32[4]{0:T(128)}, u32[]{:S(2)}) copy-start(f32[4]{0:T(128)} %scale_a_ref.1) | copy-start | bytes 52
  44.0 15.1 %collective-permute-start.8 = (bf16[256,512]{1,0:T(8,128)(2,1)S(1)}, bf16[256,512]{1,0:T(8,128)(2,1)S(1)}, u32[]{:S(2)}, u32[]{:S(2)}) collective-permute-start(bf16[256,512]{1,0:T(8,128)(2,1)S(1)} %copy-done), channel_id=1, source_target_pairs={{0,1},{1,0},{2,3},{3,2},{4,5},{5,4},{6,7},{7,6},{8,9},{9,8},{10,11... | collective-permute-start | bytes 786440 | tf_op jit(solution)/shard_map/ppermute | solution.py:397
  44.1 17.4 %collective-permute-start.5 = (bf16[32,16,256]{2,1,0:T(8,128)(2,1)S(1)}, bf16[32,16,256]{2,1,0:T(8,128)(2,1)S(1)}, u32[]{:S(2)}, u32[]{:S(2)}) collective-permute-start(bf16[32,16,256]{2,1,0:T(8,128)(2,1)S(1)} %get-tuple-element.50), channel_id=1, source_target_pairs={{0,8},{2,10},{4,12},{6,14},{8,0},{10,2},{12,4},{14,6},{1,9},{3,11}... | collective-permute-start | bytes 786440 | tf_op jit(solution)/shard_map/ppermute | solution.py:400
  59.0 4.0 %collective-permute-start.14 = (bf16[64,16,256]{2,1,0:T(8,128)(2,1)S(1)}, bf16[64,16,256]{2,1,0:T(8,128)(2,1)S(1)}, u32[]{:S(2)}, u32[]{:S(2)}) collective-permute-start(bf16[64,16,256]{2,1,0:T(8,128)(2,1)S(1)} %get-tuple-element.64), channel_id=1, source_target_pairs={{0,1},{1,0},{2,3},{3,2},{4,5},{5,4},{6,7},{7,6},{8,9},{9,8},{10,11... | collective-permute-start | bytes 1572872 | tf_op jit(solution)/shard_map/ppermute | solution.py:397
  61.5 1.5 %collective-permute-start.13 = (bf16[32,16,256]{2,1,0:T(8,128)(2,1)S(1)}, bf16[32,16,256]{2,1,0:T(8,128)(2,1)S(1)}, u32[]{:S(2)}, u32[]{:S(2)}) collective-permute-start(bf16[32,16,256]{2,1,0:T(8,128)(2,1)S(1)} %collective-permute-done.5.refs_0_), channel_id=1, source_target_pairs={{0,1},{1,0},{2,3},{3,2},{4,5},{5,4},{6,7},{7,6},{8,9},{9,8},{10,11... | collective-permute-start | bytes 786440 | tf_op jit(solution)/shard_map/ppermute | solution.py:397
  76.3 1.3 %collective-permute-start.15 = (bf16[64,512]{1,0:T(8,128)(2,1)S(1)}, bf16[64,512]{1,0:T(8,128)(2,1)S(1)}, u32[]{:S(2)}, u32[]{:S(2)}) collective-permute-start(bf16[64,512]{1,0:T(8,128)(2,1)S(1)} %shard_map.123), channel_id=1, source_target_pairs={{0,1},{1,0},{2,3},{3,2},{4,5},{5,4},{6,7},{7,6},{8,9},{9,8},{10,11... | collective-permute-start | bytes 196616 | tf_op jit(solution)/shard_map/ppermute | solution.py:397
  (2 other events, 1.6 us)

commit v8 on v7

--- a/solution.py
+++ b/solution.py
@@ -177,7 +177,7 @@
     lax.fori_loop(0, count, pick, 0, unroll=8)
 
 
-def attention_kernel(
+def compare_kernel(
     plan,
     length,
     head_dim,
@@ -194,16 +194,16 @@
         first_held_ref, far_first_held_ref, second_held_ref, *refs = refs
         *refs, rest_ref, rest_sems = refs
     own_held_ref, far_held_ref, *held_refs = refs[:14]
-    normed_ref, mean_ref, in_ref, back_ref, bias_ref = refs[14:19]
-    qkv_ref, out_ref, tokens_ref, heads_ref, mixed_ref, hidden_ref, sems, token_sems = refs[19:]
+    result_ref, normed_ref, mean_ref, pooled_ref, in_ref, back_ref, bias_ref = refs[14:21]
+    qkv_ref, out_ref, tokens_ref, heads_ref, mixed_ref, hidden_ref, sems, token_sems = refs[21:]
     units = in_ref.shape[1] // 2
     width = out_ref.shape[0]
     wide = width // 2
     homes = [qkv_ref.at[:, pl.ds(k * wide, wide)] for k in range(4)]
     homes += [out_ref.at[pl.ds(k * wide, wide)] for k in range(2)]
     homes += [in_ref.at[:, pl.ds(k * units, units)] for k in range(2)]
+    homes += [bias_ref.at[:, pl.ds(k * units, units)] for k in range(2)]
     homes += [back_ref.at[pl.ds(k * units, units)] for k in range(2)]
-    homes += [bias_ref.at[:, pl.ds(k * units, units)] for k in range(2)]
     loads = [
         pltpu.make_async_copy(held, home, sems.at[k])
         for k, (held, home) in enumerate(zip(held_refs, homes))
@@ -266,12 +266,14 @@
         )
         hidden_ref[span(step, rows), :] = tokens
         normed_ref[span(step, rows), :] = norm_rows(tokens, gain_attn_ref[...]).astype(jnp.bfloat16)
+        yield
 
     def project(step):
         here = span(step, rows)
         for index in range(4):
             cut = span(index, wide)
             heads_ref[here, cut] = dot(normed_ref[here, :], qkv_ref[:, cut]).astype(jnp.bfloat16)
+            yield
 
     def weigh(scores, factor):
         scores = jnp.where(same, scores, -1e30)
@@ -298,12 +300,14 @@
             value = [heads_ref[side, beyond] for side in sides]
             for k in range(2):
                 mixed_ref[sides[k], cut] = mix(query[k], query[1 - k], value[1 - k], factors)
+                yield
 
     def join(step):
         here = span(step, rows)
         for index in range(2):
             cut = span(index, wide)
             hidden_ref[here, cut] += dot(mixed_ref[here, :], out_ref[:, cut])
+            yield
 
     def middle(step):
         here = span(step, rows)
@@ -312,6 +316,17 @@
             hidden.reshape(2, BLOCK, length, -1), axis=(0, 2)
         )
         normed_ref[here, :] = norm_rows(hidden, gain_mlp_ref[...]).astype(jnp.bfloat16)
+        yield
+
+    def expand(step):
+        here = span(step, rows)
+        for at in range(0, 2 * units, 256):
+            cut = pl.ds(at, 256)
+            inner = dot(normed_ref[here, :], in_ref[:, cut]) + bias_ref[:, cut]
+            bent = jnp.tanh(inner * (0.7978845608028654 + 0.035677408136300125 * (inner * inner)))
+            bent = (inner * bent + inner).reshape(2, BLOCK, length, -1)
+            pooled_ref[span(step, BLOCK), cut] = jnp.sum(bent, axis=(0, 2))
+            yield
 
     for load in token_loads:
         load.wait()
@@ -335,37 +350,30 @@
             return carry
 
         lax.fori_loop(0, tokens_ref.shape[1], put, 0, unroll=4)
-    stages = (begin, project, attend, join, middle)
+    stages = (begin, project, attend, join, middle, expand)
+    needs = {1: loads[:4], 3: loads[4:6], 5: loads[6:10]}
     for turn in range(blocks + len(stages) - 1):
-        if turn == 1:
-            for load in loads[:4]:
-                load.wait()
-        if turn == 3:
-            for load in loads[4:]:
-                load.wait()
-        for index, stage in enumerate(stages):
-            if 0 <= turn - index < blocks:
-                stage(turn - index)
-
-
-def back_kernel(length, core_ref, mean_ref, pooled_ref, back_ref, result_ref):
+        for load in needs.get(turn, []):
+            load.wait()
+        active = [
+            stage(turn - index)
+            for index, stage in enumerate(stages)
+            if 0 <= turn - index < blocks
+        ]
+        while active:
+            active = [steps for steps in active if next(steps, 0) is None]
+    for load in loads[10:]:
+        load.wait()
     count = mean_ref.shape[0]
-    pooled = pooled_ref[...] * (0.5 / length)
+    pooled = pooled_ref[...] * (0.25 / length)
     coarse = pooled.astype(jnp.bfloat16)
     fine = (pooled - coarse.astype(jnp.float32)).astype(jnp.bfloat16)
     back = dot(jnp.concatenate([coarse, fine], axis=0), back_ref[...])
     mean = mean_ref[...] * (0.5 / length)
     result = (mean + back[:count] + back[count:]).astype(jnp.bfloat16)
-    start = pl.multiple_of(core_ref[0] * count, count)
-    result_ref[pl.ds(start, count), :] = result
-    result_ref[pl.ds(pl.multiple_of(count - start, count), count), :] = jnp.zeros_like(result)
-
-
-def expand(normed, w_in, bias, length):
-    inner = dot(normed, w_in) + bias
-    inner = jax.nn.gelu(inner, approximate=True).astype(jnp.bfloat16).astype(jnp.float32)
-    inner = inner.reshape(-1, 2, BLOCK, length, inner.shape[-1])
-    return jnp.sum(inner, axis=(1, 3)).reshape(-1, inner.shape[-1])
+    at = pl.multiple_of(core * count, count)
+    result_ref[pl.ds(at, count), :] = result
+    result_ref[pl.ds(pl.multiple_of(count - at, count), count), :] = jnp.zeros_like(result)
 
 
 def on_device(
@@ -480,17 +488,17 @@
     far_qk, far_value, far_out, far_in, far_back, far_bias, far_scale = swapped
     token_count = pair_count * length
     units = 2 * w_in.shape[1]
-    normed, mean, all_in, all_back, all_bias = pl.pallas_call(
-        functools.partial(attention_kernel, plan, length, head_dim),
-        out_shape=(
-            jax.ShapeDtypeStruct((token_count, width), jnp.bfloat16),
-            jax.ShapeDtypeStruct((mine, width), jnp.float32),
-            jax.ShapeDtypeStruct((width, units), jnp.bfloat16),
-            jax.ShapeDtypeStruct((units, width), jnp.bfloat16),
-            jax.ShapeDtypeStruct((1, units), jnp.float32),
-        ),
+    here = pl.pallas_call(
+        functools.partial(compare_kernel, plan, length, head_dim),
+        out_shape=jax.ShapeDtypeStruct((pair_count, width), jnp.bfloat16),
         in_specs=[smem] * 5 + [vmem] * 2 + [hbm] * len(rest) + [vmem] * 2 + [hbm] * 12,
         scratch_shapes=[
+            pltpu.VMEM((token_count, width), jnp.bfloat16),
+            pltpu.VMEM((mine, width), jnp.float32),
+            pltpu.VMEM((mine, units), jnp.float32),
+            pltpu.VMEM((width, units), jnp.bfloat16),
+            pltpu.VMEM((units, width), jnp.bfloat16),
+            pltpu.VMEM((1, units), jnp.float32),
             pltpu.VMEM((width, 2 * width), jnp.bfloat16),
             pltpu.VMEM((width, width), jnp.bfloat16),
             pltpu.VMEM((2, pair_count, length, features), jnp.bfloat16),
@@ -510,9 +518,9 @@
         ),
         compiler_params=limit(32),
         cost_estimate=pl.CostEstimate(
-            flops=6 * token_count * width * width,
-            bytes_accessed=4 * 2**20,
-            transcendentals=token_count * 1024,
+            flops=2 * token_count * width * (3 * width + units),
+            bytes_accessed=8 * 2**20,
+            transcendentals=token_count * units,
         ),
     )(
         core,
@@ -533,17 +541,11 @@
         far_out,
         w_in,
         far_in,
+        bias_in.reshape(1, -1),
+        far_bias.reshape(1, -1),
         w_back,
         far_back,
-        bias_in.reshape(1, -1),
-        far_bias.reshape(1, -1),
     )
-    here = pl.pallas_call(
-        functools.partial(back_kernel, length),
-        out_shape=jax.ShapeDtypeStruct((pair_count, width), jnp.bfloat16),
-        in_specs=[smem] + [vmem] * 3,
-        compiler_params=limit(16),
-    )(core, mean, expand(normed, all_in, all_bias, length), all_back)
     return here + swap(here)
 
 

time: 78.6 us -> 78.7 us (level)
  Pallas kernels: 15.8 us -> 21.7 us
  matrix products: 4.13 us -> 0 us
  other arithmetic: 1.83 us -> 0.65 us
  local copies, waits for them, and re-layouts: 1.62 us -> 0.57 us
    pallas_call x2 -> x1, Pallas kernels: 7.24 us -> 13.2 us  [on_device(): pl.pallas_call(functools.partial(compare_kernel, plan, length, head_dim),...]
    dot_general x1 -> x0, matrix products: 4.13 us -> none  [dot(): return jnp.dot(a, b, preferred_element_type=jnp.float32)]
    reduce_sum x1 -> x0, other arithmetic: 1.19 us -> none  [expand(): return jnp.sum(inner, axis=(1, 3)).reshape(-1, inner.shape[-1])]
    unnamed x22 -> x20, local copies, waits for them, and re-layouts: 1.62 us -> 0.57 us
where the time goes in v8:
time: 78.7 us; the launch traced here: 78.4 us
  waiting for transfers between devices  31.2 us (40%)
  Pallas kernels  21.7 us (28%)
  blocking collectives  13.6 us (17%)
  starting transfers between devices  9.66 us (12%)
    ppermute x4, waiting for transfers between devices, across(): lax.ppermute(values, 'shard', [(k, k ^ distance) for k in range(owner_cou...  15.9 us
    all_to_all x1, blocking collectives, on_device(): lax.all_to_all(wanted, 'shard', split_axis=0, concat_axis=0, tiled=True)  13.6 us
    all_to_all x1, waiting for transfers between devices, on_device(): lax.all_to_all(served, 'shard', split_axis=0, concat_axis=0, tiled=True)  13.4 us
    pallas_call x1, Pallas kernels, on_device(): pl.pallas_call(functools.partial(compare_kernel, plan, length, head_dim),...  13.2 us
    all_to_all x1, starting transfers between devices, on_device(): lax.all_to_all(served, 'shard', split_axis=0, concat_axis=0, tiled=True)  4.24 us
    ppermute x4, starting transfers between devices, across(): lax.ppermute(values, 'shard', [(k, k ^ distance) for k in range(owner_cou...  3.56 us
    pallas_call x1, Pallas kernels, on_device(): pl.pallas_call(functools.partial(serve_kernel, plan), out_shape=[images(2...  3.17 us
    pallas_call x1, Pallas kernels, on_device(): pl.pallas_call(functools.partial(pick_kernel, plan), out_shape=[images(pa...  1.99 us
  transfers between devices with their start and end apart: 15, of which 8 were waited for; matrix products, arithmetic and copies ran while one was open for 0% of the time, Pallas kernels for 5%

profile of v8, /device:TPU:0, one launch (start us, length us, event | category | flops | bytes accessed | tf_op | source)
XLA Modules:
  0.0 78.4 jit_solution(4642633514467042496)
XLA Ops:
  0.0 1.8 %shard_map.118 = (s32[8,1,36]{2,1,0:T(1,128)}, s32[1,128]{1,0:T(1,128)}) custom-call(s32[1]{0:T(128)} %bitcast.4.shard_ref, s32[2,64]{1,0:T(2,128)} %bitcast.18, s32[2,64]{1,0:T(2,128)} %bitcast.19), custom_call_target="tpu_custom_call" | custom-call | tf_op jit(solution)/shard_map/pallas_call | solution.py:420
  1.8 13.6 %all_to_all.10.incoming_ref = s32[8,1,36]{2,1,0:T(1,128)} all-to-all(s32[8,1,36]{2,1,0:T(1,128)} %get-tuple-element.39), channel_id=1, replica_groups=mesh['groups'=2,'shard'=8,'mp'=2] {'shard'}, dimensions={0} | all-to-all | bytes 2304 | tf_op jit(solution)/shard_map/all_to_all | solution.py:428
  15.4 3.2 %shard_map.119 = (bf16[32,16,256]{2,1,0:T(8,128)(2,1)}, bf16[32,16,256]{2,1,0:T(8,128)(2,1)}, bf16[32,16,256]{2,1,0:T(8,128)(2,1)}, bf16[32,16,256]{2,1,0:T(8,12...) custom-call(s32[1]{0:T(128)} %bitcast.4.shard_ref, s32[8,1,36]{2,1,0:T(1,128)} %all_to_all.10.incoming_ref, ...), custom_call_target="tpu_custom_call" | custom-call | tf_op jit(solution)/shard_map/pallas_call | solution.py:438
  18.6 0.6 collective-permute-start.2
  19.2 0.6 collective-permute-start.3
  19.8 2.4 %collective-permute-start.4 = (bf16[32,16,256]{2,1,0:T(8,128)(2,1)}, bf16[32,16,256]{2,1,0:T(8,128)(2,1)S(1)}, u32[]{:S(2)}, u32[]{:S(2)}) collective-permute-start(bf16[32,16,256]{2,1,0:T(8,128)(2,1)} %get-tuple-element.44), channel_id=1, source_target_pairs={{0,6},{2,4},{4,2},{6,0},{8,14},{10,12},{12,10},{14,8},{1,7},{3,5},... | collective-permute-start | bytes 786440 | tf_op jit(solution)/shard_map/ppermute | solution.py:408
  22.1 4.2 %all-to-all-start.1 = ((bf16[8,16,16,256]{3,2,1,0:T(8,128)(2,1)}), bf16[8,16,16,256]{3,2,1,0:T(8,128)(2,1)}, u32[]{:S(2)}, u32[]{:S(2)}) async-start(bf16[8,16,16,256]{3,2,1,0:T(8,128)(2,1)} %get-tuple-element.57), calls=%async_computation.1 | async-start | bytes 2097152 | tf_op jit(solution)/shard_map/all_to_all | solution.py:447
  26.4 1.1 %collective-permute-done.2.refs_1_.refs_2_ = bf16[32,16,256]{2,1,0:T(8,128)(2,1)S(1)} collective-permute-done((bf16[32,16,256]{2,1,0:T(8,128)(2,1)}, bf16[32,16,256]{2,1,0:T(8,128)(2,1)S(1)}, u32[]{:S(2)}, u32[]{:S(2)}) %collective-permute-start.2) | collective-permute-done | bytes 262176 | tf_op jit(solution)/shard_map/ppermute | solution.py:408
  27.5 1.2 %collective-permute-done.3.refs_2_.refs_3_ = bf16[32,16,256]{2,1,0:T(8,128)(2,1)S(1)} collective-permute-done((bf16[32,16,256]{2,1,0:T(8,128)(2,1)}, bf16[32,16,256]{2,1,0:T(8,128)(2,1)S(1)}, u32[]{:S(2)}, u32[]{:S(2)}) %collective-permute-start.3) | collective-permute-done | bytes 262176 | tf_op jit(solution)/shard_map/ppermute | solution.py:408
  28.6 11.0 %collective-permute-done.4.refs_3_.refs_4_ = bf16[32,16,256]{2,1,0:T(8,128)(2,1)S(1)} collective-permute-done((bf16[32,16,256]{2,1,0:T(8,128)(2,1)}, bf16[32,16,256]{2,1,0:T(8,128)(2,1)S(1)}, u32[]{:S(2)}, u32[]{:S(2)}) %collective-permute-start.4) | collective-permute-done | bytes 262176 | tf_op jit(solution)/shard_map/ppermute | solution.py:408
  39.7 0.5 collective-permute-start.11
  40.2 0.5 collective-permute-start.7
  40.8 0.5 copy-done.8
  41.3 0.4 collective-permute-start.10
  41.8 1.6 %shard_map.120 = (bf16[32,16,256]{2,1,0:T(8,128)(2,1)S(1)}, bf16[2,32,16,256]{3,2,1,0:T(8,128)(2,1)}) custom-call(s32[1]{0:T(128)} %bitcast.4.shard_ref, s32[8,1,36]{2,1,0:T(1,128)S(1)} %copy-done.1, bf16[32,16,256]{2,1,0:T(8,128)(2,1)S(1)} %copy-done, bf16[32,16,256]{2,1,0:T(8,128)(2,1)S(1)} %collective-permute-done.2.refs_1_.refs_2_, ...), custom_call_target="tpu_custom_call" | custom-call | flops 199999995904 | bytes 1048576 | tf_op jit(solution)/shard_map/pallas_call | solution.py:449
  43.6 13.4 %all-to-all-done.1 = bf16[8,16,16,256]{3,2,1,0:T(8,128)(2,1)} async-done(((bf16[8,16,16,256]{3,2,1,0:T(8,128)(2,1)}), bf16[8,16,16,256]{3,2,1,0:T(8,128)(2,1)}, u32[]{:S(2)}, u32[]{:S(2)}) %all-to-all-start.1) | async-done | bytes 1048608 | tf_op jit(solution)/shard_map/all_to_all | solution.py:447
  57.0 2.0 %shard_map.121 = (bf16[64,16,256]{2,1,0:T(8,128)(2,1)S(1)}, bf16[64,16,256]{2,1,0:T(8,128)(2,1)S(1)}) custom-call(s32[1]{0:T(128)} %bitcast.3.core_ref, s32[1,128]{1,0:T(1,128)S(1)} %copy-done.2, bf16[128,16,256]{2,1,0:T(8,128)(2,1)} %bitcast.10.refs_0_, bf16[32,16,256]{2,1,0:T(8,128)(2,1)S(1)} %copy-done, ...), custom_call_target="tpu_custom_call" | custom-call | tf_op jit(solution)/shard_map/pallas_call | solution.py:464
  59.1 2.6 %collective-permute-done.5.refs_0_ = bf16[32,16,256]{2,1,0:T(8,128)(2,1)S(1)} collective-permute-done((bf16[32,16,256]{2,1,0:T(8,128)(2,1)S(1)}, bf16[32,16,256]{2,1,0:T(8,128)(2,1)S(1)}, u32[]{:S(2)}, u32[]{:S(2)}) %collective-permute-start.5) | collective-permute-done | bytes 262176 | tf_op jit(solution)/shard_map/ppermute | solution.py:408
  62.3 0.2 conditional.1
  62.5 0.7 collective-permute-done.13.refs_1_
  63.2 13.2 %shard_map.122 = bf16[64,512]{1,0:T(8,128)(2,1)S(1)} custom-call(s32[1]{0:T(128)} %bitcast.3.core_ref, s32[1,128]{1,0:T(1,128)S(1)} %copy-done.2, s32[1]{0:T(128)} %get-tuple-element.40.crowded_ref, f32[4]{0:T(128)S(1)} %copy-done.7, f32[4]{0:T(128)S(1)} %copy-done.9, f32[1,512]{1,0:T(1,128)S(1)} %bitcast.14, f32[1,512]{1,0:T(1,128)S(1)} %bitcast.15, ...), custom_call_target="tpu_custom_call" | custom-call | flops 3758096384 | bytes 8388608 | tf_op jit(solution)/shard_map/pallas_call | solution.py:491
  76.4 0.2 collective-permute-start.15
  76.6 1.1 %collective-permute-done.15 = bf16[64,512]{1,0:T(8,128)(2,1)S(1)} collective-permute-done((bf16[64,512]{1,0:T(8,128)(2,1)S(1)}, bf16[64,512]{1,0:T(8,128)(2,1)S(1)}, u32[]{:S(2)}, u32[]{:S(2)}) %collective-permute-start.15) | collective-permute-done | bytes 65568 | tf_op jit(solution)/shard_map/ppermute | solution.py:405
  77.7 0.6 add.3
  (34 shorter events, 0.4 us)
Async XLA Ops:
  15.4 24.3 %copy-start.6 = (f32[4]{0:T(128)S(1)}, f32[4]{0:T(128)}, u32[]{:S(2)}) copy-start(f32[4]{0:T(128)} %scale_a_ref.1) | copy-start | bytes 52
  15.4 26.4 %copy-start.1 = (s32[8,1,36]{2,1,0:T(1,128)S(1)}, s32[8,1,36]{2,1,0:T(1,128)}, u32[]{:S(2)}) copy-start(s32[8,1,36]{2,1,0:T(1,128)} %all_to_all.10.incoming_ref) | copy-start | bytes 3460
  18.6 23.2 %copy-start = (bf16[32,16,256]{2,1,0:T(8,128)(2,1)S(1)}, bf16[32,16,256]{2,1,0:T(8,128)(2,1)}, u32[]{:S(2)}) copy-start(bf16[32,16,256]{2,1,0:T(8,128)(2,1)} %get-tuple-element.41.refs_0_.refs_1_) | copy-start | bytes 786436
  18.6 8.9 %collective-permute-start.2 = (bf16[32,16,256]{2,1,0:T(8,128)(2,1)}, bf16[32,16,256]{2,1,0:T(8,128)(2,1)S(1)}, u32[]{:S(2)}, u32[]{:S(2)}) collective-permute-start(bf16[32,16,256]{2,1,0:T(8,128)(2,1)} %get-tuple-element.42), channel_id=1, source_target_pairs={{0,2},{2,0},{4,6},{6,4},{8,10},{10,8},{12,14},{14,12},{1,3},{3,1},... | collective-permute-start | bytes 786440 | tf_op jit(solution)/shard_map/ppermute | solution.py:408
  19.2 9.5 %collective-permute-start.3 = (bf16[32,16,256]{2,1,0:T(8,128)(2,1)}, bf16[32,16,256]{2,1,0:T(8,128)(2,1)S(1)}, u32[]{:S(2)}, u32[]{:S(2)}) collective-permute-start(bf16[32,16,256]{2,1,0:T(8,128)(2,1)} %get-tuple-element.43), channel_id=1, source_target_pairs={{0,4},{2,6},{4,0},{6,2},{8,12},{10,14},{12,8},{14,10},{1,5},{3,7},... | collective-permute-start | bytes 786440 | tf_op jit(solution)/shard_map/ppermute | solution.py:408
  19.8 19.9 %collective-permute-start.4 = (bf16[32,16,256]{2,1,0:T(8,128)(2,1)}, bf16[32,16,256]{2,1,0:T(8,128)(2,1)S(1)}, u32[]{:S(2)}, u32[]{:S(2)}) collective-permute-start(bf16[32,16,256]{2,1,0:T(8,128)(2,1)} %get-tuple-element.44), channel_id=1, source_target_pairs={{0,6},{2,4},{4,2},{6,0},{8,14},{10,12},{12,10},{14,8},{1,7},{3,5},... | collective-permute-start | bytes 786440 | tf_op jit(solution)/shard_map/ppermute | solution.py:408
  22.1 34.9 %all-to-all-start.1 = ((bf16[8,16,16,256]{3,2,1,0:T(8,128)(2,1)}), bf16[8,16,16,256]{3,2,1,0:T(8,128)(2,1)}, u32[]{:S(2)}, u32[]{:S(2)}) async-start(bf16[8,16,16,256]{3,2,1,0:T(8,128)(2,1)} %get-tuple-element.57), calls=%async_computation.1 | async-start | bytes 2097152 | tf_op jit(solution)/shard_map/all_to_all | solution.py:447
  39.7 1.1 %collective-permute-start.12 = (f32[4]{0:T(128)S(1)}, f32[4]{0:T(128)S(1)}, u32[]{:S(2)}, u32[]{:S(2)}) collective-permute-start(f32[4]{0:T(128)S(1)} %copy-done.6), channel_id=1, source_target_pairs={{0,1},{1,0},{2,3},{3,2},{4,5},{5,4},{6,7},{7,6},{8,9},{9,8},{10,11... | collective-permute-start | bytes 56 | tf_op jit(solution)/shard_map/ppermute | solution.py:405
  39.7 3.7 %collective-permute-start.11 = (f32[1024]{0:T(1024)}, f32[1024]{0:T(1024)}, u32[]{:S(2)}, u32[]{:S(2)}) collective-permute-start(f32[1024]{0:T(1024)} %param.24), channel_id=1, source_target_pairs={{0,1},{1,0},{2,3},{3,2},{4,5},{5,4},{6,7},{7,6},{8,9},{9,8},{10,11... | collective-permute-start | bytes 12296 | tf_op jit(solution)/shard_map/ppermute | solution.py:405
  40.2 3.4 %collective-permute-start.6 = (bf16[512,256]{1,0:T(8,128)(2,1)}, bf16[512,256]{1,0:T(8,128)(2,1)}, u32[]{:S(2)}, u32[]{:S(2)}) collective-permute-start(bf16[512,256]{1,0:T(8,128)(2,1)} %refs_5_.1), channel_id=1, source_target_pairs={{0,1},{1,0},{2,3},{3,2},{4,5},{5,4},{6,7},{7,6},{8,9},{9,8},{10,11... | collective-permute-start | bytes 786440 | tf_op jit(solution)/shard_map/ppermute | solution.py:405
  40.2 18.8 %collective-permute-start.7 = (bf16[512,256]{1,0:T(8,128)(2,1)}, bf16[512,256]{1,0:T(8,128)(2,1)}, u32[]{:S(2)}, u32[]{:S(2)}) collective-permute-start(bf16[512,256]{1,0:T(8,128)(2,1)} %refs_7_.1), channel_id=1, source_target_pairs={{0,1},{1,0},{2,3},{3,2},{4,5},{5,4},{6,7},{7,6},{8,9},{9,8},{10,11... | collective-permute-start | bytes 786440 | tf_op jit(solution)/shard_map/ppermute | solution.py:405
  40.7 20.9 %collective-permute-start.9 = (bf16[512,1024]{1,0:T(8,128)(2,1)}, bf16[512,1024]{1,0:T(8,128)(2,1)}, u32[]{:S(2)}, u32[]{:S(2)}) collective-permute-start(bf16[512,1024]{1,0:T(8,128)(2,1)} %refs_11_.1), channel_id=1, source_target_pairs={{0,1},{1,0},{2,3},{3,2},{4,5},{5,4},{6,7},{7,6},{8,9},{9,8},{10,11... | collective-permute-start | bytes 3145736 | tf_op jit(solution)/shard_map/ppermute | solution.py:405
  41.3 20.3 %collective-permute-start.10 = (bf16[1024,512]{1,0:T(8,128)(2,1)}, bf16[1024,512]{1,0:T(8,128)(2,1)}, u32[]{:S(2)}, u32[]{:S(2)}) collective-permute-start(bf16[1024,512]{1,0:T(8,128)(2,1)} %refs_15_.1), channel_id=1, source_target_pairs={{0,1},{1,0},{2,3},{3,2},{4,5},{5,4},{6,7},{7,6},{8,9},{9,8},{10,11... | collective-permute-start | bytes 3145736 | tf_op jit(solution)/shard_map/ppermute | solution.py:405
  41.8 1.6 %copy-start.3 = (bf16[256,512]{1,0:T(8,128)(2,1)S(1)}, bf16[256,512]{1,0:T(8,128)(2,1)}, u32[]{:S(2)}) copy-start(bf16[256,512]{1,0:T(8,128)(2,1)} %refs_9_.1) | copy-start | bytes 786436
  41.8 15.2 %copy-start.2 = (s32[1,128]{1,0:T(1,128)S(1)}, s32[1,128]{1,0:T(1,128)}, u32[]{:S(2)}) copy-start(s32[1,128]{1,0:T(1,128)} %get-tuple-element.38.list_ref) | copy-start | bytes 1540
  43.4 19.8 %copy-start.4 = (f32[512]{0:T(512)S(1)}, f32[512]{0:T(512)}, u32[]{:S(2)}) copy-start(f32[512]{0:T(512)} %param.17) | copy-start | bytes 6148
  43.4 19.8 %copy-start.5 = (f32[512]{0:T(512)S(1)}, f32[512]{0:T(512)}, u32[]{:S(2)}) copy-start(f32[512]{0:T(512)} %param.22) | copy-start | bytes 6148
  43.4 19.8 %copy-start.7 = (f32[4]{0:T(128)S(1)}, f32[4]{0:T(128)}, u32[]{:S(2)}) copy-start(f32[4]{0:T(128)} %scale_a_ref.1) | copy-start | bytes 52
  43.4 19.8 %copy-start.9 = (f32[4]{0:T(128)S(1)}, f32[4]{0:T(128)}, u32[]{:S(2)}) copy-start(f32[4]{0:T(128)} %copy-done.8) | copy-start | bytes 52
  43.4 15.7 %collective-permute-start.8 = (bf16[256,512]{1,0:T(8,128)(2,1)S(1)}, bf16[256,512]{1,0:T(8,128)(2,1)S(1)}, u32[]{:S(2)}, u32[]{:S(2)}) collective-permute-start(bf16[256,512]{1,0:T(8,128)(2,1)S(1)} %copy-done.3), channel_id=1, source_target_pairs={{0,1},{1,0},{2,3},{3,2},{4,5},{5,4},{6,7},{7,6},{8,9},{9,8},{10,11... | collective-permute-start | bytes 786440 | tf_op jit(solution)/shard_map/ppermute | solution.py:405
  43.6 18.1 %collective-permute-start.5 = (bf16[32,16,256]{2,1,0:T(8,128)(2,1)S(1)}, bf16[32,16,256]{2,1,0:T(8,128)(2,1)S(1)}, u32[]{:S(2)}, u32[]{:S(2)}) collective-permute-start(bf16[32,16,256]{2,1,0:T(8,128)(2,1)S(1)} %get-tuple-element.45), channel_id=1, source_target_pairs={{0,8},{2,10},{4,12},{6,14},{8,0},{10,2},{12,4},{14,6},{1,9},{3,11}... | collective-permute-start | bytes 786440 | tf_op jit(solution)/shard_map/ppermute | solution.py:408
  59.0 4.2 %collective-permute-start.14 = (bf16[64,16,256]{2,1,0:T(8,128)(2,1)S(1)}, bf16[64,16,256]{2,1,0:T(8,128)(2,1)S(1)}, u32[]{:S(2)}, u32[]{:S(2)}) collective-permute-start(bf16[64,16,256]{2,1,0:T(8,128)(2,1)S(1)} %get-tuple-element.59), channel_id=1, source_target_pairs={{0,1},{1,0},{2,3},{3,2},{4,5},{5,4},{6,7},{7,6},{8,9},{9,8},{10,11... | collective-permute-start | bytes 1572872 | tf_op jit(solution)/shard_map/ppermute | solution.py:405
  61.7 1.5 %collective-permute-start.13 = (bf16[32,16,256]{2,1,0:T(8,128)(2,1)S(1)}, bf16[32,16,256]{2,1,0:T(8,128)(2,1)S(1)}, u32[]{:S(2)}, u32[]{:S(2)}) collective-permute-start(bf16[32,16,256]{2,1,0:T(8,128)(2,1)S(1)} %collective-permute-done.5.refs_0_), channel_id=1, source_target_pairs={{0,1},{1,0},{2,3},{3,2},{4,5},{5,4},{6,7},{7,6},{8,9},{9,8},{10,11... | collective-permute-start | bytes 786440 | tf_op jit(solution)/shard_map/ppermute | solution.py:405
  76.4 1.3 %collective-permute-start.15 = (bf16[64,512]{1,0:T(8,128)(2,1)S(1)}, bf16[64,512]{1,0:T(8,128)(2,1)S(1)}, u32[]{:S(2)}, u32[]{:S(2)}) collective-permute-start(bf16[64,512]{1,0:T(8,128)(2,1)S(1)} %shard_map.122), channel_id=1, source_target_pairs={{0,1},{1,0},{2,3},{3,2},{4,5},{5,4},{6,7},{7,6},{8,9},{9,8},{10,11... | collective-permute-start | bytes 196616 | tf_op jit(solution)/shard_map/ppermute | solution.py:405
  (1 other events, 0.5 us)

commit v9 on v8

--- a/solution.py
+++ b/solution.py
@@ -318,14 +318,19 @@
         normed_ref[here, :] = norm_rows(hidden, gain_mlp_ref[...]).astype(jnp.bfloat16)
         yield
 
+    row_pair = lax.broadcasted_iota(jnp.int32, (2 * BLOCK, rows), 1) % half // length
+    pool = jnp.where(row_pair == lax.broadcasted_iota(jnp.int32, row_pair.shape, 0), 1.0, 0.0)
+    pool = pool.astype(jnp.bfloat16)
+
     def expand(step):
         here = span(step, rows)
         for at in range(0, 2 * units, 256):
             cut = pl.ds(at, 256)
             inner = dot(normed_ref[here, :], in_ref[:, cut]) + bias_ref[:, cut]
-            bent = jnp.tanh(inner * (0.7978845608028654 + 0.035677408136300125 * (inner * inner)))
-            bent = (inner * bent + inner).reshape(2, BLOCK, length, -1)
-            pooled_ref[span(step, BLOCK), cut] = jnp.sum(bent, axis=(0, 2))
+            inner = inner.astype(jnp.bfloat16)
+            cubic = inner * inner * jnp.bfloat16(0.0356774081) + jnp.bfloat16(0.7978845608)
+            bent = (jnp.tanh(inner * cubic) + jnp.bfloat16(1.0)) * inner
+            pooled_ref[span(step, BLOCK), cut] = dot(pool, bent)[:BLOCK]
             yield
 
     for load in token_loads:

time: 78.7 us -> 84.3 us (1.071)
  Pallas kernels: 21.7 us -> 27.3 us
    pallas_call x1, Pallas kernels: 13.2 us -> 18.7 us  [on_device(): pl.pallas_call(functools.partial(compare_kernel, plan, length, head_dim),...]
  transfers between devices with their start and end apart: 15 -> 15, of which waited for: 8 -> 8; matrix products, arithmetic and copies ran while one was open for 0% -> 0% of each run, Pallas kernels for 5% -> 4%
where the time goes in v9:
time: 84.3 us; the launch traced here: 83.9 us
  waiting for transfers between devices  31.2 us (37%)
  Pallas kernels  27.3 us (32%)
  blocking collectives  13.6 us (16%)
  starting transfers between devices  9.65 us (11%)
    pallas_call x1, Pallas kernels, on_device(): pl.pallas_call(functools.partial(compare_kernel, plan, length, head_dim),...  18.7 us
    ppermute x4, waiting for transfers between devices, across(): lax.ppermute(values, 'shard', [(k, k ^ distance) for k in range(owner_cou...  15.9 us
    all_to_all x1, blocking collectives, on_device(): lax.all_to_all(wanted, 'shard', split_axis=0, concat_axis=0, tiled=True)  13.6 us
    all_to_all x1, waiting for transfers between devices, on_device(): lax.all_to_all(served, 'shard', split_axis=0, concat_axis=0, tiled=True)  13.4 us
    all_to_all x1, starting transfers between devices, on_device(): lax.all_to_all(served, 'shard', split_axis=0, concat_axis=0, tiled=True)  4.24 us
    ppermute x4, starting transfers between devices, across(): lax.ppermute(values, 'shard', [(k, k ^ distance) for k in range(owner_cou...  3.56 us
    pallas_call x1, Pallas kernels, on_device(): pl.pallas_call(functools.partial(serve_kernel, plan), out_shape=[images(2...  3.17 us
    pallas_call x1, Pallas kernels, on_device(): pl.pallas_call(functools.partial(pick_kernel, plan), out_shape=[images(pa...  1.99 us
  transfers between devices with their start and end apart: 15, of which 8 were waited for; matrix products, arithmetic and copies ran while one was open for 0% of the time, Pallas kernels for 4%

profile of v9, /device:TPU:0, one launch (start us, length us, event | category | flops | bytes accessed | tf_op | source)
XLA Modules:
  0.0 83.9 jit_solution(10092363592668861067)
XLA Ops:
  0.0 1.8 %shard_map.118 = (s32[8,1,36]{2,1,0:T(1,128)}, s32[1,128]{1,0:T(1,128)}) custom-call(s32[1]{0:T(128)} %bitcast.4.shard_ref, s32[2,64]{1,0:T(2,128)} %bitcast.18, s32[2,64]{1,0:T(2,128)} %bitcast.19), custom_call_target="tpu_custom_call" | custom-call | tf_op jit(solution)/shard_map/pallas_call | solution.py:425
  1.8 13.6 %all_to_all.10.incoming_ref = s32[8,1,36]{2,1,0:T(1,128)} all-to-all(s32[8,1,36]{2,1,0:T(1,128)} %get-tuple-element.39), channel_id=1, replica_groups=mesh['groups'=2,'shard'=8,'mp'=2] {'shard'}, dimensions={0} | all-to-all | bytes 2304 | tf_op jit(solution)/shard_map/all_to_all | solution.py:433
  15.4 3.2 %shard_map.119 = (bf16[32,16,256]{2,1,0:T(8,128)(2,1)}, bf16[32,16,256]{2,1,0:T(8,128)(2,1)}, bf16[32,16,256]{2,1,0:T(8,128)(2,1)}, bf16[32,16,256]{2,1,0:T(8,12...) custom-call(s32[1]{0:T(128)} %bitcast.4.shard_ref, s32[8,1,36]{2,1,0:T(1,128)} %all_to_all.10.incoming_ref, ...), custom_call_target="tpu_custom_call" | custom-call | tf_op jit(solution)/shard_map/pallas_call | solution.py:443
  18.6 0.6 collective-permute-start.2
  19.2 0.6 collective-permute-start.3
  19.8 2.4 %collective-permute-start.4 = (bf16[32,16,256]{2,1,0:T(8,128)(2,1)}, bf16[32,16,256]{2,1,0:T(8,128)(2,1)S(1)}, u32[]{:S(2)}, u32[]{:S(2)}) collective-permute-start(bf16[32,16,256]{2,1,0:T(8,128)(2,1)} %get-tuple-element.44), channel_id=1, source_target_pairs={{0,6},{2,4},{4,2},{6,0},{8,14},{10,12},{12,10},{14,8},{1,7},{3,5},... | collective-permute-start | bytes 786440 | tf_op jit(solution)/shard_map/ppermute | solution.py:413
  22.1 4.2 %all-to-all-start.1 = ((bf16[8,16,16,256]{3,2,1,0:T(8,128)(2,1)}), bf16[8,16,16,256]{3,2,1,0:T(8,128)(2,1)}, u32[]{:S(2)}, u32[]{:S(2)}) async-start(bf16[8,16,16,256]{3,2,1,0:T(8,128)(2,1)} %get-tuple-element.57), calls=%async_computation.1 | async-start | bytes 2097152 | tf_op jit(solution)/shard_map/all_to_all | solution.py:452
  26.4 1.1 %collective-permute-done.2.refs_1_.refs_2_ = bf16[32,16,256]{2,1,0:T(8,128)(2,1)S(1)} collective-permute-done((bf16[32,16,256]{2,1,0:T(8,128)(2,1)}, bf16[32,16,256]{2,1,0:T(8,128)(2,1)S(1)}, u32[]{:S(2)}, u32[]{:S(2)}) %collective-permute-start.2) | collective-permute-done | bytes 262176 | tf_op jit(solution)/shard_map/ppermute | solution.py:413
  27.5 1.2 %collective-permute-done.3.refs_2_.refs_3_ = bf16[32,16,256]{2,1,0:T(8,128)(2,1)S(1)} collective-permute-done((bf16[32,16,256]{2,1,0:T(8,128)(2,1)}, bf16[32,16,256]{2,1,0:T(8,128)(2,1)S(1)}, u32[]{:S(2)}, u32[]{:S(2)}) %collective-permute-start.3) | collective-permute-done | bytes 262176 | tf_op jit(solution)/shard_map/ppermute | solution.py:413
  28.6 11.0 %collective-permute-done.4.refs_3_.refs_4_ = bf16[32,16,256]{2,1,0:T(8,128)(2,1)S(1)} collective-permute-done((bf16[32,16,256]{2,1,0:T(8,128)(2,1)}, bf16[32,16,256]{2,1,0:T(8,128)(2,1)S(1)}, u32[]{:S(2)}, u32[]{:S(2)}) %collective-permute-start.4) | collective-permute-done | bytes 262176 | tf_op jit(solution)/shard_map/ppermute | solution.py:413
  39.7 0.5 collective-permute-start.11
  40.2 0.5 collective-permute-start.7
  40.8 0.5 copy-done.8
  41.3 0.4 collective-permute-start.10
  41.8 1.6 %shard_map.120 = (bf16[32,16,256]{2,1,0:T(8,128)(2,1)S(1)}, bf16[2,32,16,256]{3,2,1,0:T(8,128)(2,1)}) custom-call(s32[1]{0:T(128)} %bitcast.4.shard_ref, s32[8,1,36]{2,1,0:T(1,128)S(1)} %copy-done.1, bf16[32,16,256]{2,1,0:T(8,128)(2,1)S(1)} %copy-done, bf16[32,16,256]{2,1,0:T(8,128)(2,1)S(1)} %collective-permute-done.2.refs_1_.refs_2_, ...), custom_call_target="tpu_custom_call" | custom-call | flops 199999995904 | bytes 1048576 | tf_op jit(solution)/shard_map/pallas_call | solution.py:454
  43.6 13.4 %all-to-all-done.1 = bf16[8,16,16,256]{3,2,1,0:T(8,128)(2,1)} async-done(((bf16[8,16,16,256]{3,2,1,0:T(8,128)(2,1)}), bf16[8,16,16,256]{3,2,1,0:T(8,128)(2,1)}, u32[]{:S(2)}, u32[]{:S(2)}) %all-to-all-start.1) | async-done | bytes 1048608 | tf_op jit(solution)/shard_map/all_to_all | solution.py:452
  57.0 2.0 %shard_map.121 = (bf16[64,16,256]{2,1,0:T(8,128)(2,1)S(1)}, bf16[64,16,256]{2,1,0:T(8,128)(2,1)S(1)}) custom-call(s32[1]{0:T(128)} %bitcast.3.core_ref, s32[1,128]{1,0:T(1,128)S(1)} %copy-done.2, bf16[128,16,256]{2,1,0:T(8,128)(2,1)} %bitcast.10.refs_0_, bf16[32,16,256]{2,1,0:T(8,128)(2,1)S(1)} %copy-done, ...), custom_call_target="tpu_custom_call" | custom-call | tf_op jit(solution)/shard_map/pallas_call | solution.py:469
  59.1 2.6 %collective-permute-done.5.refs_0_ = bf16[32,16,256]{2,1,0:T(8,128)(2,1)S(1)} collective-permute-done((bf16[32,16,256]{2,1,0:T(8,128)(2,1)S(1)}, bf16[32,16,256]{2,1,0:T(8,128)(2,1)S(1)}, u32[]{:S(2)}, u32[]{:S(2)}) %collective-permute-start.5) | collective-permute-done | bytes 262176 | tf_op jit(solution)/shard_map/ppermute | solution.py:413
  62.3 0.2 conditional.1
  62.5 0.7 collective-permute-done.13.refs_1_
  63.2 18.7 %shard_map.122 = bf16[64,512]{1,0:T(8,128)(2,1)S(1)} custom-call(s32[1]{0:T(128)} %bitcast.3.core_ref, s32[1,128]{1,0:T(1,128)S(1)} %copy-done.2, s32[1]{0:T(128)} %get-tuple-element.40.crowded_ref, f32[4]{0:T(128)S(1)} %copy-done.7, f32[4]{0:T(128)S(1)} %copy-done.9, f32[1,512]{1,0:T(1,128)S(1)} %bitcast.14, f32[1,512]{1,0:T(1,128)S(1)} %bitcast.15, ...), custom_call_target="tpu_custom_call" | custom-call | flops 3758096384 | bytes 8388608 | tf_op jit(solution)/shard_map/pallas_call | solution.py:496
  82.0 0.2 collective-permute-start.15
  82.2 1.1 %collective-permute-done.15 = bf16[64,512]{1,0:T(8,128)(2,1)S(1)} collective-permute-done((bf16[64,512]{1,0:T(8,128)(2,1)S(1)}, bf16[64,512]{1,0:T(8,128)(2,1)S(1)}, u32[]{:S(2)}, u32[]{:S(2)}) %collective-permute-start.15) | collective-permute-done | bytes 65568 | tf_op jit(solution)/shard_map/ppermute | solution.py:410
  83.3 0.6 add.3
  (34 shorter events, 0.4 us)
Async XLA Ops:
  15.4 24.3 %copy-start.6 = (f32[4]{0:T(128)S(1)}, f32[4]{0:T(128)}, u32[]{:S(2)}) copy-start(f32[4]{0:T(128)} %scale_a_ref.1) | copy-start | bytes 52
  15.4 26.4 %copy-start.1 = (s32[8,1,36]{2,1,0:T(1,128)S(1)}, s32[8,1,36]{2,1,0:T(1,128)}, u32[]{:S(2)}) copy-start(s32[8,1,36]{2,1,0:T(1,128)} %all_to_all.10.incoming_ref) | copy-start | bytes 3460
  18.6 23.2 %copy-start = (bf16[32,16,256]{2,1,0:T(8,128)(2,1)S(1)}, bf16[32,16,256]{2,1,0:T(8,128)(2,1)}, u32[]{:S(2)}) copy-start(bf16[32,16,256]{2,1,0:T(8,128)(2,1)} %get-tuple-element.41.refs_0_.refs_1_) | copy-start | bytes 786436
  18.6 8.9 %collective-permute-start.2 = (bf16[32,16,256]{2,1,0:T(8,128)(2,1)}, bf16[32,16,256]{2,1,0:T(8,128)(2,1)S(1)}, u32[]{:S(2)}, u32[]{:S(2)}) collective-permute-start(bf16[32,16,256]{2,1,0:T(8,128)(2,1)} %get-tuple-element.42), channel_id=1, source_target_pairs={{0,2},{2,0},{4,6},{6,4},{8,10},{10,8},{12,14},{14,12},{1,3},{3,1},... | collective-permute-start | bytes 786440 | tf_op jit(solution)/shard_map/ppermute | solution.py:413
  19.2 9.5 %collective-permute-start.3 = (bf16[32,16,256]{2,1,0:T(8,128)(2,1)}, bf16[32,16,256]{2,1,0:T(8,128)(2,1)S(1)}, u32[]{:S(2)}, u32[]{:S(2)}) collective-permute-start(bf16[32,16,256]{2,1,0:T(8,128)(2,1)} %get-tuple-element.43), channel_id=1, source_target_pairs={{0,4},{2,6},{4,0},{6,2},{8,12},{10,14},{12,8},{14,10},{1,5},{3,7},... | collective-permute-start | bytes 786440 | tf_op jit(solution)/shard_map/ppermute | solution.py:413
  19.8 19.9 %collective-permute-start.4 = (bf16[32,16,256]{2,1,0:T(8,128)(2,1)}, bf16[32,16,256]{2,1,0:T(8,128)(2,1)S(1)}, u32[]{:S(2)}, u32[]{:S(2)}) collective-permute-start(bf16[32,16,256]{2,1,0:T(8,128)(2,1)} %get-tuple-element.44), channel_id=1, source_target_pairs={{0,6},{2,4},{4,2},{6,0},{8,14},{10,12},{12,10},{14,8},{1,7},{3,5},... | collective-permute-start | bytes 786440 | tf_op jit(solution)/shard_map/ppermute | solution.py:413
  22.1 34.9 %all-to-all-start.1 = ((bf16[8,16,16,256]{3,2,1,0:T(8,128)(2,1)}), bf16[8,16,16,256]{3,2,1,0:T(8,128)(2,1)}, u32[]{:S(2)}, u32[]{:S(2)}) async-start(bf16[8,16,16,256]{3,2,1,0:T(8,128)(2,1)} %get-tuple-element.57), calls=%async_computation.1 | async-start | bytes 2097152 | tf_op jit(solution)/shard_map/all_to_all | solution.py:452
  39.7 1.1 %collective-permute-start.12 = (f32[4]{0:T(128)S(1)}, f32[4]{0:T(128)S(1)}, u32[]{:S(2)}, u32[]{:S(2)}) collective-permute-start(f32[4]{0:T(128)S(1)} %copy-done.6), channel_id=1, source_target_pairs={{0,1},{1,0},{2,3},{3,2},{4,5},{5,4},{6,7},{7,6},{8,9},{9,8},{10,11... | collective-permute-start | bytes 56 | tf_op jit(solution)/shard_map/ppermute | solution.py:410
  39.7 3.7 %collective-permute-start.11 = (f32[1024]{0:T(1024)}, f32[1024]{0:T(1024)}, u32[]{:S(2)}, u32[]{:S(2)}) collective-permute-start(f32[1024]{0:T(1024)} %param.24), channel_id=1, source_target_pairs={{0,1},{1,0},{2,3},{3,2},{4,5},{5,4},{6,7},{7,6},{8,9},{9,8},{10,11... | collective-permute-start | bytes 12296 | tf_op jit(solution)/shard_map/ppermute | solution.py:410
  40.2 3.4 %collective-permute-start.6 = (bf16[512,256]{1,0:T(8,128)(2,1)}, bf16[512,256]{1,0:T(8,128)(2,1)}, u32[]{:S(2)}, u32[]{:S(2)}) collective-permute-start(bf16[512,256]{1,0:T(8,128)(2,1)} %refs_5_.1), channel_id=1, source_target_pairs={{0,1},{1,0},{2,3},{3,2},{4,5},{5,4},{6,7},{7,6},{8,9},{9,8},{10,11... | collective-permute-start | bytes 786440 | tf_op jit(solution)/shard_map/ppermute | solution.py:410
  40.2 18.8 %collective-permute-start.7 = (bf16[512,256]{1,0:T(8,128)(2,1)}, bf16[512,256]{1,0:T(8,128)(2,1)}, u32[]{:S(2)}, u32[]{:S(2)}) collective-permute-start(bf16[512,256]{1,0:T(8,128)(2,1)} %refs_7_.1), channel_id=1, source_target_pairs={{0,1},{1,0},{2,3},{3,2},{4,5},{5,4},{6,7},{7,6},{8,9},{9,8},{10,11... | collective-permute-start | bytes 786440 | tf_op jit(solution)/shard_map/ppermute | solution.py:410
  40.7 20.9 %collective-permute-start.9 = (bf16[512,1024]{1,0:T(8,128)(2,1)}, bf16[512,1024]{1,0:T(8,128)(2,1)}, u32[]{:S(2)}, u32[]{:S(2)}) collective-permute-start(bf16[512,1024]{1,0:T(8,128)(2,1)} %refs_11_.1), channel_id=1, source_target_pairs={{0,1},{1,0},{2,3},{3,2},{4,5},{5,4},{6,7},{7,6},{8,9},{9,8},{10,11... | collective-permute-start | bytes 3145736 | tf_op jit(solution)/shard_map/ppermute | solution.py:410
  41.3 20.3 %collective-permute-start.10 = (bf16[1024,512]{1,0:T(8,128)(2,1)}, bf16[1024,512]{1,0:T(8,128)(2,1)}, u32[]{:S(2)}, u32[]{:S(2)}) collective-permute-start(bf16[1024,512]{1,0:T(8,128)(2,1)} %refs_15_.1), channel_id=1, source_target_pairs={{0,1},{1,0},{2,3},{3,2},{4,5},{5,4},{6,7},{7,6},{8,9},{9,8},{10,11... | collective-permute-start | bytes 3145736 | tf_op jit(solution)/shard_map/ppermute | solution.py:410
  41.8 1.7 %copy-start.3 = (bf16[256,512]{1,0:T(8,128)(2,1)S(1)}, bf16[256,512]{1,0:T(8,128)(2,1)}, u32[]{:S(2)}) copy-start(bf16[256,512]{1,0:T(8,128)(2,1)} %refs_9_.1) | copy-start | bytes 786436
  41.8 15.2 %copy-start.2 = (s32[1,128]{1,0:T(1,128)S(1)}, s32[1,128]{1,0:T(1,128)}, u32[]{:S(2)}) copy-start(s32[1,128]{1,0:T(1,128)} %get-tuple-element.38.list_ref) | copy-start | bytes 1540
  43.4 19.8 %copy-start.4 = (f32[512]{0:T(512)S(1)}, f32[512]{0:T(512)}, u32[]{:S(2)}) copy-start(f32[512]{0:T(512)} %param.17) | copy-start | bytes 6148
  43.4 19.8 %copy-start.5 = (f32[512]{0:T(512)S(1)}, f32[512]{0:T(512)}, u32[]{:S(2)}) copy-start(f32[512]{0:T(512)} %param.22) | copy-start | bytes 6148
  43.4 19.8 %copy-start.7 = (f32[4]{0:T(128)S(1)}, f32[4]{0:T(128)}, u32[]{:S(2)}) copy-start(f32[4]{0:T(128)} %scale_a_ref.1) | copy-start | bytes 52
  43.4 19.8 %copy-start.9 = (f32[4]{0:T(128)S(1)}, f32[4]{0:T(128)}, u32[]{:S(2)}) copy-start(f32[4]{0:T(128)} %copy-done.8) | copy-start | bytes 52
  43.4 15.7 %collective-permute-start.8 = (bf16[256,512]{1,0:T(8,128)(2,1)S(1)}, bf16[256,512]{1,0:T(8,128)(2,1)S(1)}, u32[]{:S(2)}, u32[]{:S(2)}) collective-permute-start(bf16[256,512]{1,0:T(8,128)(2,1)S(1)} %copy-done.3), channel_id=1, source_target_pairs={{0,1},{1,0},{2,3},{3,2},{4,5},{5,4},{6,7},{7,6},{8,9},{9,8},{10,11... | collective-permute-start | bytes 786440 | tf_op jit(solution)/shard_map/ppermute | solution.py:410
  43.6 18.1 %collective-permute-start.5 = (bf16[32,16,256]{2,1,0:T(8,128)(2,1)S(1)}, bf16[32,16,256]{2,1,0:T(8,128)(2,1)S(1)}, u32[]{:S(2)}, u32[]{:S(2)}) collective-permute-start(bf16[32,16,256]{2,1,0:T(8,128)(2,1)S(1)} %get-tuple-element.45), channel_id=1, source_target_pairs={{0,8},{2,10},{4,12},{6,14},{8,0},{10,2},{12,4},{14,6},{1,9},{3,11}... | collective-permute-start | bytes 786440 | tf_op jit(solution)/shard_map/ppermute | solution.py:413
  59.0 4.2 %collective-permute-start.14 = (bf16[64,16,256]{2,1,0:T(8,128)(2,1)S(1)}, bf16[64,16,256]{2,1,0:T(8,128)(2,1)S(1)}, u32[]{:S(2)}, u32[]{:S(2)}) collective-permute-start(bf16[64,16,256]{2,1,0:T(8,128)(2,1)S(1)} %get-tuple-element.59), channel_id=1, source_target_pairs={{0,1},{1,0},{2,3},{3,2},{4,5},{5,4},{6,7},{7,6},{8,9},{9,8},{10,11... | collective-permute-start | bytes 1572872 | tf_op jit(solution)/shard_map/ppermute | solution.py:410
  61.7 1.5 %collective-permute-start.13 = (bf16[32,16,256]{2,1,0:T(8,128)(2,1)S(1)}, bf16[32,16,256]{2,1,0:T(8,128)(2,1)S(1)}, u32[]{:S(2)}, u32[]{:S(2)}) collective-permute-start(bf16[32,16,256]{2,1,0:T(8,128)(2,1)S(1)} %collective-permute-done.5.refs_0_), channel_id=1, source_target_pairs={{0,1},{1,0},{2,3},{3,2},{4,5},{5,4},{6,7},{7,6},{8,9},{9,8},{10,11... | collective-permute-start | bytes 786440 | tf_op jit(solution)/shard_map/ppermute | solution.py:410
  82.0 1.3 %collective-permute-start.15 = (bf16[64,512]{1,0:T(8,128)(2,1)S(1)}, bf16[64,512]{1,0:T(8,128)(2,1)S(1)}, u32[]{:S(2)}, u32[]{:S(2)}) collective-permute-start(bf16[64,512]{1,0:T(8,128)(2,1)S(1)} %shard_map.122), channel_id=1, source_target_pairs={{0,1},{1,0},{2,3},{3,2},{4,5},{5,4},{6,7},{7,6},{8,9},{9,8},{10,11... | collective-permute-start | bytes 196616 | tf_op jit(solution)/shard_map/ppermute | solution.py:410
  (1 other events, 0.5 us)

commit v10 on v8

--- a/solution.py
+++ b/solution.py
@@ -257,8 +257,6 @@
             [jnp.where(even, values, zero), jnp.where(even, zero, values)], axis=0
         )
 
-    ones = split(jnp.ones((half, pair_dim), jnp.bfloat16))
-
     def begin(step):
         images = pl.ds(step * 2 * BLOCK, 2 * BLOCK)
         tokens = jnp.concatenate(
@@ -278,16 +276,14 @@
     def weigh(scores, factor):
         scores = jnp.where(same, scores, -1e30)
         top = jnp.max(scores, axis=1, keepdims=True)
-        return jnp.exp2((scores - top) * factor).astype(jnp.bfloat16)
+        weights = jnp.exp2((scores - top) * factor)
+        return (weights * (1.0 / jnp.sum(weights, axis=1, keepdims=True))).astype(jnp.bfloat16)
 
     def mix(query, key, value, factors):
         scores = dot_nt(query, split(key))
         weights = [weigh(scores[:, k * half : (k + 1) * half], factors[k]) for k in range(2)]
-        mixed = dot(jnp.concatenate(weights, axis=1), jnp.concatenate([split(value), ones], axis=1))
-        total = mixed[:, pair_dim:]
-        inverse = pl.reciprocal(total, approx=True)
-        inverse = inverse * (2.0 - total * inverse)
-        return (mixed[:, :pair_dim] * inverse).astype(jnp.bfloat16)
+        mixed = dot(jnp.concatenate(weights, axis=1), split(value))
+        return mixed.astype(jnp.bfloat16)
 
     def attend(step):
         for index in range(width // pair_dim):

time: 78.7 us -> 80 us (1.017)
  Pallas kernels: 21.7 us -> 23 us
    pallas_call x1, Pallas kernels: 13.2 us -> 14.5 us  [on_device(): pl.pallas_call(functools.partial(compare_kernel, plan, length, head_dim),...]
  transfers between devices with their start and end apart: 15 -> 15, of which waited for: 8 -> 8; matrix products, arithmetic and copies ran while one was open for 0% -> 0% of each run, Pallas kernels for 5% -> 4%
where the time goes in v10:
time: 80 us; the launch traced here: 79.7 us
  waiting for transfers between devices  31.3 us (39%)
  Pallas kernels  23 us (29%)
  blocking collectives  13.6 us (17%)
  starting transfers between devices  9.66 us (12%)
    ppermute x4, waiting for transfers between devices, across(): lax.ppermute(values, 'shard', [(k, k ^ distance) for k in range(owner_cou...  15.9 us
    pallas_call x1, Pallas kernels, on_device(): pl.pallas_call(functools.partial(compare_kernel, plan, length, head_dim),...  14.5 us
    all_to_all x1, blocking collectives, on_device(): lax.all_to_all(wanted, 'shard', split_axis=0, concat_axis=0, tiled=True)  13.6 us
    all_to_all x1, waiting for transfers between devices, on_device(): lax.all_to_all(served, 'shard', split_axis=0, concat_axis=0, tiled=True)  13.4 us
    all_to_all x1, starting transfers between devices, on_device(): lax.all_to_all(served, 'shard', split_axis=0, concat_axis=0, tiled=True)  4.24 us
    ppermute x4, starting transfers between devices, across(): lax.ppermute(values, 'shard', [(k, k ^ distance) for k in range(owner_cou...  3.56 us
    pallas_call x1, Pallas kernels, on_device(): pl.pallas_call(functools.partial(serve_kernel, plan), out_shape=[images(2...  3.17 us
    pallas_call x1, Pallas kernels, on_device(): pl.pallas_call(functools.partial(pick_kernel, plan), out_shape=[images(pa...  1.99 us
  transfers between devices with their start and end apart: 15, of which 8 were waited for; matrix products, arithmetic and copies ran while one was open for 0% of the time, Pallas kernels for 4%

profile of v10, /device:TPU:0, one launch (start us, length us, event | category | flops | bytes accessed | tf_op | source)
XLA Modules:
  0.0 79.7 jit_solution(16679087951378051175)
XLA Ops:
  0.0 1.8 %shard_map.118 = (s32[8,1,36]{2,1,0:T(1,128)}, s32[1,128]{1,0:T(1,128)}) custom-call(s32[1]{0:T(128)} %bitcast.4.shard_ref, s32[2,64]{1,0:T(2,128)} %bitcast.18, s32[2,64]{1,0:T(2,128)} %bitcast.19), custom_call_target="tpu_custom_call" | custom-call | tf_op jit(solution)/shard_map/pallas_call | solution.py:416
  1.8 13.6 %all_to_all.10.incoming_ref = s32[8,1,36]{2,1,0:T(1,128)} all-to-all(s32[8,1,36]{2,1,0:T(1,128)} %get-tuple-element.39), channel_id=1, replica_groups=mesh['groups'=2,'shard'=8,'mp'=2] {'shard'}, dimensions={0} | all-to-all | bytes 2304 | tf_op jit(solution)/shard_map/all_to_all | solution.py:424
  15.4 3.2 %shard_map.119 = (bf16[32,16,256]{2,1,0:T(8,128)(2,1)}, bf16[32,16,256]{2,1,0:T(8,128)(2,1)}, bf16[32,16,256]{2,1,0:T(8,128)(2,1)}, bf16[32,16,256]{2,1,0:T(8,12...) custom-call(s32[1]{0:T(128)} %bitcast.4.shard_ref, s32[8,1,36]{2,1,0:T(1,128)} %all_to_all.10.incoming_ref, ...), custom_call_target="tpu_custom_call" | custom-call | tf_op jit(solution)/shard_map/pallas_call | solution.py:434
  18.6 0.6 collective-permute-start.2
  19.2 0.6 collective-permute-start.3
  19.8 2.4 %collective-permute-start.4 = (bf16[32,16,256]{2,1,0:T(8,128)(2,1)}, bf16[32,16,256]{2,1,0:T(8,128)(2,1)S(1)}, u32[]{:S(2)}, u32[]{:S(2)}) collective-permute-start(bf16[32,16,256]{2,1,0:T(8,128)(2,1)} %get-tuple-element.44), channel_id=1, source_target_pairs={{0,6},{2,4},{4,2},{6,0},{8,14},{10,12},{12,10},{14,8},{1,7},{3,5},... | collective-permute-start | bytes 786440 | tf_op jit(solution)/shard_map/ppermute | solution.py:404
  22.1 4.2 %all-to-all-start.1 = ((bf16[8,16,16,256]{3,2,1,0:T(8,128)(2,1)}), bf16[8,16,16,256]{3,2,1,0:T(8,128)(2,1)}, u32[]{:S(2)}, u32[]{:S(2)}) async-start(bf16[8,16,16,256]{3,2,1,0:T(8,128)(2,1)} %get-tuple-element.57), calls=%async_computation.1 | async-start | bytes 2097152 | tf_op jit(solution)/shard_map/all_to_all | solution.py:443
  26.4 1.1 %collective-permute-done.2.refs_1_.refs_2_ = bf16[32,16,256]{2,1,0:T(8,128)(2,1)S(1)} collective-permute-done((bf16[32,16,256]{2,1,0:T(8,128)(2,1)}, bf16[32,16,256]{2,1,0:T(8,128)(2,1)S(1)}, u32[]{:S(2)}, u32[]{:S(2)}) %collective-permute-start.2) | collective-permute-done | bytes 262176 | tf_op jit(solution)/shard_map/ppermute | solution.py:404
  27.5 1.2 %collective-permute-done.3.refs_2_.refs_3_ = bf16[32,16,256]{2,1,0:T(8,128)(2,1)S(1)} collective-permute-done((bf16[32,16,256]{2,1,0:T(8,128)(2,1)}, bf16[32,16,256]{2,1,0:T(8,128)(2,1)S(1)}, u32[]{:S(2)}, u32[]{:S(2)}) %collective-permute-start.3) | collective-permute-done | bytes 262176 | tf_op jit(solution)/shard_map/ppermute | solution.py:404
  28.6 11.0 %collective-permute-done.4.refs_3_.refs_4_ = bf16[32,16,256]{2,1,0:T(8,128)(2,1)S(1)} collective-permute-done((bf16[32,16,256]{2,1,0:T(8,128)(2,1)}, bf16[32,16,256]{2,1,0:T(8,128)(2,1)S(1)}, u32[]{:S(2)}, u32[]{:S(2)}) %collective-permute-start.4) | collective-permute-done | bytes 262176 | tf_op jit(solution)/shard_map/ppermute | solution.py:404
  39.7 0.5 collective-permute-start.11
  40.2 0.5 collective-permute-start.7
  40.8 0.5 copy-done.8
  41.3 0.4 collective-permute-start.10
  41.8 1.6 %shard_map.120 = (bf16[32,16,256]{2,1,0:T(8,128)(2,1)S(1)}, bf16[2,32,16,256]{3,2,1,0:T(8,128)(2,1)}) custom-call(s32[1]{0:T(128)} %bitcast.4.shard_ref, s32[8,1,36]{2,1,0:T(1,128)S(1)} %copy-done.1, bf16[32,16,256]{2,1,0:T(8,128)(2,1)S(1)} %copy-done, bf16[32,16,256]{2,1,0:T(8,128)(2,1)S(1)} %collective-permute-done.2.refs_1_.refs_2_, ...), custom_call_target="tpu_custom_call" | custom-call | flops 199999995904 | bytes 1048576 | tf_op jit(solution)/shard_map/pallas_call | solution.py:445
  43.5 13.4 %all-to-all-done.1 = bf16[8,16,16,256]{3,2,1,0:T(8,128)(2,1)} async-done(((bf16[8,16,16,256]{3,2,1,0:T(8,128)(2,1)}), bf16[8,16,16,256]{3,2,1,0:T(8,128)(2,1)}, u32[]{:S(2)}, u32[]{:S(2)}) %all-to-all-start.1) | async-done | bytes 1048608 | tf_op jit(solution)/shard_map/all_to_all | solution.py:443
  57.0 2.0 %shard_map.121 = (bf16[64,16,256]{2,1,0:T(8,128)(2,1)S(1)}, bf16[64,16,256]{2,1,0:T(8,128)(2,1)S(1)}) custom-call(s32[1]{0:T(128)} %bitcast.3.core_ref, s32[1,128]{1,0:T(1,128)S(1)} %copy-done.2, bf16[128,16,256]{2,1,0:T(8,128)(2,1)} %bitcast.10.refs_0_, bf16[32,16,256]{2,1,0:T(8,128)(2,1)S(1)} %copy-done, ...), custom_call_target="tpu_custom_call" | custom-call | tf_op jit(solution)/shard_map/pallas_call | solution.py:460
  59.1 2.6 %collective-permute-done.5.refs_0_ = bf16[32,16,256]{2,1,0:T(8,128)(2,1)S(1)} collective-permute-done((bf16[32,16,256]{2,1,0:T(8,128)(2,1)S(1)}, bf16[32,16,256]{2,1,0:T(8,128)(2,1)S(1)}, u32[]{:S(2)}, u32[]{:S(2)}) %collective-permute-start.5) | collective-permute-done | bytes 262176 | tf_op jit(solution)/shard_map/ppermute | solution.py:404
  62.3 0.2 conditional.1
  62.5 0.7 collective-permute-done.13.refs_1_
  63.2 14.5 %shard_map.122 = bf16[64,512]{1,0:T(8,128)(2,1)S(1)} custom-call(s32[1]{0:T(128)} %bitcast.3.core_ref, s32[1,128]{1,0:T(1,128)S(1)} %copy-done.2, s32[1]{0:T(128)} %get-tuple-element.40.crowded_ref, f32[4]{0:T(128)S(1)} %copy-done.7, f32[4]{0:T(128)S(1)} %copy-done.9, f32[1,512]{1,0:T(1,128)S(1)} %bitcast.14, f32[1,512]{1,0:T(1,128)S(1)} %bitcast.15, ...), custom_call_target="tpu_custom_call" | custom-call | flops 3758096384 | bytes 8388608 | tf_op jit(solution)/shard_map/pallas_call | solution.py:487
  77.8 0.2 collective-permute-start.15
  78.0 1.1 %collective-permute-done.15 = bf16[64,512]{1,0:T(8,128)(2,1)S(1)} collective-permute-done((bf16[64,512]{1,0:T(8,128)(2,1)S(1)}, bf16[64,512]{1,0:T(8,128)(2,1)S(1)}, u32[]{:S(2)}, u32[]{:S(2)}) %collective-permute-start.15) | collective-permute-done | bytes 65568 | tf_op jit(solution)/shard_map/ppermute | solution.py:401
  79.1 0.6 add.3
  (34 shorter events, 0.4 us)
Async XLA Ops:
  15.4 24.3 %copy-start.6 = (f32[4]{0:T(128)S(1)}, f32[4]{0:T(128)}, u32[]{:S(2)}) copy-start(f32[4]{0:T(128)} %scale_a_ref.1) | copy-start | bytes 52
  15.4 26.4 %copy-start.1 = (s32[8,1,36]{2,1,0:T(1,128)S(1)}, s32[8,1,36]{2,1,0:T(1,128)}, u32[]{:S(2)}) copy-start(s32[8,1,36]{2,1,0:T(1,128)} %all_to_all.10.incoming_ref) | copy-start | bytes 3460
  18.6 23.2 %copy-start = (bf16[32,16,256]{2,1,0:T(8,128)(2,1)S(1)}, bf16[32,16,256]{2,1,0:T(8,128)(2,1)}, u32[]{:S(2)}) copy-start(bf16[32,16,256]{2,1,0:T(8,128)(2,1)} %get-tuple-element.41.refs_0_.refs_1_) | copy-start | bytes 786436
  18.6 8.9 %collective-permute-start.2 = (bf16[32,16,256]{2,1,0:T(8,128)(2,1)}, bf16[32,16,256]{2,1,0:T(8,128)(2,1)S(1)}, u32[]{:S(2)}, u32[]{:S(2)}) collective-permute-start(bf16[32,16,256]{2,1,0:T(8,128)(2,1)} %get-tuple-element.42), channel_id=1, source_target_pairs={{0,2},{2,0},{4,6},{6,4},{8,10},{10,8},{12,14},{14,12},{1,3},{3,1},... | collective-permute-start | bytes 786440 | tf_op jit(solution)/shard_map/ppermute | solution.py:404
  19.2 9.5 %collective-permute-start.3 = (bf16[32,16,256]{2,1,0:T(8,128)(2,1)}, bf16[32,16,256]{2,1,0:T(8,128)(2,1)S(1)}, u32[]{:S(2)}, u32[]{:S(2)}) collective-permute-start(bf16[32,16,256]{2,1,0:T(8,128)(2,1)} %get-tuple-element.43), channel_id=1, source_target_pairs={{0,4},{2,6},{4,0},{6,2},{8,12},{10,14},{12,8},{14,10},{1,5},{3,7},... | collective-permute-start | bytes 786440 | tf_op jit(solution)/shard_map/ppermute | solution.py:404
  19.8 19.9 %collective-permute-start.4 = (bf16[32,16,256]{2,1,0:T(8,128)(2,1)}, bf16[32,16,256]{2,1,0:T(8,128)(2,1)S(1)}, u32[]{:S(2)}, u32[]{:S(2)}) collective-permute-start(bf16[32,16,256]{2,1,0:T(8,128)(2,1)} %get-tuple-element.44), channel_id=1, source_target_pairs={{0,6},{2,4},{4,2},{6,0},{8,14},{10,12},{12,10},{14,8},{1,7},{3,5},... | collective-permute-start | bytes 786440 | tf_op jit(solution)/shard_map/ppermute | solution.py:404
  22.1 34.9 %all-to-all-start.1 = ((bf16[8,16,16,256]{3,2,1,0:T(8,128)(2,1)}), bf16[8,16,16,256]{3,2,1,0:T(8,128)(2,1)}, u32[]{:S(2)}, u32[]{:S(2)}) async-start(bf16[8,16,16,256]{3,2,1,0:T(8,128)(2,1)} %get-tuple-element.57), calls=%async_computation.1 | async-start | bytes 2097152 | tf_op jit(solution)/shard_map/all_to_all | solution.py:443
  39.7 1.1 %collective-permute-start.12 = (f32[4]{0:T(128)S(1)}, f32[4]{0:T(128)S(1)}, u32[]{:S(2)}, u32[]{:S(2)}) collective-permute-start(f32[4]{0:T(128)S(1)} %copy-done.6), channel_id=1, source_target_pairs={{0,1},{1,0},{2,3},{3,2},{4,5},{5,4},{6,7},{7,6},{8,9},{9,8},{10,11... | collective-permute-start | bytes 56 | tf_op jit(solution)/shard_map/ppermute | solution.py:401
  39.7 3.7 %collective-permute-start.11 = (f32[1024]{0:T(1024)}, f32[1024]{0:T(1024)}, u32[]{:S(2)}, u32[]{:S(2)}) collective-permute-start(f32[1024]{0:T(1024)} %param.24), channel_id=1, source_target_pairs={{0,1},{1,0},{2,3},{3,2},{4,5},{5,4},{6,7},{7,6},{8,9},{9,8},{10,11... | collective-permute-start | bytes 12296 | tf_op jit(solution)/shard_map/ppermute | solution.py:401
  40.2 3.4 %collective-permute-start.6 = (bf16[512,256]{1,0:T(8,128)(2,1)}, bf16[512,256]{1,0:T(8,128)(2,1)}, u32[]{:S(2)}, u32[]{:S(2)}) collective-permute-start(bf16[512,256]{1,0:T(8,128)(2,1)} %refs_5_.1), channel_id=1, source_target_pairs={{0,1},{1,0},{2,3},{3,2},{4,5},{5,4},{6,7},{7,6},{8,9},{9,8},{10,11... | collective-permute-start | bytes 786440 | tf_op jit(solution)/shard_map/ppermute | solution.py:401
  40.2 18.8 %collective-permute-start.7 = (bf16[512,256]{1,0:T(8,128)(2,1)}, bf16[512,256]{1,0:T(8,128)(2,1)}, u32[]{:S(2)}, u32[]{:S(2)}) collective-permute-start(bf16[512,256]{1,0:T(8,128)(2,1)} %refs_7_.1), channel_id=1, source_target_pairs={{0,1},{1,0},{2,3},{3,2},{4,5},{5,4},{6,7},{7,6},{8,9},{9,8},{10,11... | collective-permute-start | bytes 786440 | tf_op jit(solution)/shard_map/ppermute | solution.py:401
  40.7 20.9 %collective-permute-start.9 = (bf16[512,1024]{1,0:T(8,128)(2,1)}, bf16[512,1024]{1,0:T(8,128)(2,1)}, u32[]{:S(2)}, u32[]{:S(2)}) collective-permute-start(bf16[512,1024]{1,0:T(8,128)(2,1)} %refs_11_.1), channel_id=1, source_target_pairs={{0,1},{1,0},{2,3},{3,2},{4,5},{5,4},{6,7},{7,6},{8,9},{9,8},{10,11... | collective-permute-start | bytes 3145736 | tf_op jit(solution)/shard_map/ppermute | solution.py:401
  41.3 20.3 %collective-permute-start.10 = (bf16[1024,512]{1,0:T(8,128)(2,1)}, bf16[1024,512]{1,0:T(8,128)(2,1)}, u32[]{:S(2)}, u32[]{:S(2)}) collective-permute-start(bf16[1024,512]{1,0:T(8,128)(2,1)} %refs_15_.1), channel_id=1, source_target_pairs={{0,1},{1,0},{2,3},{3,2},{4,5},{5,4},{6,7},{7,6},{8,9},{9,8},{10,11... | collective-permute-start | bytes 3145736 | tf_op jit(solution)/shard_map/ppermute | solution.py:401
  41.8 1.6 %copy-start.3 = (bf16[256,512]{1,0:T(8,128)(2,1)S(1)}, bf16[256,512]{1,0:T(8,128)(2,1)}, u32[]{:S(2)}) copy-start(bf16[256,512]{1,0:T(8,128)(2,1)} %refs_9_.1) | copy-start | bytes 786436
  41.8 15.2 %copy-start.2 = (s32[1,128]{1,0:T(1,128)S(1)}, s32[1,128]{1,0:T(1,128)}, u32[]{:S(2)}) copy-start(s32[1,128]{1,0:T(1,128)} %get-tuple-element.38.list_ref) | copy-start | bytes 1540
  43.3 19.9 %copy-start.4 = (f32[512]{0:T(512)S(1)}, f32[512]{0:T(512)}, u32[]{:S(2)}) copy-start(f32[512]{0:T(512)} %param.17) | copy-start | bytes 6148
  43.3 19.9 %copy-start.5 = (f32[512]{0:T(512)S(1)}, f32[512]{0:T(512)}, u32[]{:S(2)}) copy-start(f32[512]{0:T(512)} %param.22) | copy-start | bytes 6148
  43.3 19.9 %copy-start.7 = (f32[4]{0:T(128)S(1)}, f32[4]{0:T(128)}, u32[]{:S(2)}) copy-start(f32[4]{0:T(128)} %scale_a_ref.1) | copy-start | bytes 52
  43.3 19.9 %copy-start.9 = (f32[4]{0:T(128)S(1)}, f32[4]{0:T(128)}, u32[]{:S(2)}) copy-start(f32[4]{0:T(128)} %copy-done.8) | copy-start | bytes 52
  43.4 15.7 %collective-permute-start.8 = (bf16[256,512]{1,0:T(8,128)(2,1)S(1)}, bf16[256,512]{1,0:T(8,128)(2,1)S(1)}, u32[]{:S(2)}, u32[]{:S(2)}) collective-permute-start(bf16[256,512]{1,0:T(8,128)(2,1)S(1)} %copy-done.3), channel_id=1, source_target_pairs={{0,1},{1,0},{2,3},{3,2},{4,5},{5,4},{6,7},{7,6},{8,9},{9,8},{10,11... | collective-permute-start | bytes 786440 | tf_op jit(solution)/shard_map/ppermute | solution.py:401
  43.5 18.1 %collective-permute-start.5 = (bf16[32,16,256]{2,1,0:T(8,128)(2,1)S(1)}, bf16[32,16,256]{2,1,0:T(8,128)(2,1)S(1)}, u32[]{:S(2)}, u32[]{:S(2)}) collective-permute-start(bf16[32,16,256]{2,1,0:T(8,128)(2,1)S(1)} %get-tuple-element.45), channel_id=1, source_target_pairs={{0,8},{2,10},{4,12},{6,14},{8,0},{10,2},{12,4},{14,6},{1,9},{3,11}... | collective-permute-start | bytes 786440 | tf_op jit(solution)/shard_map/ppermute | solution.py:404
  59.0 4.2 %collective-permute-start.14 = (bf16[64,16,256]{2,1,0:T(8,128)(2,1)S(1)}, bf16[64,16,256]{2,1,0:T(8,128)(2,1)S(1)}, u32[]{:S(2)}, u32[]{:S(2)}) collective-permute-start(bf16[64,16,256]{2,1,0:T(8,128)(2,1)S(1)} %get-tuple-element.59), channel_id=1, source_target_pairs={{0,1},{1,0},{2,3},{3,2},{4,5},{5,4},{6,7},{7,6},{8,9},{9,8},{10,11... | collective-permute-start | bytes 1572872 | tf_op jit(solution)/shard_map/ppermute | solution.py:401
  61.7 1.5 %collective-permute-start.13 = (bf16[32,16,256]{2,1,0:T(8,128)(2,1)S(1)}, bf16[32,16,256]{2,1,0:T(8,128)(2,1)S(1)}, u32[]{:S(2)}, u32[]{:S(2)}) collective-permute-start(bf16[32,16,256]{2,1,0:T(8,128)(2,1)S(1)} %collective-permute-done.5.refs_0_), channel_id=1, source_target_pairs={{0,1},{1,0},{2,3},{3,2},{4,5},{5,4},{6,7},{7,6},{8,9},{9,8},{10,11... | collective-permute-start | bytes 786440 | tf_op jit(solution)/shard_map/ppermute | solution.py:401
  77.8 1.3 %collective-permute-start.15 = (bf16[64,512]{1,0:T(8,128)(2,1)S(1)}, bf16[64,512]{1,0:T(8,128)(2,1)S(1)}, u32[]{:S(2)}, u32[]{:S(2)}) collective-permute-start(bf16[64,512]{1,0:T(8,128)(2,1)S(1)} %shard_map.122), channel_id=1, source_target_pairs={{0,1},{1,0},{2,3},{3,2},{4,5},{5,4},{6,7},{7,6},{8,9},{9,8},{10,11... | collective-permute-start | bytes 196616 | tf_op jit(solution)/shard_map/ppermute | solution.py:401
  (1 other events, 0.5 us)
